TPU v7x, 256 devices: a whole 4x4x8 slice. The times are simulated.
256 devices in a mesh: row: 32 (over x, z), col: 8 (over y, core).
Axes of the slice: x: 4, y: 4, z: 8, core: 2. Of those that a mesh axis runs over, the one named last changes fastest.
Arguments:
- spectrum: float32 [2, 8192, 8192], P(None, 'row', 'col'), may hold values from -6 to 6
- pupil: float32 [2, 512, 512], replicated, may hold values from -4.2 to 4.2
- amplitude: float32 [32, 8, 512, 512], P('row', 'col'), may hold values from 0 to 4, as said below
- offsets: int32 [32, 8, 2], P('row', 'col'), may hold values from 0 to 7680, as said below
- holds: int32 [32, 8], P('row', 'col'), may hold values from 0 to 1, as said below
Outputs:
- spectrum_grad: float32 [2, 8192, 8192], P(None, 'row', 'col')
- transposed_image: float32 [2, 8192, 8192], P(None, ('row', 'col'))
Inputs may be any that keep to these rules, and one draw needn't show every extreme that they name: In each pair of devices in one col whose row indices differ only in the lowest bit, exactly one has holds 1; 128 LEDs in all. `offsets`: both rows of a pair carry the corner (oy, ox) of that pair's LED. With h the row index of the holding device and c the col index: h * 256 - 256 <= oy <= h * 256 + 256, both ends reached by some LED in every draw; c * 1024 <= ox <= c * 1024 + 512, both ends reached by some LED in every draw. `amplitude`: zero on devices whose holds is 0, positive elsewhere.
All inputs are finite; a program needn't handle non-finite values.
Results may differ from a plain program's by a relative error of at most 0.00011.
Values sent between devices are 32-bit elements; how exact they have to be, the bound alone decides.
No kernel may reach another device: no remote copies, remote signals or barrier semaphores. Data moves between devices by JAX's collectives and lax.ppermute only.
A program may use at most 128 MiB of HBM per device.

v0:
```python
import math

import jax
import jax.numpy as jnp
import ml_dtypes
import numpy as np
from jax import lax
from jax.experimental import pallas as pl
from jax.experimental.pallas import tpu as pltpu
from jax.sharding import PartitionSpec as P

GAMMA = 1.0
N = 8192
M = 512
ROWS = 256
COLS = 1024
N_ROW = 32
N_COL = 8
PARTS = N_ROW * N_COL
LOW = 32
F32 = jnp.float32
BF16 = jnp.bfloat16
VMEM_BYTES = 32 * 1024 * 1024


def halves(table):
    high = table.astype(np.float32).astype(ml_dtypes.bfloat16)
    low = (table - high.astype(np.float64)).astype(np.float32).astype(ml_dtypes.bfloat16)
    return high, low


def dft_tables(length, scale):
    counter = np.arange(length)
    angles = 2.0 * np.pi / length * (np.outer(counter, counter) % length)
    return np.stack(halves(np.cos(angles) * scale) + halves(np.sin(angles) * scale))


def twist_tables():
    angles = 2.0 * np.pi / N * np.outer(np.arange(LOW), np.arange(PARTS))
    return np.stack([np.cos(angles), np.sin(angles)]).astype(np.float32)


def split(values):
    high = values.astype(BF16)
    low = (values - high.astype(F32)).astype(BF16)
    return high, low


def mm(left, right):
    return jnp.dot(left, right, preferred_element_type=F32)


def mm3(left, right):
    return mm(left[0], right[0]) + mm(left[0], right[1]) + mm(left[1], right[0])


def complex_times_table(re, im, cos, sin, sign):
    rc, rs, ic, is_ = mm3(re, cos), mm3(re, sin), mm3(im, cos), mm3(im, sin)
    if sign > 0:
        return rc - is_, rs + ic
    return rc + is_, ic - rs


def table_times_complex(cos, sin, sign, re, im):
    rc, rs, ic, is_ = mm3(cos, re), mm3(sin, re), mm3(cos, im), mm3(sin, im)
    if sign > 0:
        return rc - is_, rs + ic
    return rc + is_, ic - rs


def turn(value, numer, denom):
    re, im = value
    numer %= denom
    if numer == 0:
        return re, im
    if 4 * numer == denom:
        return -im, re
    if 2 * numer == denom:
        return -re, -im
    cos = math.cos(2.0 * math.pi * numer / denom)
    sin = math.sin(2.0 * math.pi * numer / denom)
    if 8 * numer == denom:
        return (re - im) * cos, (re + im) * cos
    if 8 * numer == 3 * denom:
        return (re + im) * -sin, (re - im) * sin
    return re * cos - im * sin, re * sin + im * cos


def fft_list(values):
    count = len(values)
    if count == 1:
        return values
    even = fft_list(values[0::2])
    odd = fft_list(values[1::2])
    first, second = [], []
    for at in range(count // 2):
        er, ei = even[at]
        tr, ti = turn(odd[at], at, count)
        first.append((er + tr, ei + ti))
        second.append((er - tr, ei - ti))
    return first + second


def window_rows(base, corner, shape):
    rows = lax.broadcasted_iota(jnp.int32, shape, 0) + base
    return rows, rows < corner, rows >= corner + M


def call(kernel, outs, smem, *args):
    specs = [pl.BlockSpec(memory_space=pltpu.SMEM if at in smem else pltpu.VMEM) for at in range(len(args))]
    return lambda scratch=(): pl.pallas_call(
        kernel,
        out_shape=tuple(jax.ShapeDtypeStruct(shape, F32) for shape in outs),
        in_specs=specs,
        out_specs=tuple(pl.BlockSpec(memory_space=pltpu.VMEM) for _ in outs),
        scratch_shapes=scratch,
        compiler_params=pltpu.CompilerParams(vmem_limit_bytes=VMEM_BYTES),
    )(*args)


def pack_kernel(scal, spec, to_prev, to_next):
    cols = lax.broadcasted_iota(jnp.int32, (ROWS, M), 1)
    for part in range(2):
        left = spec[part, :, :M]
        right = spec[part, :, M:]
        to_prev[part] = jnp.where(cols >= scal[4], left, right)
        to_next[part] = jnp.where(cols >= scal[6], left, right)


def pupil_kernel(scal, pupil, amplitude, rolled, other_amp):
    parity = scal[0]
    shift = lax.rem(scal[2], M)
    down = lax.rem(scal[1] - parity * ROWS + M, M)
    for part in range(2):
        rolled[part] = pltpu.roll(pltpu.roll(pupil[part], shift, 1), down, 0)[:ROWS]
    other_amp[...] = jnp.where(parity == 0, amplitude[:, ROWS:], amplitude[:, :ROWS])


def first_kernel(scal, spec, below, above, pupil, table, keep, send):
    parity = scal[0]
    base = parity * ROWS
    cols = lax.broadcasted_iota(jnp.int32, (ROWS, M), 1)
    rows = lax.broadcasted_iota(jnp.int32, (ROWS, M), 0) + base
    field = []
    for part in range(2):
        own = jnp.where(cols >= scal[2], spec[part, :, :M], spec[part, :, M:])
        field.append(
            jnp.where(rows < scal[1], below[part], jnp.where(rows >= scal[1] + M, above[part], own))
        )
    re = split(pupil[0] * field[0] - pupil[1] * field[1])
    im = split(pupil[0] * field[1] + pupil[1] * field[0])
    for out, half in ((send, 1 - parity), (keep, parity)):
        where = pl.ds(pl.multiple_of(half * ROWS, ROWS), ROWS)
        cos = (table[0, where, :], table[1, where, :])
        sin = (table[2, where, :], table[3, where, :])
        res = complex_times_rows(re, im, cos, sin)
        out[0], out[1] = res


def mmt(left, right):
    return lax.dot_general(left, right, (((1,), (1,)), ((), ())), preferred_element_type=F32)


def mmt3(left, right):
    return mmt(left[0], right[0]) + mmt(left[0], right[1]) + mmt(left[1], right[0])


def complex_times_rows(re, im, cos, sin):
    return mmt3(re, cos) - mmt3(im, sin), mmt3(re, sin) + mmt3(im, cos)


def second_kernel(scal, keep, other, amplitude, other_amp, table, keep_out, send_out):
    parity = scal[0]
    mine = pl.ds(pl.multiple_of(parity * ROWS, ROWS), ROWS)
    yours = pl.ds(pl.multiple_of((1 - parity) * ROWS, ROWS), ROWS)
    low = parity == 0
    pair = []
    for part in range(2):
        top = jnp.where(low, keep[part], other[part])
        bottom = jnp.where(low, other[part], keep[part])
        pair.append(split(jnp.concatenate([top, bottom], axis=0)))
    cos = (table[0], table[1])
    sin = (table[2], table[3])
    wave_re, wave_im = table_times_complex(cos, sin, 1, *pair)
    measured = jnp.where(low, amplitude[:, :ROWS], amplitude[:, ROWS:]) + other_amp[...]
    modulus = jnp.sqrt(wave_re * wave_re + wave_im * wave_im + GAMMA)
    keeping = 1.0 - measured / modulus
    fit_re = split(wave_re * keeping)
    fit_im = split(wave_im * keeping)
    for out, where in ((send_out, yours), (keep_out, mine)):
        cos = (table[0, where, :], table[1, where, :])
        sin = (table[2, where, :], table[3, where, :])
        res = table_times_complex(cos, sin, -1, fit_re, fit_im)
        out[0], out[1] = res


def third_kernel(scal, keep, other, pupil, table, grad):
    low = scal[0] == 0
    pair = []
    for part in range(2):
        left = jnp.where(low, keep[part], other[part])
        right = jnp.where(low, other[part], keep[part])
        pair.append(split(jnp.concatenate([left, right], axis=1)))
    cos = (table[0], table[1])
    sin = (table[2], table[3])
    back_re, back_im = complex_times_table(*pair, cos, sin, -1)
    grad[0] = pupil[0] * back_re + pupil[1] * back_im
    grad[1] = pupil[0] * back_im - pupil[1] * back_re


def gather_kernel(scal, own, from_prev, from_next, total, outgoing):
    base = scal[0] * ROWS
    cols = lax.broadcasted_iota(jnp.int32, (LOW, M), 1)
    for at in range(N_COL):
        rows = lax.broadcasted_iota(jnp.int32, (LOW, M), 0) + base + at * LOW
        here = pl.ds(at * LOW, LOW)
        own_rows = jnp.logical_and(rows >= scal[1], rows < scal[1] + M)
        prev_rows = rows < scal[3]
        next_rows = rows >= scal[5] + M
        for part in range(2):
            mine = jnp.where(own_rows, own[part, here, :], 0.0)
            prev = jnp.where(prev_rows, from_prev[part, here, :], 0.0)
            nxt = jnp.where(next_rows, from_next[part, here, :], 0.0)
            left = (
                jnp.where(cols >= scal[2], mine, 0.0)
                + jnp.where(cols >= scal[4], prev, 0.0)
                + jnp.where(cols >= scal[6], nxt, 0.0)
            )
            right = (
                jnp.where(cols < scal[2], mine, 0.0)
                + jnp.where(cols < scal[4], prev, 0.0)
                + jnp.where(cols < scal[6], nxt, 0.0)
            )
            total[part, here, :M] = left
            total[part, here, M:] = right
            outgoing[at, part, :, :M] = left
            outgoing[at, part, :, M:] = right


def rows_kernel(pencil, twist, table, outgoing, digits):
    for group in range(LOW // 8):
        for tile in range(2):
            lanes = slice(tile * 128, tile * 128 + 128)
            values = [
                tuple(
                    pencil[
                        at // 4,
                        part,
                        group * 8 : group * 8 + 8,
                        (at % 4) * 256 + tile * 128 : (at % 4) * 256 + tile * 128 + 128,
                    ]
                    for part in range(2)
                )
                for at in range(LOW)
            ]
            for at, (re, im) in enumerate(fft_list(values)):
                cos = twist[0, at : at + 1, lanes]
                sin = twist[1, at : at + 1, lanes]
                place = pl.ds((at // 8) * 256 + group * 64 + at % 8, 8, 8)
                digits[tile, place, :] = re * cos - im * sin
                digits[2 + tile, place, :] = re * sin + im * cos
    re = split(jnp.concatenate([digits[0], digits[1]], axis=1))
    im = split(jnp.concatenate([digits[2], digits[3]], axis=1))
    cos = (table[0], table[1])
    sin = (table[2], table[3])
    for part, flat in enumerate(complex_times_table(re, im, cos, sin, 1)):
        turned = flat.T
        for at in range(8):
            outgoing[pl.ds(part * 8 + at, PARTS, 16), :] = turned[:, at * 128 : at * 128 + 128]


def final_kernel(incoming, twist, table, image, digits):
    pair = []
    for part in range(2):
        flat = jnp.concatenate([incoming[pl.ds(part * 8 + at, PARTS, 16), :] for at in range(8)], axis=1)
        pair.append(split(flat.T))
    cos = (table[0], table[1])
    sin = (table[2], table[3])
    digits[0], digits[1] = complex_times_table(*pair, cos, sin, 1)
    for group in range(LOW // 8):
        for tile in range(2):
            lanes = slice(tile * 128, tile * 128 + 128)
            values = []
            for at in range(LOW):
                rows = slice(group * 256 + at * 8, group * 256 + at * 8 + 8)
                re = digits[0, rows, lanes]
                im = digits[1, rows, lanes]
                cos = twist[0, at : at + 1, lanes]
                sin = twist[1, at : at + 1, lanes]
                values.append((re * cos - im * sin, re * sin + im * cos))
            for at, value in enumerate(fft_list(values)):
                for part in range(2):
                    image[
                        part,
                        group * 8 : group * 8 + 8,
                        at * 256 + tile * 128 : at * 256 + tile * 128 + 128,
                    ] = value[part]


def stepped(by, odd_only=False):
    return [(i, i + by) for i in range(N_ROW) if 0 <= i + by < N_ROW and not (odd_only and i % 2 == 0)]


PARTNERS = [(i, i ^ 1) for i in range(N_ROW)]


def on_device(spectrum, pupil, amplitude, offsets, holds, window_table, part_table, twist):
    row = lax.axis_index("row")
    col = lax.axis_index("col")
    corner = offsets[0, 0]
    prev_corner = lax.ppermute(corner, "row", stepped(2))
    next_corner = lax.ppermute(corner, "row", stepped(-2))
    pair_row = (row // 2) * M
    scal = jnp.stack(
        [
            row % 2,
            corner[0] - pair_row,
            corner[1] - col * COLS,
            prev_corner[0] - pair_row + M,
            prev_corner[1] - col * COLS,
            next_corner[0] - pair_row - M,
            next_corner[1] - col * COLS,
            holds[0, 0],
        ]
    )
    measured = amplitude[0, 0]
    half = (2, ROWS, M)
    quarter = (2, ROWS, ROWS)

    to_prev, to_next = call(pack_kernel, [half, half], (0,), scal, spectrum)()
    below = lax.ppermute(to_prev, "row", stepped(-2))
    above = lax.ppermute(to_next, "row", stepped(2, odd_only=True))
    rolled, amp_out = call(pupil_kernel, [half, (M, ROWS)], (0,), scal, pupil, measured)()
    other_amp = lax.ppermute(amp_out, "row", PARTNERS)

    keep, send = call(first_kernel, [quarter, quarter], (0,), scal, spectrum, below, above, rolled, window_table)()
    other = lax.ppermute(send, "row", PARTNERS)
    keep, send = call(
        second_kernel, [quarter, quarter], (0,), scal, keep, other, measured, other_amp, window_table
    )()
    other = lax.ppermute(send, "row", PARTNERS)
    (grad,) = call(third_kernel, [half], (0,), scal, keep, other, rolled, window_table)()

    from_prev = lax.ppermute(grad, "row", stepped(2))
    from_next = lax.ppermute(grad, "row", stepped(-2, odd_only=True))
    total, outgoing = call(
        gather_kernel,
        [(2, ROWS, COLS), (N_COL, 2, LOW, COLS)],
        (0,),
        scal,
        grad,
        from_prev,
        from_next,
    )()
    pencil = lax.all_to_all(outgoing, "col", split_axis=0, concat_axis=0, tiled=True)
    (outgoing,) = call(rows_kernel, [(PARTS * 16, 128)], (), pencil, twist, part_table)(
        [pltpu.VMEM((4, COLS, 128), F32)]
    )
    incoming = lax.all_to_all(
        outgoing.reshape(PARTS, 16, 128), ("row", "col"), split_axis=0, concat_axis=0, tiled=True
    ).reshape(PARTS * 16, 128)
    (image,) = call(final_kernel, [(2, LOW, N)], (), incoming, twist, part_table)(
        [pltpu.VMEM((2, COLS, PARTS), F32)]
    )
    return (total, image)


def solution(mesh):
    window_table = dft_tables(M, 1.0 / math.sqrt(M))
    part_table = dft_tables(PARTS, 1.0 / math.sqrt(N))
    twist = twist_tables()
    mapped = jax.shard_map(
        on_device,
        mesh=mesh,
        in_specs=(
            P(None, "row", "col"),
            P(),
            P("row", "col", None, None),
            P("row", "col", None),
            P("row", "col"),
            P(),
            P(),
            P(),
        ),
        out_specs=(P(None, "row", "col"), P(None, ("row", "col"), None)),
        check_vma=False,
    )

    def run(spectrum, pupil, amplitude, offsets, holds):
        return mapped(
            spectrum,
            pupil,
            amplitude,
            offsets,
            holds,
            jnp.asarray(window_table),
            jnp.asarray(part_table),
            jnp.asarray(twist),
        )

    return run
```

profile of v0, /device:TPU:1, one launch (start us, length us, event | category | flops | bytes accessed | tf_op | source)
XLA Modules:
  0.0 268.2 jit_solution(16982673046617638261)
XLA Ops:
  0.6 1.3 collective-permute-start.1
  1.9 6.4 %collective-permute-start = (s32[2]{0:T(128)}, s32[2]{0:T(128)S(1)}, u32[]{:S(2)}, u32[]{:S(2)}) collective-permute-start(s32[2]{0:T(128)} %bitcast.24), channel_id=1, source_target_pairs={{0,16},{8,24},{16,32},{24,40},{32,48},{40,56},{48,64},{56,72},{64,... | collective-permute-start | bytes 32 | tf_op jit(solution)/shard_map/ppermute | solution.py:311
  8.3 1.3 fusion.2
  15.4 1.6 copy-done.1
  17.7 1.4 collective-permute-start.2
  19.1 0.7 collective-permute-start.3
  19.9 1.2 copy-done.3
  21.1 1.6 copy-done.6
  22.7 2.0 shard_map.96
  24.6 7.2 %collective-permute-start.5 = (f32[512,256]{1,0:T(8,128)S(1)}, f32[512,256]{1,0:T(8,128)S(1)}, u32[]{:S(2)}, u32[]{:S(2)}) collective-permute-start(f32[512,256]{1,0:T(8,128)S(1)} %get-tuple-element.17), channel_id=1, source_target_pairs={{0,8},{8,0},{16,24},{24,16},{32,40},{40,32},{48,56},{56,48},{64,72... | collective-permute-start | bytes 1572872 | tf_op jit(solution)/shard_map/ppermute | solution.py:334
  31.8 37.5 %collective-permute-done.2.below = f32[2,256,512]{2,1,0:T(8,128)S(1)} collective-permute-done((f32[2,256,512]{2,1,0:T(8,128)S(1)}, f32[2,256,512]{2,1,0:T(8,128)S(1)}, u32[]{:S(2)}, u32[]{:S(2)}) %collective-permute-start.2) | collective-permute-done | bytes 1048608 | tf_op jit(solution)/shard_map/ppermute | solution.py:331
  69.3 2.8 %shard_map.97 = (f32[2,256,256]{2,1,0:T(8,128)S(1)}, f32[2,256,256]{2,1,0:T(8,128)S(1)}) custom-call(s32[8]{0:T(128)S(1)} %stack.31.scal, f32[2,256,1024]{2,1,0:T(8,128)S(1)} %copy-done.2, f32[2,256,512]{2,1,0:T(8,128)S(1)} %collective-permute-done.2.below, f32[2,256,512]{2,1,0:T(8,128)S(1)} %collective-permute-done.3.above, ...), custom_call_target="tpu_custom_call" | custom-call | tf_op jit(solution)/shard_map/pallas_call | solution.py:111
  72.3 12.2 %collective-permute-done.4.other = f32[2,256,256]{2,1,0:T(8,128)S(1)} collective-permute-done((f32[2,256,256]{2,1,0:T(8,128)S(1)}, f32[2,256,256]{2,1,0:T(8,128)S(1)}, u32[]{:S(2)}, u32[]{:S(2)}) %collective-permute-start.4) | collective-permute-done | bytes 524320 | tf_op jit(solution)/shard_map/ppermute | solution.py:337
  84.4 4.5 %shard_map.98 = (f32[2,256,256]{2,1,0:T(8,128)S(1)}, f32[2,256,256]{2,1,0:T(8,128)S(1)}) custom-call(s32[8]{0:T(128)S(1)} %stack.31.scal, f32[2,256,256]{2,1,0:T(8,128)S(1)} %get-tuple-element.15.keep, f32[2,256,256]{2,1,0:T(8,128)S(1)} %collective-permute-done.4.other, f32[512,512]{1,0:T(8,128)S(1)} %bitcast.22, ...), custom_call_target="tpu_custom_call" | custom-call | tf_op jit(solution)/shard_map/pallas_call | solution.py:111
  89.3 11.0 %collective-permute-done.6.other = f32[2,256,256]{2,1,0:T(8,128)S(1)} collective-permute-done((f32[2,256,256]{2,1,0:T(8,128)S(1)}, f32[2,256,256]{2,1,0:T(8,128)S(1)}, u32[]{:S(2)}, u32[]{:S(2)}) %collective-permute-start.6) | collective-permute-done | bytes 524320 | tf_op jit(solution)/shard_map/ppermute | solution.py:341
  100.3 2.5 shard_map.99.own
  102.8 0.7 collective-permute-start.8
  103.5 10.1 %collective-permute-start.7 = (f32[2,256,512]{2,1,0:T(8,128)S(1)}, f32[2,256,512]{2,1,0:T(8,128)S(1)}, u32[]{:S(2)}, u32[]{:S(2)}) collective-permute-start(f32[2,256,512]{2,1,0:T(8,128)S(1)} %shard_map.99.own), channel_id=1, source_target_pairs={{0,16},{8,24},{16,32},{24,40},{32,48},{40,56},{48,64},{56,72},{64,... | collective-permute-start | bytes 3145736 | tf_op jit(solution)/shard_map/ppermute | solution.py:344
  113.7 19.8 %collective-permute-done.7.from_prev = f32[2,256,512]{2,1,0:T(8,128)S(1)} collective-permute-done((f32[2,256,512]{2,1,0:T(8,128)S(1)}, f32[2,256,512]{2,1,0:T(8,128)S(1)}, u32[]{:S(2)}, u32[]{:S(2)}) %collective-permute-start.7) | collective-permute-done | bytes 1048608 | tf_op jit(solution)/shard_map/ppermute | solution.py:344
  133.5 2.5 shard_map.100
  136.0 34.5 %all_to_all.10.pencil = f32[8,2,32,1024]{3,2,1,0:T(8,128)S(1)} all-to-all(f32[8,2,32,1024]{3,2,1,0:T(8,128)S(1)} %get-tuple-element.21), channel_id=1, replica_groups=mesh['row'=32,'col'=8] {'col'}, dimensions={0} | all-to-all | bytes 4194304 | tf_op jit(solution)/shard_map/all_to_all | solution.py:355
  170.5 3.7 %shard_map.101 = f32[4096,128]{1,0:T(8,128)S(1)} custom-call(f32[8,2,32,1024]{3,2,1,0:T(8,128)S(1)} %all_to_all.10.pencil, f32[2,32,256]{2,1,0:T(8,128)S(1)} %copy-done.7, bf16[4,256,256]{2,1,0:T(8,128)(2,1)S(1)} %copy-done.5), custom_call_target="tpu_custom_call" | custom-call | tf_op jit(solution)/shard_map/pallas_call | solution.py:111
  174.2 89.7 %all_to_all.11 = f32[256,16,128]{2,1,0:T(8,128)S(1)} all-to-all(f32[256,16,128]{2,1,0:T(8,128)S(1)} %bitcast.20), channel_id=1, replica_groups=mesh['row'=32,'col'=8] {'row','col'}, dimensions={0} | all-to-all | bytes 4194304 | tf_op jit(solution)/shard_map/all_to_all | solution.py:359
  263.9 4.3 %shard_map.102 = f32[2,32,8192]{2,1,0:T(8,128)} custom-call(f32[4096,128]{1,0:T(8,128)S(1)} %bitcast.19, f32[2,32,256]{2,1,0:T(8,128)S(1)} %copy-done.7, bf16[4,256,256]{2,1,0:T(8,128)(2,1)S(1)} %copy-done.5), custom_call_target="tpu_custom_call" | custom-call | tf_op jit(solution)/shard_map/pallas_call | solution.py:111
  (24 shorter events, 2.5 us)
Async XLA Ops:
  0.6 10.8 %collective-permute-start.1 = (s32[2]{0:T(128)}, s32[2]{0:T(128)S(1)}, u32[]{:S(2)}, u32[]{:S(2)}) collective-permute-start(s32[2]{0:T(128)} %bitcast.23), channel_id=1, source_target_pairs={{16,0},{24,8},{32,16},{40,24},{48,32},{56,40},{64,48},{72,56},{80,... | collective-permute-start | bytes 32 | tf_op jit(solution)/shard_map/ppermute | solution.py:312
  1.9 11.4 %collective-permute-start = (s32[2]{0:T(128)}, s32[2]{0:T(128)S(1)}, u32[]{:S(2)}, u32[]{:S(2)}) collective-permute-start(s32[2]{0:T(128)} %bitcast.24), channel_id=1, source_target_pairs={{0,16},{8,24},{16,32},{24,40},{32,48},{40,56},{48,64},{56,72},{64,... | collective-permute-start | bytes 32 | tf_op jit(solution)/shard_map/ppermute | solution.py:311
  15.4 1.6 copy-start.1
  17.0 52.3 %copy-start.2 = (f32[2,256,1024]{2,1,0:T(8,128)S(1)}, f32[2,256,1024]{2,1,0:T(8,128)}, u32[]{:S(2)}) copy-start(f32[2,256,1024]{2,1,0:T(8,128)} %spec.3) | copy-start | bytes 6291460
  17.7 51.6 %copy-start = (bf16[4,512,512]{2,1,0:T(8,128)(2,1)S(1)}, bf16[4,512,512]{2,1,0:T(8,128)(2,1)}, u32[]{:S(2)}) copy-start(bf16[4,512,512]{2,1,0:T(8,128)(2,1)} %constant.45.clone.table) | copy-start | bytes 6291460
  17.7 51.6 %collective-permute-start.2 = (f32[2,256,512]{2,1,0:T(8,128)S(1)}, f32[2,256,512]{2,1,0:T(8,128)S(1)}, u32[]{:S(2)}, u32[]{:S(2)}) collective-permute-start(f32[2,256,512]{2,1,0:T(8,128)S(1)} %get-tuple-element.12), channel_id=1, source_target_pairs={{16,0},{24,8},{32,16},{40,24},{48,32},{56,40},{64,48},{72,56},{80,... | collective-permute-start | bytes 3145736 | tf_op jit(solution)/shard_map/ppermute | solution.py:331
  19.1 50.2 %collective-permute-start.3 = (f32[2,256,512]{2,1,0:T(8,128)S(1)}, f32[2,256,512]{2,1,0:T(8,128)S(1)}, u32[]{:S(2)}, u32[]{:S(2)}) collective-permute-start(f32[2,256,512]{2,1,0:T(8,128)S(1)} %get-tuple-element.13), channel_id=1, source_target_pairs={{8,24},{24,40},{40,56},{56,72},{72,88},{88,104},{104,120},{120,136... | collective-permute-start | bytes 3145736 | tf_op jit(solution)/shard_map/ppermute | solution.py:332
  19.9 1.2 copy-start.3
  21.1 1.6 copy-start.6
  24.6 47.6 %collective-permute-start.5 = (f32[512,256]{1,0:T(8,128)S(1)}, f32[512,256]{1,0:T(8,128)S(1)}, u32[]{:S(2)}, u32[]{:S(2)}) collective-permute-start(f32[512,256]{1,0:T(8,128)S(1)} %get-tuple-element.17), channel_id=1, source_target_pairs={{0,8},{8,0},{16,24},{24,16},{32,40},{40,32},{48,56},{56,48},{64,72... | collective-permute-start | bytes 1572872 | tf_op jit(solution)/shard_map/ppermute | solution.py:334
  69.3 15.1 %copy-start.4 = (f32[1,1,512,512]{3,2,1,0:T(8,128)S(1)}, f32[1,1,512,512]{3,2,1,0:T(8,128)}, u32[]{:S(2)}) copy-start(f32[1,1,512,512]{3,2,1,0:T(8,128)} %param.10) | copy-start | bytes 3145732
  72.2 12.3 %collective-permute-start.4 = (f32[2,256,256]{2,1,0:T(8,128)S(1)}, f32[2,256,256]{2,1,0:T(8,128)S(1)}, u32[]{:S(2)}, u32[]{:S(2)}) collective-permute-start(f32[2,256,256]{2,1,0:T(8,128)S(1)} %get-tuple-element.16), channel_id=1, source_target_pairs={{0,8},{8,0},{16,24},{24,16},{32,40},{40,32},{48,56},{56,48},{64,72... | collective-permute-start | bytes 1572872 | tf_op jit(solution)/shard_map/ppermute | solution.py:337
  88.9 11.3 %collective-permute-start.6 = (f32[2,256,256]{2,1,0:T(8,128)S(1)}, f32[2,256,256]{2,1,0:T(8,128)S(1)}, u32[]{:S(2)}, u32[]{:S(2)}) collective-permute-start(f32[2,256,256]{2,1,0:T(8,128)S(1)} %get-tuple-element.19), channel_id=1, source_target_pairs={{0,8},{8,0},{16,24},{24,16},{32,40},{40,32},{48,56},{56,48},{64,72... | collective-permute-start | bytes 1572872 | tf_op jit(solution)/shard_map/ppermute | solution.py:341
  102.8 10.9 %collective-permute-start.8 = (f32[2,256,512]{2,1,0:T(8,128)S(1)}, f32[2,256,512]{2,1,0:T(8,128)S(1)}, u32[]{:S(2)}, u32[]{:S(2)}) collective-permute-start(f32[2,256,512]{2,1,0:T(8,128)S(1)} %shard_map.99.own), channel_id=1, source_target_pairs={{24,8},{40,24},{56,40},{72,56},{88,72},{104,88},{120,104},{136,120... | collective-permute-start | bytes 3145736 | tf_op jit(solution)/shard_map/ppermute | solution.py:345
  103.5 30.0 %collective-permute-start.7 = (f32[2,256,512]{2,1,0:T(8,128)S(1)}, f32[2,256,512]{2,1,0:T(8,128)S(1)}, u32[]{:S(2)}, u32[]{:S(2)}) collective-permute-start(f32[2,256,512]{2,1,0:T(8,128)S(1)} %shard_map.99.own), channel_id=1, source_target_pairs={{0,16},{8,24},{16,32},{24,40},{32,48},{40,56},{48,64},{56,72},{64,... | collective-permute-start | bytes 3145736 | tf_op jit(solution)/shard_map/ppermute | solution.py:344
  136.0 34.5 %copy-start.5 = (bf16[4,256,256]{2,1,0:T(8,128)(2,1)S(1)}, bf16[4,256,256]{2,1,0:T(8,128)(2,1)}, u32[]{:S(2)}) copy-start(bf16[4,256,256]{2,1,0:T(8,128)(2,1)} %constant.46.clone.table) | copy-start | bytes 1572868
  136.0 34.5 %copy-start.7 = (f32[2,32,256]{2,1,0:T(8,128)S(1)}, f32[2,32,256]{2,1,0:T(8,128)}, u32[]{:S(2)}) copy-start(f32[2,32,256]{2,1,0:T(8,128)} %constant.47.clone.twist) | copy-start | bytes 196612
where the time goes:
time: 269 us; the launch traced here: 268 us
  blocking collectives  124 us (46%)
  waiting for transfers between devices  80.4 us (30%)
  starting transfers between devices  28.3 us (11%)
  Pallas kernels  22.9 us (9%)
  local copies, waits for them, and re-layouts  7.05 us (3%)
  between operations  5.26 us (2%)
    all_to_all x1, blocking collectives, on_device(): lax.all_to_all(outgoing.reshape(PARTS, 16, 128), ('row', 'col'), split_ax...  89.7 us
    ppermute x1, waiting for transfers between devices, on_device(): below = lax.ppermute(to_prev, 'row', stepped(-2))  37.5 us
    all_to_all x1, blocking collectives, on_device(): lax.all_to_all(outgoing, 'col', split_axis=0, concat_axis=0, tiled=True)  34.5 us
    ppermute x2, waiting for transfers between devices, on_device(): other = lax.ppermute(send, 'row', PARTNERS)  23.1 us
    pallas_call x8, Pallas kernels, call(): pl.pallas_call(kernel, out_shape=tuple((jax.ShapeDtypeStruct(shape, F32)...  22.9 us
    ppermute x1, waiting for transfers between devices, on_device(): from_prev = lax.ppermute(grad, 'row', stepped(2))  19.8 us
    ppermute x1, starting transfers between devices, on_device(): from_prev = lax.ppermute(grad, 'row', stepped(2))  10.1 us
    ppermute x1, starting transfers between devices, on_device(): other_amp = lax.ppermute(amp_out, 'row', PARTNERS)  7.2 us
  transfers between devices with their start and end apart: 9, of which 4 were waited for; matrix products, arithmetic and copies ran while one was open for 1% of the time, Pallas kernels for 2%

commit v1 on v0

--- a/solution.py
+++ b/solution.py
@@ -101,11 +101,6 @@
     return first + second
 
 
-def window_rows(base, corner, shape):
-    rows = lax.broadcasted_iota(jnp.int32, shape, 0) + base
-    return rows, rows < corner, rows >= corner + M
-
-
 def call(kernel, outs, smem, *args):
     specs = [pl.BlockSpec(memory_space=pltpu.SMEM if at in smem else pltpu.VMEM) for at in range(len(args))]
     return lambda scratch=(): pl.pallas_call(
@@ -118,43 +113,57 @@
     )(*args)
 
 
-def pack_kernel(scal, spec, to_prev, to_next):
+def frame(pos, corner):
+    return corner[0] - pos[0] * ROWS, corner[1] - pos[1] * COLS
+
+
+def corners(pos, local, lower, upper):
+    moved = jnp.logical_and(lax.rem(pos[0], 2) == 0, lax.rem(pos[1], 2) == 1)
+    local, lower, upper = frame(pos, local), frame(pos, lower), frame(pos, upper)
+    here = tuple(jnp.where(moved, x, y) for x, y in zip(lower, local))
+    up = tuple(jnp.where(moved, x, y) for x, y in zip(local, upper))
+    return here, lower, up
+
+
+def inside(rows, start):
+    return jnp.logical_and(rows >= start, rows < start + M)
+
+
+def pack_kernel(pos, local, lower, upper, spec, to_lower, to_upper):
+    _, down, up = corners(pos, local, lower, upper)
     cols = lax.broadcasted_iota(jnp.int32, (ROWS, M), 1)
     for part in range(2):
         left = spec[part, :, :M]
         right = spec[part, :, M:]
-        to_prev[part] = jnp.where(cols >= scal[4], left, right)
-        to_next[part] = jnp.where(cols >= scal[6], left, right)
-
-
-def pupil_kernel(scal, pupil, amplitude, rolled, other_amp):
-    parity = scal[0]
-    shift = lax.rem(scal[2], M)
-    down = lax.rem(scal[1] - parity * ROWS + M, M)
+        to_lower[part] = jnp.where(cols >= down[1], left, right)
+        to_upper[part] = jnp.where(cols >= up[1], left, right)
+
+
+def pupil_kernel(pos, local, lower, upper, pupil, rolled):
+    (at_row, at_col), _, _ = corners(pos, local, lower, upper)
+    shift = lax.rem(at_col, M)
+    down = lax.rem(at_row + 2 * N, M)
     for part in range(2):
         rolled[part] = pltpu.roll(pltpu.roll(pupil[part], shift, 1), down, 0)[:ROWS]
-    other_amp[...] = jnp.where(parity == 0, amplitude[:, ROWS:], amplitude[:, :ROWS])
-
-
-def first_kernel(scal, spec, below, above, pupil, table, keep, send):
-    parity = scal[0]
-    base = parity * ROWS
+
+
+def first_kernel(pos, local, lower, upper, spec, from_lower, from_upper, pupil, table, keep, send):
+    parity = lax.rem(pos[0], 2)
+    (at_row, at_col), _, _ = corners(pos, local, lower, upper)
     cols = lax.broadcasted_iota(jnp.int32, (ROWS, M), 1)
-    rows = lax.broadcasted_iota(jnp.int32, (ROWS, M), 0) + base
+    rows = lax.broadcasted_iota(jnp.int32, (ROWS, M), 0)
     field = []
     for part in range(2):
-        own = jnp.where(cols >= scal[2], spec[part, :, :M], spec[part, :, M:])
-        field.append(
-            jnp.where(rows < scal[1], below[part], jnp.where(rows >= scal[1] + M, above[part], own))
-        )
+        own = jnp.where(cols >= at_col, spec[part, :, :M], spec[part, :, M:])
+        other = jnp.where(inside(rows + M, at_row), from_upper[part], from_lower[part])
+        field.append(jnp.where(inside(rows, at_row), own, other))
     re = split(pupil[0] * field[0] - pupil[1] * field[1])
     im = split(pupil[0] * field[1] + pupil[1] * field[0])
     for out, half in ((send, 1 - parity), (keep, parity)):
         where = pl.ds(pl.multiple_of(half * ROWS, ROWS), ROWS)
         cos = (table[0, where, :], table[1, where, :])
         sin = (table[2, where, :], table[3, where, :])
-        res = complex_times_rows(re, im, cos, sin)
-        out[0], out[1] = res
+        out[0], out[1] = complex_times_rows(re, im, cos, sin)
 
 
 def mmt(left, right):
@@ -169,8 +178,9 @@
     return mmt3(re, cos) - mmt3(im, sin), mmt3(re, sin) + mmt3(im, cos)
 
 
-def second_kernel(scal, keep, other, amplitude, other_amp, table, keep_out, send_out):
-    parity = scal[0]
+def second_kernel(pos, keep, other, amplitude, near_amp, far_amp, table, keep_out, send_out):
+    parity = lax.rem(pos[0], 2)
+    moved = jnp.logical_and(parity == 0, lax.rem(pos[1], 2) == 1)
     mine = pl.ds(pl.multiple_of(parity * ROWS, ROWS), ROWS)
     yours = pl.ds(pl.multiple_of((1 - parity) * ROWS, ROWS), ROWS)
     low = parity == 0
@@ -182,7 +192,8 @@
     cos = (table[0], table[1])
     sin = (table[2], table[3])
     wave_re, wave_im = table_times_complex(cos, sin, 1, *pair)
-    measured = jnp.where(low, amplitude[:, :ROWS], amplitude[:, ROWS:]) + other_amp[...]
+    measured = jnp.where(low, amplitude[:, :ROWS], amplitude[:, ROWS:])
+    measured = jnp.where(moved, far_amp[...], measured) + near_amp[...]
     modulus = jnp.sqrt(wave_re * wave_re + wave_im * wave_im + GAMMA)
     keeping = 1.0 - measured / modulus
     fit_re = split(wave_re * keeping)
@@ -190,12 +201,11 @@
     for out, where in ((send_out, yours), (keep_out, mine)):
         cos = (table[0, where, :], table[1, where, :])
         sin = (table[2, where, :], table[3, where, :])
-        res = table_times_complex(cos, sin, -1, fit_re, fit_im)
-        out[0], out[1] = res
-
-
-def third_kernel(scal, keep, other, pupil, table, grad):
-    low = scal[0] == 0
+        out[0], out[1] = table_times_complex(cos, sin, -1, fit_re, fit_im)
+
+
+def third_kernel(pos, keep, other, pupil, table, grad_re, grad_im):
+    low = lax.rem(pos[0], 2) == 0
     pair = []
     for part in range(2):
         left = jnp.where(low, keep[part], other[part])
@@ -204,40 +214,26 @@
     cos = (table[0], table[1])
     sin = (table[2], table[3])
     back_re, back_im = complex_times_table(*pair, cos, sin, -1)
-    grad[0] = pupil[0] * back_re + pupil[1] * back_im
-    grad[1] = pupil[0] * back_im - pupil[1] * back_re
-
-
-def gather_kernel(scal, own, from_prev, from_next, total, outgoing):
-    base = scal[0] * ROWS
+    grad_re[...] = pupil[0] * back_re + pupil[1] * back_im
+    grad_im[...] = pupil[0] * back_im - pupil[1] * back_re
+
+
+def gather_kernel(pos, local, lower, upper, own, from_lower, from_upper, total):
+    leds = corners(pos, local, lower, upper)
     cols = lax.broadcasted_iota(jnp.int32, (LOW, M), 1)
     for at in range(N_COL):
-        rows = lax.broadcasted_iota(jnp.int32, (LOW, M), 0) + base + at * LOW
+        rows = lax.broadcasted_iota(jnp.int32, (LOW, M), 0) + at * LOW
         here = pl.ds(at * LOW, LOW)
-        own_rows = jnp.logical_and(rows >= scal[1], rows < scal[1] + M)
-        prev_rows = rows < scal[3]
-        next_rows = rows >= scal[5] + M
-        for part in range(2):
-            mine = jnp.where(own_rows, own[part, here, :], 0.0)
-            prev = jnp.where(prev_rows, from_prev[part, here, :], 0.0)
-            nxt = jnp.where(next_rows, from_next[part, here, :], 0.0)
-            left = (
-                jnp.where(cols >= scal[2], mine, 0.0)
-                + jnp.where(cols >= scal[4], prev, 0.0)
-                + jnp.where(cols >= scal[6], nxt, 0.0)
-            )
-            right = (
-                jnp.where(cols < scal[2], mine, 0.0)
-                + jnp.where(cols < scal[4], prev, 0.0)
-                + jnp.where(cols < scal[6], nxt, 0.0)
-            )
-            total[part, here, :M] = left
-            total[part, here, M:] = right
-            outgoing[at, part, :, :M] = left
-            outgoing[at, part, :, M:] = right
-
-
-def rows_kernel(pencil, twist, table, outgoing, digits):
+        left = right = 0.0
+        for (at_row, at_col), source in zip(leds, (own, from_lower, from_upper)):
+            value = jnp.where(inside(rows, at_row), source[here, :], 0.0)
+            left = left + jnp.where(cols >= at_col, value, 0.0)
+            right = right + jnp.where(cols < at_col, value, 0.0)
+        total[here, :M] = left
+        total[here, M:] = right
+
+
+def rows_kernel(pencil_re, pencil_im, twist, table, outgoing, digits):
     for group in range(LOW // 8):
         for tile in range(2):
             lanes = slice(tile * 128, tile * 128 + 128)
@@ -245,11 +241,10 @@
                 tuple(
                     pencil[
                         at // 4,
-                        part,
                         group * 8 : group * 8 + 8,
                         (at % 4) * 256 + tile * 128 : (at % 4) * 256 + tile * 128 + 128,
                     ]
-                    for part in range(2)
+                    for pencil in (pencil_re, pencil_im)
                 )
                 for at in range(LOW)
             ]
@@ -297,63 +292,87 @@
                     ] = value[part]
 
 
-def stepped(by, odd_only=False):
-    return [(i, i + by) for i in range(N_ROW) if 0 <= i + by < N_ROW and not (odd_only and i % 2 == 0)]
-
-
-PARTNERS = [(i, i ^ 1) for i in range(N_ROW)]
+def moves(rule):
+    pairs = [(row, col, rule(row, col % 2)) for row in range(N_ROW) for col in range(N_COL)]
+    return [(row * N_COL + col, to * N_COL + col) for row, col, to in pairs if to is not None]
+
+
+def downward(row, core):
+    return row - 2 if row >= 2 and (row % 2 == 1 or core == 0) else None
+
+
+def upward(row, core):
+    if row % 2 == 0:
+        return (row + 2) % N_ROW if core == 1 else None
+    return row + 2 if row + 2 < N_ROW else None
+
+
+def partner(row, core):
+    return row ^ 1 if core == 0 else (row + (1 if row % 2 == 1 else -1)) % N_ROW
+
+
+def near(row, core):
+    return row ^ 1 if core == 0 else (row + 1) % N_ROW
+
+
+def far(row, core):
+    return (row + 2) % N_ROW if core == 1 and row % 2 == 0 else None
+
+
+def back(pairs):
+    return [(to, source) for source, to in pairs]
+
+
+BOTH = ("row", "col")
+DOWN = moves(downward)
+UP = moves(upward)
+PARTNERS = moves(partner)
+NEAR = moves(near)
+FAR = moves(far)
+FROM_LOWER = moves(lambda row, core: (row + 2) % N_ROW)
+FROM_UPPER = moves(lambda row, core: row - 2 if row >= 2 and row % 2 == 1 else None)
 
 
 def on_device(spectrum, pupil, amplitude, offsets, holds, window_table, part_table, twist):
     row = lax.axis_index("row")
     col = lax.axis_index("col")
-    corner = offsets[0, 0]
-    prev_corner = lax.ppermute(corner, "row", stepped(2))
-    next_corner = lax.ppermute(corner, "row", stepped(-2))
-    pair_row = (row // 2) * M
-    scal = jnp.stack(
-        [
-            row % 2,
-            corner[0] - pair_row,
-            corner[1] - col * COLS,
-            prev_corner[0] - pair_row + M,
-            prev_corner[1] - col * COLS,
-            next_corner[0] - pair_row - M,
-            next_corner[1] - col * COLS,
-            holds[0, 0],
-        ]
-    )
+    pos = jnp.stack([row, col]).astype(jnp.int32)
+    local = offsets[0, 0]
+    lower = lax.ppermute(local, BOTH, FROM_LOWER)
+    upper = lax.ppermute(local, BOTH, FROM_UPPER)
+    where = (pos, local, lower, upper)
+    smem = (0, 1, 2, 3)
     measured = amplitude[0, 0]
-    half = (2, ROWS, M)
+    half = (ROWS, M)
     quarter = (2, ROWS, ROWS)
-
-    to_prev, to_next = call(pack_kernel, [half, half], (0,), scal, spectrum)()
-    below = lax.ppermute(to_prev, "row", stepped(-2))
-    above = lax.ppermute(to_next, "row", stepped(2, odd_only=True))
-    rolled, amp_out = call(pupil_kernel, [half, (M, ROWS)], (0,), scal, pupil, measured)()
-    other_amp = lax.ppermute(amp_out, "row", PARTNERS)
-
-    keep, send = call(first_kernel, [quarter, quarter], (0,), scal, spectrum, below, above, rolled, window_table)()
-    other = lax.ppermute(send, "row", PARTNERS)
+    near_half = lax.dynamic_slice(measured, (jnp.int32(0), (1 - row % 2) * ROWS), (M, ROWS))
+    near_amp = lax.ppermute(near_half, BOTH, NEAR)
+    far_amp = lax.ppermute(measured[:, :ROWS], BOTH, FAR)
+
+    to_lower, to_upper = call(pack_kernel, [(2,) + half, (2,) + half], smem, *where, spectrum)()
+    from_upper = lax.ppermute(to_lower, BOTH, DOWN)
+    from_lower = lax.ppermute(to_upper, BOTH, UP)
+    (rolled,) = call(pupil_kernel, [(2,) + half], smem, *where, pupil)()
+
     keep, send = call(
-        second_kernel, [quarter, quarter], (0,), scal, keep, other, measured, other_amp, window_table
+        first_kernel, [quarter, quarter], smem, *where, spectrum, from_lower, from_upper, rolled, window_table
     )()
-    other = lax.ppermute(send, "row", PARTNERS)
-    (grad,) = call(third_kernel, [half], (0,), scal, keep, other, rolled, window_table)()
-
-    from_prev = lax.ppermute(grad, "row", stepped(2))
-    from_next = lax.ppermute(grad, "row", stepped(-2, odd_only=True))
-    total, outgoing = call(
-        gather_kernel,
-        [(2, ROWS, COLS), (N_COL, 2, LOW, COLS)],
-        (0,),
-        scal,
-        grad,
-        from_prev,
-        from_next,
+    other = lax.ppermute(send, BOTH, PARTNERS)
+    keep, send = call(
+        second_kernel, [quarter, quarter], (0,), pos, keep, other, measured, near_amp, far_amp, window_table
     )()
-    pencil = lax.all_to_all(outgoing, "col", split_axis=0, concat_axis=0, tiled=True)
-    (outgoing,) = call(rows_kernel, [(PARTS * 16, 128)], (), pencil, twist, part_table)(
+    other = lax.ppermute(send, BOTH, PARTNERS)
+    grads = call(third_kernel, [half, half], (0,), pos, keep, other, rolled, window_table)()
+
+    moved = [(lax.ppermute(grad, BOTH, back(DOWN)), lax.ppermute(grad, BOTH, back(UP))) for grad in grads]
+    totals, pencils = [], []
+    for grad, sources in zip(grads, moved):
+        (total,) = call(gather_kernel, [(ROWS, COLS)], smem, *where, grad, *sources)()
+        totals.append(total)
+        pencils.append(
+            lax.all_to_all(total.reshape(N_COL, LOW, COLS), "col", split_axis=0, concat_axis=0, tiled=True)
+        )
+    (outgoing,) = call(rows_kernel, [(PARTS * 16, 128)], (), *pencils, twist, part_table)(
         [pltpu.VMEM((4, COLS, 128), F32)]
     )
     incoming = lax.all_to_all(
@@ -362,7 +381,7 @@
     (image,) = call(final_kernel, [(2, LOW, N)], (), incoming, twist, part_table)(
         [pltpu.VMEM((2, COLS, PARTS), F32)]
     )
-    return (total, image)
+    return (jnp.stack(totals), image)
 
 
 def solution(mesh):

time: 269 us -> 241 us (0.90)
  blocking collectives: 124 us -> 19.4 us
  waiting for transfers between devices: 80.4 us -> 120 us
  starting transfers between devices: 28.3 us -> 66.2 us
  between operations: 5.26 us -> 0.82 us
  other arithmetic: 0 us -> 2.81 us
  Pallas kernels: 22.9 us -> 25.7 us
    all_to_all x2 -> x1, blocking collectives: 124 us -> 19.4 us  [on_device(): lax.all_to_all(total.reshape(N_COL, LOW, COLS), 'col', split_axis=0, conc...]
    all_to_all x0 -> x2, waiting for transfers between devices: none -> 50.7 us  [the longest x1 50.7 us: on_device(): lax.all_to_all(outgoing.reshape(PARTS, 16, 128), ('row', 'col'), split_ax...]
    ppermute x9 -> x12, starting transfers between devices: 28.3 us -> 49.8 us  [the longest x2 30.7 us: on_device(): other = lax.ppermute(send, BOTH, PARTNERS)]
    all_to_all x0 -> x2, starting transfers between devices: none -> 16.4 us  [the longest x1 11.8 us: on_device(): lax.all_to_all(outgoing.reshape(PARTS, 16, 128), ('row', 'col'), split_ax...]
    ppermute x9 -> x12, waiting for transfers between devices: 80.4 us -> 69.2 us  [the longest x2 36.6 us: on_device(): lax.ppermute(grad, BOTH, back(UP))]
    another operation x0 -> x2, other arithmetic: none -> 2.81 us  [the longest x1 2.73 us: on_device(): return (jnp.stack(totals), image)]
    pallas_call x8 -> x9, Pallas kernels: 22.9 us -> 25.7 us  [call(): pl.pallas_call(kernel, out_shape=tuple((jax.ShapeDtypeStruct(shape, F32)...]
  transfers between devices with their start and end apart: 9 -> 14, of which waited for: 4 -> 8; matrix products, arithmetic and copies ran while one was open for 1% -> 2% of each run, Pallas kernels for 2% -> 3%
where the time goes in v1:
time: 241 us; the launch traced here: 240 us
  waiting for transfers between devices  120 us (50%)
  starting transfers between devices  66.2 us (27%)
  Pallas kernels  25.7 us (11%)
  blocking collectives  19.4 us (8%)
  local copies, waits for them, and re-layouts  5.53 us (2%)
  other arithmetic  2.81 us (1%)
    all_to_all x1, waiting for transfers between devices, on_device(): lax.all_to_all(outgoing.reshape(PARTS, 16, 128), ('row', 'col'), split_ax...  50.7 us
    ppermute x2, waiting for transfers between devices, on_device(): lax.ppermute(grad, BOTH, back(UP))  36.6 us
    ppermute x2, starting transfers between devices, on_device(): other = lax.ppermute(send, BOTH, PARTNERS)  30.7 us
    pallas_call x9, Pallas kernels, call(): pl.pallas_call(kernel, out_shape=tuple((jax.ShapeDtypeStruct(shape, F32)...  25.7 us
    all_to_all x1, blocking collectives, on_device(): lax.all_to_all(total.reshape(N_COL, LOW, COLS), 'col', split_axis=0, conc...  19.4 us
    all_to_all x1, starting transfers between devices, on_device(): lax.all_to_all(outgoing.reshape(PARTS, 16, 128), ('row', 'col'), split_ax...  11.8 us
    ppermute x1, waiting for transfers between devices, on_device(): from_lower = lax.ppermute(to_upper, BOTH, UP)  10.6 us
    ppermute x2, waiting for transfers between devices, on_device(): other = lax.ppermute(send, BOTH, PARTNERS)  6.57 us
  transfers between devices with their start and end apart: 14, of which 8 were waited for; matrix products, arithmetic and copies ran while one was open for 2% of the time, Pallas kernels for 3%

profile of v1, /device:TPU:1, one launch (start us, length us, event | category | flops | bytes accessed | tf_op | source)
XLA Modules:
  0.0 240.3 jit_solution(12637865720134555235)
XLA Ops:
  1.3 3.9 %collective-permute-start = (s32[2]{0:T(128)}, s32[2]{0:T(128)S(1)}, u32[]{:S(2)}, u32[]{:S(2)}) collective-permute-start(s32[2]{0:T(128)} %bitcast.19), channel_id=1, source_target_pairs={{0,16},{1,17},{2,18},{3,19},{4,20},{5,21},{6,22},{7,23},{8,24},{9,... | collective-permute-start | bytes 32 | tf_op jit(solution)/shard_map/ppermute | solution.py:341
  5.3 6.2 %collective-permute-done.lower = s32[2]{0:T(128)S(1)} collective-permute-done((s32[2]{0:T(128)}, s32[2]{0:T(128)S(1)}, u32[]{:S(2)}, u32[]{:S(2)}) %collective-permute-start) | collective-permute-done | bytes 40 | tf_op jit(solution)/shard_map/ppermute | solution.py:341
  13.7 2.0 shard_map.86
  20.2 4.4 %collective-permute-start.6 = (f32[512,256]{1,0:T(8,128)}, f32[512,256]{1,0:T(8,128)}, u32[]{:S(2)}, u32[]{:S(2)}) collective-permute-start(f32[512,256]{1,0:T(8,128)} %slice.4), channel_id=1, source_target_pairs={{1,17},{3,19},{5,21},{7,23},{17,33},{19,35},{21,37},{23,39},{33,49... | collective-permute-start | bytes 1572872 | tf_op jit(solution)/shard_map/ppermute | solution.py:350
  26.8 10.6 %collective-permute-done.2.from_lower = f32[2,256,512]{2,1,0:T(8,128)} collective-permute-done((f32[2,256,512]{2,1,0:T(8,128)}, f32[2,256,512]{2,1,0:T(8,128)}, u32[]{:S(2)}, u32[]{:S(2)}) %collective-permute-start.2) | collective-permute-done | bytes 1048608 | tf_op jit(solution)/shard_map/ppermute | solution.py:354
  37.5 3.7 %shard_map.88 = (f32[2,256,256]{2,1,0:T(8,128)S(1)}, f32[2,256,256]{2,1,0:T(8,128)S(1)}) custom-call(s32[2]{0:T(128)S(1)} %pad_add_fusion.pos, s32[2]{0:T(128)S(1)} %bitcast.22, s32[2]{0:T(128)S(1)} %collective-permute-done.lower, s32[2]{0:T(128)S(1)} %collective-permute-done.1.upper, f32[2,256,1024]{2,1,0:T(8,128)S(1)} %copy-done.3, ...), custom_call_target="tpu_custom_call" | custom-call | tf_op jit(solution)/shard_map/pallas_call | solution.py:106
  41.2 23.7 %collective-permute-start.4 = (f32[2,256,256]{2,1,0:T(8,128)S(1)}, f32[2,256,256]{2,1,0:T(8,128)S(1)}, u32[]{:S(2)}, u32[]{:S(2)}) collective-permute-start(f32[2,256,256]{2,1,0:T(8,128)S(1)} %get-tuple-element.13), channel_id=1, source_target_pairs={{0,8},{1,249},{2,10},{3,251},{4,12},{5,253},{6,14},{7,255},{8,0},{... | collective-permute-start | bytes 1572872 | tf_op jit(solution)/shard_map/ppermute | solution.py:360
  64.9 5.6 %collective-permute-done.6.far_amp = f32[512,256]{1,0:T(8,128)} collective-permute-done((f32[512,256]{1,0:T(8,128)}, f32[512,256]{1,0:T(8,128)}, u32[]{:S(2)}, u32[]{:S(2)}) %collective-permute-start.6) | collective-permute-done | bytes 524320 | tf_op jit(solution)/shard_map/ppermute | solution.py:350
  70.5 3.6 %collective-permute-done.5.near_amp = f32[512,256]{1,0:T(8,128)S(1)} collective-permute-done((f32[512,256]{1,0:T(8,128)S(1)}, f32[512,256]{1,0:T(8,128)S(1)}, u32[]{:S(2)}, u32[]{:S(2)}) %collective-permute-start.5) | collective-permute-done | bytes 524320 | tf_op jit(solution)/shard_map/ppermute | solution.py:349
  74.1 4.9 %shard_map.89 = (f32[2,256,256]{2,1,0:T(8,128)S(1)}, f32[2,256,256]{2,1,0:T(8,128)S(1)}) custom-call(s32[2]{0:T(128)S(1)} %pad_add_fusion.pos, f32[2,256,256]{2,1,0:T(8,128)S(1)} %get-tuple-element.12.keep, f32[2,256,256]{2,1,0:T(8,128)S(1)} %collective-permute-done.4.other, f32[512,512]{1,0:T(8,128)S(1)} %bitcast.17, ...), custom_call_target="tpu_custom_call" | custom-call | tf_op jit(solution)/shard_map/pallas_call | solution.py:106
  79.1 7.0 %collective-permute-start.7 = (f32[2,256,256]{2,1,0:T(8,128)S(1)}, f32[2,256,256]{2,1,0:T(8,128)S(1)}, u32[]{:S(2)}, u32[]{:S(2)}) collective-permute-start(f32[2,256,256]{2,1,0:T(8,128)S(1)} %get-tuple-element.15), channel_id=1, source_target_pairs={{0,8},{1,249},{2,10},{3,251},{4,12},{5,253},{6,14},{7,255},{8,0},{... | collective-permute-start | bytes 1572872 | tf_op jit(solution)/shard_map/ppermute | solution.py:364
  86.0 6.6 %collective-permute-done.7.other = f32[2,256,256]{2,1,0:T(8,128)S(1)} collective-permute-done((f32[2,256,256]{2,1,0:T(8,128)S(1)}, f32[2,256,256]{2,1,0:T(8,128)S(1)}, u32[]{:S(2)}, u32[]{:S(2)}) %collective-permute-start.7) | collective-permute-done | bytes 524320 | tf_op jit(solution)/shard_map/ppermute | solution.py:364
  92.6 2.4 shard_map.90
  95.0 2.9 %collective-permute-start.9 = (f32[256,512]{1,0:T(8,128)S(1)}, f32[256,512]{1,0:T(8,128)S(1)}, u32[]{:S(2)}, u32[]{:S(2)}) collective-permute-start(f32[256,512]{1,0:T(8,128)S(1)} %get-tuple-element.16.own), channel_id=1, source_target_pairs={{17,1},{19,3},{21,5},{23,7},{24,8},{25,9},{26,10},{27,11},{28,12},... | collective-permute-start | bytes 1572872 | tf_op jit(solution)/shard_map/ppermute | solution.py:367
  98.7 17.9 %collective-permute-done.9.from_upper = f32[256,512]{1,0:T(8,128)S(1)} collective-permute-done((f32[256,512]{1,0:T(8,128)S(1)}, f32[256,512]{1,0:T(8,128)S(1)}, u32[]{:S(2)}, u32[]{:S(2)}) %collective-permute-start.9) | collective-permute-done | bytes 524320 | tf_op jit(solution)/shard_map/ppermute | solution.py:367
  118.4 4.6 %all-to-all-start = ((f32[8,32,1024]{2,1,0:T(8,128)}), f32[8,32,1024]{2,1,0:T(8,128)S(1)}, u32[]{:S(2)}, u32[]{:S(2)}) async-start(f32[8,32,1024]{2,1,0:T(8,128)} %bitcast.7), calls=%async_computation | async-start | bytes 2097152 | tf_op jit(solution)/shard_map/all_to_all | solution.py:373
  123.0 2.0 collective-permute-start.11
  125.7 18.7 %collective-permute-done.11.from_upper = f32[256,512]{1,0:T(8,128)S(1)} collective-permute-done((f32[256,512]{1,0:T(8,128)S(1)}, f32[256,512]{1,0:T(8,128)S(1)}, u32[]{:S(2)}, u32[]{:S(2)}) %collective-permute-start.11) | collective-permute-done | bytes 524320 | tf_op jit(solution)/shard_map/ppermute | solution.py:367
  145.3 19.4 %all_to_all.15.pencil_im = f32[8,32,1024]{2,1,0:T(8,128)S(1)} all-to-all(f32[8,32,1024]{2,1,0:T(8,128)S(1)} %bitcast.12), channel_id=1, replica_groups=mesh['row'=32,'col'=8] {'col'}, dimensions={0} | all-to-all | bytes 2097152 | tf_op jit(solution)/shard_map/all_to_all | solution.py:373
  164.8 3.7 %shard_map.93 = f32[4096,128]{1,0:T(8,128)S(1)} custom-call(f32[8,32,1024]{2,1,0:T(8,128)S(1)} %all-to-all-done.pencil_re, f32[8,32,1024]{2,1,0:T(8,128)S(1)} %all_to_all.15.pencil_im, f32[2,32,256]{2,1,0:T(8,128)S(1)} %copy-done.8, bf16[4,256,256]{2,1,0:T(8,128)(2,1)S(1)} %copy-done.5), custom_call_target="tpu_custom_call" | custom-call | tf_op jit(solution)/shard_map/pallas_call | solution.py:106
  169.8 11.8 %all-to-all-start.2 = ((f32[256,16,128]{2,1,0:T(8,128)}), f32[256,16,128]{2,1,0:T(8,128)S(1)}, u32[]{:S(2)}, u32[]{:S(2)}) async-start(f32[256,16,128]{2,1,0:T(8,128)} %bitcast.15), calls=%async_computation.2 | async-start | bytes 4194304 | tf_op jit(solution)/shard_map/all_to_all | solution.py:378
  181.6 2.7 %pad_maximum_fusion = f32[2,256,1024]{2,1,0:T(8,128)} fusion(f32[1,256,1024]{2,1,0:T(8,128)S(1)} %bitcast.13, f32[1,256,1024]{2,1,0:T(8,128)} %bitcast.5), kind=kLoop, calls=%fused_computation | loop fusion | flops 524288 | bytes 4194304 | tf_op jit(solution)/shard_map/stack | solution.py:384
  184.4 50.7 %all-to-all-done.2 = f32[256,16,128]{2,1,0:T(8,128)S(1)} async-done(((f32[256,16,128]{2,1,0:T(8,128)}), f32[256,16,128]{2,1,0:T(8,128)S(1)}, u32[]{:S(2)}, u32[]{:S(2)}) %all-to-all-start.2) | async-done | bytes 2097184 | tf_op jit(solution)/shard_map/all_to_all | solution.py:378
  236.1 4.3 %shard_map.94 = f32[2,32,8192]{2,1,0:T(8,128)} custom-call(f32[4096,128]{1,0:T(8,128)S(1)} %bitcast.14, f32[2,32,256]{2,1,0:T(8,128)S(1)} %copy-done.8, bf16[4,256,256]{2,1,0:T(8,128)(2,1)S(1)} %copy-done.6), custom_call_target="tpu_custom_call" | custom-call | tf_op jit(solution)/shard_map/pallas_call | solution.py:106
  (40 shorter events, 16.1 us)
Async XLA Ops:
  0.6 4.6 %collective-permute-start.1 = (s32[2]{0:T(128)}, s32[2]{0:T(128)S(1)}, u32[]{:S(2)}, u32[]{:S(2)}) collective-permute-start(s32[2]{0:T(128)} %bitcast.18), channel_id=1, source_target_pairs={{24,8},{25,9},{26,10},{27,11},{28,12},{29,13},{30,14},{31,15},{40,... | collective-permute-start | bytes 32 | tf_op jit(solution)/shard_map/ppermute | solution.py:342
  1.3 10.2 %collective-permute-start = (s32[2]{0:T(128)}, s32[2]{0:T(128)S(1)}, u32[]{:S(2)}, u32[]{:S(2)}) collective-permute-start(s32[2]{0:T(128)} %bitcast.19), channel_id=1, source_target_pairs={{0,16},{1,17},{2,18},{3,19},{4,20},{5,21},{6,22},{7,23},{8,24},{9,... | collective-permute-start | bytes 32 | tf_op jit(solution)/shard_map/ppermute | solution.py:341
  5.2 19.7 %copy-start.10 = (s32[1,1,2]{2,1,0:T(1,128)S(1)}, s32[1,1,2]{2,1,0:T(1,128)}, u32[]{:S(2)}) copy-start(s32[1,1,2]{2,1,0:T(1,128)} %param.11) | copy-start | bytes 28
  11.5 1.6 copy-start.2
  13.7 5.6 %copy-start.4 = (f32[1,1,512,512]{3,2,1,0:T(8,128)S(1)}, f32[1,1,512,512]{3,2,1,0:T(8,128)}, u32[]{:S(2)}) copy-start(f32[1,1,512,512]{3,2,1,0:T(8,128)} %param.10) | copy-start | bytes 3145732
  13.7 11.2 %copy-start.7 = (f32[2,512,512]{2,1,0:T(8,128)S(1)}, f32[2,512,512]{2,1,0:T(8,128)}, u32[]{:S(2)}) copy-start(f32[2,512,512]{2,1,0:T(8,128)} %pupil.1) | copy-start | bytes 6291460
  15.8 21.7 %collective-permute-start.2 = (f32[2,256,512]{2,1,0:T(8,128)}, f32[2,256,512]{2,1,0:T(8,128)}, u32[]{:S(2)}, u32[]{:S(2)}) collective-permute-start(f32[2,256,512]{2,1,0:T(8,128)} %get-tuple-element.10), channel_id=1, source_target_pairs={{1,17},{3,19},{5,21},{7,23},{8,24},{9,25},{10,26},{11,27},{12,28},... | collective-permute-start | bytes 3145736 | tf_op jit(solution)/shard_map/ppermute | solution.py:354
  17.7 19.8 %collective-permute-start.3 = (f32[2,256,512]{2,1,0:T(8,128)}, f32[2,256,512]{2,1,0:T(8,128)}, u32[]{:S(2)}, u32[]{:S(2)}) collective-permute-start(f32[2,256,512]{2,1,0:T(8,128)} %get-tuple-element.11), channel_id=1, source_target_pairs={{16,0},{18,2},{20,4},{22,6},{24,8},{25,9},{26,10},{27,11},{28,12},... | collective-permute-start | bytes 3145736 | tf_op jit(solution)/shard_map/ppermute | solution.py:353
  20.2 50.4 %collective-permute-start.6 = (f32[512,256]{1,0:T(8,128)}, f32[512,256]{1,0:T(8,128)}, u32[]{:S(2)}, u32[]{:S(2)}) collective-permute-start(f32[512,256]{1,0:T(8,128)} %slice.4), channel_id=1, source_target_pairs={{1,17},{3,19},{5,21},{7,23},{17,33},{19,35},{21,37},{23,39},{33,49... | collective-permute-start | bytes 1572872 | tf_op jit(solution)/shard_map/ppermute | solution.py:350
  24.6 12.9 %copy-start = (bf16[4,512,512]{2,1,0:T(8,128)(2,1)S(1)}, bf16[4,512,512]{2,1,0:T(8,128)(2,1)}, u32[]{:S(2)}) copy-start(bf16[4,512,512]{2,1,0:T(8,128)(2,1)} %constant.35.clone.table) | copy-start | bytes 6291460
  24.6 12.8 %copy-start.3 = (f32[2,256,1024]{2,1,0:T(8,128)S(1)}, f32[2,256,1024]{2,1,0:T(8,128)}, u32[]{:S(2)}) copy-start(f32[2,256,1024]{2,1,0:T(8,128)} %spec.3) | copy-start | bytes 6291460
  24.7 49.4 %collective-permute-start.5 = (f32[512,256]{1,0:T(8,128)S(1)}, f32[512,256]{1,0:T(8,128)S(1)}, u32[]{:S(2)}, u32[]{:S(2)}) collective-permute-start(f32[512,256]{1,0:T(8,128)S(1)} %dynamic-slice_bitcast_fusion), channel_id=1, source_target_pairs={{0,8},{1,9},{2,10},{3,11},{4,12},{5,13},{6,14},{7,15},{8,0},{9,17}... | collective-permute-start | bytes 1572872 | tf_op jit(solution)/shard_map/ppermute | solution.py:349
  41.2 32.9 %collective-permute-start.4 = (f32[2,256,256]{2,1,0:T(8,128)S(1)}, f32[2,256,256]{2,1,0:T(8,128)S(1)}, u32[]{:S(2)}, u32[]{:S(2)}) collective-permute-start(f32[2,256,256]{2,1,0:T(8,128)S(1)} %get-tuple-element.13), channel_id=1, source_target_pairs={{0,8},{1,249},{2,10},{3,251},{4,12},{5,253},{6,14},{7,255},{8,0},{... | collective-permute-start | bytes 1572872 | tf_op jit(solution)/shard_map/ppermute | solution.py:360
  79.1 13.5 %collective-permute-start.7 = (f32[2,256,256]{2,1,0:T(8,128)S(1)}, f32[2,256,256]{2,1,0:T(8,128)S(1)}, u32[]{:S(2)}, u32[]{:S(2)}) collective-permute-start(f32[2,256,256]{2,1,0:T(8,128)S(1)} %get-tuple-element.15), channel_id=1, source_target_pairs={{0,8},{1,249},{2,10},{3,251},{4,12},{5,253},{6,14},{7,255},{8,0},{... | collective-permute-start | bytes 1572872 | tf_op jit(solution)/shard_map/ppermute | solution.py:364
  95.0 21.5 %collective-permute-start.9 = (f32[256,512]{1,0:T(8,128)S(1)}, f32[256,512]{1,0:T(8,128)S(1)}, u32[]{:S(2)}, u32[]{:S(2)}) collective-permute-start(f32[256,512]{1,0:T(8,128)S(1)} %get-tuple-element.16.own), channel_id=1, source_target_pairs={{17,1},{19,3},{21,5},{23,7},{24,8},{25,9},{26,10},{27,11},{28,12},... | collective-permute-start | bytes 1572872 | tf_op jit(solution)/shard_map/ppermute | solution.py:367
  97.9 18.6 %collective-permute-start.8 = (f32[256,512]{1,0:T(8,128)S(1)}, f32[256,512]{1,0:T(8,128)S(1)}, u32[]{:S(2)}, u32[]{:S(2)}) collective-permute-start(f32[256,512]{1,0:T(8,128)S(1)} %get-tuple-element.16.own), channel_id=1, source_target_pairs={{0,16},{2,18},{4,20},{6,22},{8,24},{9,25},{10,26},{11,27},{12,28},... | collective-permute-start | bytes 1572872 | tf_op jit(solution)/shard_map/ppermute | solution.py:367
  118.4 26.9 %all-to-all-start = ((f32[8,32,1024]{2,1,0:T(8,128)}), f32[8,32,1024]{2,1,0:T(8,128)S(1)}, u32[]{:S(2)}, u32[]{:S(2)}) async-start(f32[8,32,1024]{2,1,0:T(8,128)} %bitcast.7), calls=%async_computation | async-start | bytes 2097152 | tf_op jit(solution)/shard_map/all_to_all | solution.py:373
  123.0 41.8 %copy-start.5 = (bf16[4,256,256]{2,1,0:T(8,128)(2,1)S(1)}, bf16[4,256,256]{2,1,0:T(8,128)(2,1)}, u32[]{:S(2)}) copy-start(bf16[4,256,256]{2,1,0:T(8,128)(2,1)} %constant.36.clone.table) | copy-start | bytes 1572868
  123.0 41.8 %copy-start.8 = (f32[2,32,256]{2,1,0:T(8,128)S(1)}, f32[2,32,256]{2,1,0:T(8,128)}, u32[]{:S(2)}) copy-start(f32[2,32,256]{2,1,0:T(8,128)} %constant.37.clone.twist) | copy-start | bytes 196612
  123.0 21.5 %collective-permute-start.11 = (f32[256,512]{1,0:T(8,128)S(1)}, f32[256,512]{1,0:T(8,128)S(1)}, u32[]{:S(2)}, u32[]{:S(2)}) collective-permute-start(f32[256,512]{1,0:T(8,128)S(1)} %get-tuple-element.17.own), channel_id=1, source_target_pairs={{17,1},{19,3},{21,5},{23,7},{24,8},{25,9},{26,10},{27,11},{28,12},... | collective-permute-start | bytes 1572872 | tf_op jit(solution)/shard_map/ppermute | solution.py:367
  125.0 19.4 %collective-permute-start.10 = (f32[256,512]{1,0:T(8,128)S(1)}, f32[256,512]{1,0:T(8,128)S(1)}, u32[]{:S(2)}, u32[]{:S(2)}) collective-permute-start(f32[256,512]{1,0:T(8,128)S(1)} %get-tuple-element.17.own), channel_id=1, source_target_pairs={{0,16},{2,18},{4,20},{6,22},{8,24},{9,25},{10,26},{11,27},{12,28},... | collective-permute-start | bytes 1572872 | tf_op jit(solution)/shard_map/ppermute | solution.py:367
  168.5 1.3 copy-start.1
  169.8 65.3 %all-to-all-start.2 = ((f32[256,16,128]{2,1,0:T(8,128)}), f32[256,16,128]{2,1,0:T(8,128)S(1)}, u32[]{:S(2)}, u32[]{:S(2)}) async-start(f32[256,16,128]{2,1,0:T(8,128)} %bitcast.15), calls=%async_computation.2 | async-start | bytes 4194304 | tf_op jit(solution)/shard_map/all_to_all | solution.py:378
  235.0 1.0 copy-start.6
  (1 other events, 0.7 us)

commit v2 on v1

--- a/solution.py
+++ b/solution.py
@@ -18,8 +18,10 @@
 N_COL = 8
 PARTS = N_ROW * N_COL
 LOW = 32
+ORDER = [0, 2, 4, 6, 1, 3, 5, 7]
 F32 = jnp.float32
 BF16 = jnp.bfloat16
+SLOW = 10**11
 VMEM_BYTES = 32 * 1024 * 1024
 
 
@@ -101,7 +103,7 @@
     return first + second
 
 
-def call(kernel, outs, smem, *args):
+def call(kernel, outs, smem, *args, cost=None):
     specs = [pl.BlockSpec(memory_space=pltpu.SMEM if at in smem else pltpu.VMEM) for at in range(len(args))]
     return lambda scratch=(): pl.pallas_call(
         kernel,
@@ -109,6 +111,7 @@
         in_specs=specs,
         out_specs=tuple(pl.BlockSpec(memory_space=pltpu.VMEM) for _ in outs),
         scratch_shapes=scratch,
+        cost_estimate=cost and pl.CostEstimate(flops=cost, bytes_accessed=0, transcendentals=0),
         compiler_params=pltpu.CompilerParams(vmem_limit_bytes=VMEM_BYTES),
     )(*args)
 
@@ -147,9 +150,22 @@
         rolled[part] = pltpu.roll(pltpu.roll(pupil[part], shift, 1), down, 0)[:ROWS]
 
 
-def first_kernel(pos, local, lower, upper, spec, from_lower, from_upper, pupil, table, keep, send):
-    parity = lax.rem(pos[0], 2)
-    (at_row, at_col), _, _ = corners(pos, local, lower, upper)
+def stage_kernel(spec, staged):
+    staged[...] = spec[...]
+
+
+def half_rows(table, half):
+    where = pl.ds(pl.multiple_of(half * ROWS, ROWS), ROWS)
+    return (table[0, where, :], table[1, where, :]), (table[2, where, :], table[3, where, :])
+
+
+def half_cols(table, half):
+    where = pl.ds(pl.multiple_of(half * ROWS, ROWS), ROWS)
+    return (table[0, :, where], table[1, :, where]), (table[2, :, where], table[3, :, where])
+
+
+def field_of(where, spec, from_lower, from_upper, pupil):
+    (at_row, at_col), _, _ = corners(*where)
     cols = lax.broadcasted_iota(jnp.int32, (ROWS, M), 1)
     rows = lax.broadcasted_iota(jnp.int32, (ROWS, M), 0)
     field = []
@@ -159,81 +175,77 @@
         field.append(jnp.where(inside(rows, at_row), own, other))
     re = split(pupil[0] * field[0] - pupil[1] * field[1])
     im = split(pupil[0] * field[1] + pupil[1] * field[0])
-    for out, half in ((send, 1 - parity), (keep, parity)):
-        where = pl.ds(pl.multiple_of(half * ROWS, ROWS), ROWS)
-        cos = (table[0, where, :], table[1, where, :])
-        sin = (table[2, where, :], table[3, where, :])
-        out[0], out[1] = complex_times_rows(re, im, cos, sin)
-
-
-def mmt(left, right):
-    return lax.dot_general(left, right, (((1,), (1,)), ((), ())), preferred_element_type=F32)
-
-
-def mmt3(left, right):
-    return mmt(left[0], right[0]) + mmt(left[0], right[1]) + mmt(left[1], right[0])
-
-
-def complex_times_rows(re, im, cos, sin):
-    return mmt3(re, cos) - mmt3(im, sin), mmt3(re, sin) + mmt3(im, cos)
-
-
-def second_kernel(pos, keep, other, amplitude, near_amp, far_amp, table, keep_out, send_out):
+    return re, im
+
+
+def send_kernel(pos, local, lower, upper, spec, from_lower, from_upper, pupil, table, send):
+    re, im = field_of((pos, local, lower, upper), spec, from_lower, from_upper, pupil)
+    cos, sin = half_cols(table, 1 - lax.rem(pos[0], 2))
+    send[0], send[1] = complex_times_table(re, im, cos, sin, 1)
+
+
+def keep_kernel(pos, local, lower, upper, spec, from_lower, from_upper, pupil, table, wave):
+    parity = lax.rem(pos[0], 2)
+    re, im = field_of((pos, local, lower, upper), spec, from_lower, from_upper, pupil)
+    cos, sin = half_cols(table, parity)
+    re, im = complex_times_table(re, im, cos, sin, 1)
+    wave[0], wave[1] = table_times_complex(cos, sin, 1, split(re), split(im))
+
+
+def fit_kernel(pos, wave, other, amplitude, near_amp, far_amp, table, fit, send):
     parity = lax.rem(pos[0], 2)
     moved = jnp.logical_and(parity == 0, lax.rem(pos[1], 2) == 1)
-    mine = pl.ds(pl.multiple_of(parity * ROWS, ROWS), ROWS)
-    yours = pl.ds(pl.multiple_of((1 - parity) * ROWS, ROWS), ROWS)
-    low = parity == 0
-    pair = []
-    for part in range(2):
-        top = jnp.where(low, keep[part], other[part])
-        bottom = jnp.where(low, other[part], keep[part])
-        pair.append(split(jnp.concatenate([top, bottom], axis=0)))
-    cos = (table[0], table[1])
-    sin = (table[2], table[3])
-    wave_re, wave_im = table_times_complex(cos, sin, 1, *pair)
-    measured = jnp.where(low, amplitude[:, :ROWS], amplitude[:, ROWS:])
+    cos, sin = half_cols(table, 1 - parity)
+    wave_re, wave_im = table_times_complex(cos, sin, 1, split(other[0]), split(other[1]))
+    wave_re += wave[0]
+    wave_im += wave[1]
+    measured = jnp.where(parity == 0, amplitude[:, :ROWS], amplitude[:, ROWS:])
     measured = jnp.where(moved, far_amp[...], measured) + near_amp[...]
     modulus = jnp.sqrt(wave_re * wave_re + wave_im * wave_im + GAMMA)
     keeping = 1.0 - measured / modulus
-    fit_re = split(wave_re * keeping)
-    fit_im = split(wave_im * keeping)
-    for out, where in ((send_out, yours), (keep_out, mine)):
-        cos = (table[0, where, :], table[1, where, :])
-        sin = (table[2, where, :], table[3, where, :])
-        out[0], out[1] = table_times_complex(cos, sin, -1, fit_re, fit_im)
-
-
-def third_kernel(pos, keep, other, pupil, table, grad_re, grad_im):
-    low = lax.rem(pos[0], 2) == 0
-    pair = []
-    for part in range(2):
-        left = jnp.where(low, keep[part], other[part])
-        right = jnp.where(low, other[part], keep[part])
-        pair.append(split(jnp.concatenate([left, right], axis=1)))
-    cos = (table[0], table[1])
-    sin = (table[2], table[3])
-    back_re, back_im = complex_times_table(*pair, cos, sin, -1)
-    grad_re[...] = pupil[0] * back_re + pupil[1] * back_im
-    grad_im[...] = pupil[0] * back_im - pupil[1] * back_re
-
-
-def gather_kernel(pos, local, lower, upper, own, from_lower, from_upper, total):
-    leds = corners(pos, local, lower, upper)
+    fit[0] = wave_re * keeping
+    fit[1] = wave_im * keeping
+    cos, sin = half_rows(table, 1 - parity)
+    send[0], send[1] = table_times_complex(cos, sin, -1, split(fit[0]), split(fit[1]))
+
+
+def stay_kernel(pos, fit, table, part):
+    cos, sin = half_rows(table, lax.rem(pos[0], 2))
+    re, im = table_times_complex(cos, sin, -1, split(fit[0]), split(fit[1]))
+    part[0], part[1] = complex_times_table(split(re), split(im), cos, sin, -1)
+
+
+def grad_kernel(pos, part, other, pupil, table, grad):
+    cos, sin = half_rows(table, 1 - lax.rem(pos[0], 2))
+    re, im = complex_times_table(split(other[0]), split(other[1]), cos, sin, -1)
+    re += part[0]
+    im += part[1]
+    back_re = pupil[0] * re + pupil[1] * im
+    back_im = pupil[0] * im - pupil[1] * re
+    for at, col in enumerate(ORDER):
+        grad[at, 0] = back_re[col * LOW : col * LOW + LOW]
+        grad[at, 1] = back_im[col * LOW : col * LOW + LOW]
+
+
+def rows_kernel(pos, leds, own, lower_even, lower_odd, upper_even, upper_odd, twist, table, outgoing, shares, pencil, digits):
+    row, col = pos[0], pos[1]
     cols = lax.broadcasted_iota(jnp.int32, (LOW, M), 1)
-    for at in range(N_COL):
-        rows = lax.broadcasted_iota(jnp.int32, (LOW, M), 0) + at * LOW
-        here = pl.ds(at * LOW, LOW)
-        left = right = 0.0
-        for (at_row, at_col), source in zip(leds, (own, from_lower, from_upper)):
-            value = jnp.where(inside(rows, at_row), source[here, :], 0.0)
-            left = left + jnp.where(cols >= at_col, value, 0.0)
-            right = right + jnp.where(cols < at_col, value, 0.0)
-        total[here, :M] = left
-        total[here, M:] = right
-
-
-def rows_kernel(pencil_re, pencil_im, twist, table, outgoing, digits):
+    rows = lax.broadcasted_iota(jnp.int32, (LOW, M), 0) + col * LOW
+    for at, source_col in enumerate(ORDER):
+        lower, upper = (lower_even, upper_even) if at < 4 else (lower_odd, upper_odd)
+        corner = [leds[source_col, index] for index in range(6)]
+        around = corners((row, source_col), corner[:2], corner[2:4], corner[4:])
+        place = lax.rem(source_col - col + N_COL, N_COL)
+        for part in range(2):
+            left = right = 0.0
+            for (at_row, at_col), source in zip(around, (own[at, part], lower[at % 4, part], upper[at % 4, part])):
+                value = jnp.where(inside(rows, at_row), source, 0.0)
+                left = left + jnp.where(cols >= at_col, value, 0.0)
+                right = right + jnp.where(cols < at_col, value, 0.0)
+            pencil[source_col, part, :, :M] = left
+            pencil[source_col, part, :, M:] = right
+            shares[place, part, :, :M] = left
+            shares[place, part, :, M:] = right
     for group in range(LOW // 8):
         for tile in range(2):
             lanes = slice(tile * 128, tile * 128 + 128)
@@ -241,10 +253,11 @@
                 tuple(
                     pencil[
                         at // 4,
+                        part,
                         group * 8 : group * 8 + 8,
                         (at % 4) * 256 + tile * 128 : (at % 4) * 256 + tile * 128 + 128,
                     ]
-                    for pencil in (pencil_re, pencil_im)
+                    for part in range(2)
                 )
                 for at in range(LOW)
             ]
@@ -262,6 +275,14 @@
         turned = flat.T
         for at in range(8):
             outgoing[pl.ds(part * 8 + at, PARTS, 16), :] = turned[:, at * 128 : at * 128 + 128]
+
+
+def assemble_kernel(pos, *refs):
+    total = refs[-1]
+    for step, share in enumerate(refs[:-1]):
+        where = pl.ds(pl.multiple_of(lax.rem(pos[1] - step + N_COL, N_COL) * LOW, LOW), LOW)
+        for part in range(2):
+            total[part, where, :] = share[part]
 
 
 def final_kernel(incoming, twist, table, image, digits):
@@ -319,10 +340,6 @@
     return (row + 2) % N_ROW if core == 1 and row % 2 == 0 else None
 
 
-def back(pairs):
-    return [(to, source) for source, to in pairs]
-
-
 BOTH = ("row", "col")
 DOWN = moves(downward)
 UP = moves(upward)
@@ -341,6 +358,7 @@
     lower = lax.ppermute(local, BOTH, FROM_LOWER)
     upper = lax.ppermute(local, BOTH, FROM_UPPER)
     where = (pos, local, lower, upper)
+    leds = lax.all_gather(jnp.concatenate([local, lower, upper]), "col")
     smem = (0, 1, 2, 3)
     measured = amplitude[0, 0]
     half = (ROWS, M)
@@ -349,39 +367,55 @@
     near_amp = lax.ppermute(near_half, BOTH, NEAR)
     far_amp = lax.ppermute(measured[:, :ROWS], BOTH, FAR)
 
-    to_lower, to_upper = call(pack_kernel, [(2,) + half, (2,) + half], smem, *where, spectrum)()
+    (staged,) = call(stage_kernel, [(2, ROWS, COLS)], (), spectrum)()
+    to_lower, to_upper = call(pack_kernel, [(2,) + half, (2,) + half], smem, *where, staged)()
     from_upper = lax.ppermute(to_lower, BOTH, DOWN)
     from_lower = lax.ppermute(to_upper, BOTH, UP)
     (rolled,) = call(pupil_kernel, [(2,) + half], smem, *where, pupil)()
 
-    keep, send = call(
-        first_kernel, [quarter, quarter], smem, *where, spectrum, from_lower, from_upper, rolled, window_table
+    sources = (*where, staged, from_lower, from_upper, rolled, window_table)
+    (send,) = call(send_kernel, [quarter], smem, *sources)()
+    other = lax.ppermute(send, BOTH, PARTNERS)
+    (wave,) = call(keep_kernel, [(2, M, ROWS)], smem, *sources)()
+    fit, send = call(
+        fit_kernel, [(2, M, ROWS), quarter], (0,), pos, wave, other, measured, near_amp, far_amp, window_table
     )()
     other = lax.ppermute(send, BOTH, PARTNERS)
-    keep, send = call(
-        second_kernel, [quarter, quarter], (0,), pos, keep, other, measured, near_amp, far_amp, window_table
-    )()
-    other = lax.ppermute(send, BOTH, PARTNERS)
-    grads = call(third_kernel, [half, half], (0,), pos, keep, other, rolled, window_table)()
-
-    moved = [(lax.ppermute(grad, BOTH, back(DOWN)), lax.ppermute(grad, BOTH, back(UP))) for grad in grads]
-    totals, pencils = [], []
-    for grad, sources in zip(grads, moved):
-        (total,) = call(gather_kernel, [(ROWS, COLS)], smem, *where, grad, *sources)()
-        totals.append(total)
-        pencils.append(
-            lax.all_to_all(total.reshape(N_COL, LOW, COLS), "col", split_axis=0, concat_axis=0, tiled=True)
-        )
-    (outgoing,) = call(rows_kernel, [(PARTS * 16, 128)], (), *pencils, twist, part_table)(
-        [pltpu.VMEM((4, COLS, 128), F32)]
-    )
+    (part,) = call(stay_kernel, [(2,) + half], (0,), pos, fit, window_table)()
+    (grad,) = call(grad_kernel, [(N_COL, 2, LOW, M)], (0,), pos, part, other, rolled, window_table)()
+
+    own = lax.all_to_all(grad, "col", split_axis=0, concat_axis=0, tiled=True, axis_index_groups=[ORDER])
+    even, odd = own[:4], own[4:]
+    lower_even = lax.ppermute(even, "row", [(row, row + 2) for row in range(N_ROW - 2)])
+    upper_odd = lax.ppermute(odd, "row", [(row, row - 2) for row in range(2, N_ROW)] + [(0, N_ROW - 2)])
+    lower_odd = lax.ppermute(odd, "row", [(row, row + 2) for row in range(1, N_ROW - 2, 2)])
+    upper_even = lax.ppermute(even, "row", [(row, row - 2) for row in range(3, N_ROW, 2)])
+    outgoing, shares = call(
+        rows_kernel,
+        [(PARTS * 16, 128), (N_COL, 2, LOW, COLS)],
+        (0, 1),
+        pos,
+        leds,
+        own,
+        lower_even,
+        lower_odd,
+        upper_even,
+        upper_odd,
+        twist,
+        part_table,
+    )([pltpu.VMEM((N_COL, 2, LOW, COLS), F32), pltpu.VMEM((4, COLS, 128), F32)])
+    back_shares = [shares[0]] + [
+        lax.ppermute(shares[step], "col", [(at, (at + step) % N_COL) for at in range(N_COL)])
+        for step in range(1, N_COL)
+    ]
+    (total,) = call(assemble_kernel, [(2, ROWS, COLS)], (0,), pos, *back_shares)()
     incoming = lax.all_to_all(
         outgoing.reshape(PARTS, 16, 128), ("row", "col"), split_axis=0, concat_axis=0, tiled=True
     ).reshape(PARTS * 16, 128)
     (image,) = call(final_kernel, [(2, LOW, N)], (), incoming, twist, part_table)(
         [pltpu.VMEM((2, COLS, PARTS), F32)]
     )
-    return (jnp.stack(totals), image)
+    return (total, image)
 
 
 def solution(mesh):

time: 241 us -> 229 us (0.950)
  starting transfers between devices: 66.2 us -> 45.5 us
  blocking collectives: 19.4 us -> 26.7 us
  waiting for transfers between devices: 120 us -> 113 us
  Pallas kernels: 25.7 us -> 31 us
  local copies, waits for them, and re-layouts: 5.53 us -> 10.2 us
  other arithmetic: 2.81 us -> 0.25 us
    all_to_all x1, waiting for transfers between devices: 50.7 us -> 2.63 us  [on_device(): lax.all_to_all(outgoing.reshape(PARTS, 16, 128), ('row', 'col'), split_ax...]
    ppermute x2, starting transfers between devices: 30.7 us -> 0.37 us  [on_device(): other = lax.ppermute(send, BOTH, PARTNERS)]
    ppermute x4 -> x11, waiting for transfers between devices: 36.6 us -> 58.6 us  [the longest x7 35.4 us: on_device(): lax.ppermute(shares[step], 'col', [(at, (at + step) % N_COL) for at in ra...]
    ppermute x1, waiting for transfers between devices: 10.6 us -> 26.9 us  [on_device(): from_lower = lax.ppermute(to_upper, BOTH, UP)]
    ppermute x4 -> x11, starting transfers between devices: 6.36 us -> 20 us  [the longest x7 11.7 us: on_device(): lax.ppermute(shares[step], 'col', [(at, (at + step) % N_COL) for at in ra...]
    ppermute x1, waiting for transfers between devices: 5.63 us -> 13.8 us  [on_device(): far_amp = lax.ppermute(measured[:, :ROWS], BOTH, FAR)]
    unnamed x0 -> x1, blocking collectives: none -> 7.25 us
    pallas_call x9 -> x11, Pallas kernels: 25.7 us -> 31 us  [call(): pl.pallas_call(kernel, out_shape=tuple((jax.ShapeDtypeStruct(shape, F32)...]
  transfers between devices with their start and end apart: 14 -> 20, of which waited for: 8 -> 13; matrix products, arithmetic and copies ran while one was open for 2% -> 2% of each run, Pallas kernels for 3% -> 6%
where the time goes in v2:
time: 229 us
  waiting for transfers between devices  113 us (49%)
  starting transfers between devices  45.5 us (20%)
  Pallas kernels  31 us (14%)
  blocking collectives  26.7 us (12%)
  local copies, waits for them, and re-layouts  10.2 us (4%)
    ppermute x7, waiting for transfers between devices, on_device(): lax.ppermute(shares[step], 'col', [(at, (at + step) % N_COL) for at in ra...  35.4 us
    pallas_call x11, Pallas kernels, call(): pl.pallas_call(kernel, out_shape=tuple((jax.ShapeDtypeStruct(shape, F32)...  31 us
    ppermute x1, waiting for transfers between devices, on_device(): from_lower = lax.ppermute(to_upper, BOTH, UP)  26.9 us
    all_to_all x1, blocking collectives, on_device(): lax.all_to_all(grad, 'col', split_axis=0, concat_axis=0, tiled=True, axis...  19.5 us
    ppermute x1, waiting for transfers between devices, on_device(): lax.ppermute(odd, 'row', [(row, row - 2) for row in range(2, N_ROW)] + [(...  17.2 us
    ppermute x1, waiting for transfers between devices, on_device(): far_amp = lax.ppermute(measured[:, :ROWS], BOTH, FAR)  13.8 us
    ppermute x7, starting transfers between devices, on_device(): lax.ppermute(shares[step], 'col', [(at, (at + step) % N_COL) for at in ra...  11.7 us
    ppermute x2, waiting for transfers between devices, on_device(): other = lax.ppermute(send, BOTH, PARTNERS)  7.75 us
  transfers between devices with their start and end apart: 20, of which 13 were waited for; matrix products, arithmetic and copies ran while one was open for 2% of the time, Pallas kernels for 6%

profile of v2, /device:TPU:1, one launch (start us, length us, event | category | flops | bytes accessed | tf_op | source)
XLA Modules:
  0.0 228.7 jit_solution(16600865146469540709)
XLA Ops:
  0.6 3.9 %collective-permute-start = (s32[2]{0:T(128)}, s32[2]{0:T(128)S(1)}, u32[]{:S(2)}, u32[]{:S(2)}) collective-permute-start(s32[2]{0:T(128)} %bitcast.29), channel_id=1, source_target_pairs={{0,16},{1,17},{2,18},{3,19},{4,20},{5,21},{6,22},{7,23},{8,24},{9,... | collective-permute-start | bytes 32 | tf_op jit(solution)/shard_map/ppermute | solution.py:358
  7.0 3.8 %collective-permute-done.lower = s32[2]{0:T(128)S(1)} collective-permute-done((s32[2]{0:T(128)}, s32[2]{0:T(128)S(1)}, u32[]{:S(2)}, u32[]{:S(2)}) %collective-permute-start) | collective-permute-done | bytes 40 | tf_op jit(solution)/shard_map/ppermute | solution.py:358
  12.8 2.7 %collective-permute-start.2 = (f32[2,256,512]{2,1,0:T(8,128)}, f32[2,256,512]{2,1,0:T(8,128)S(1)}, u32[]{:S(2)}, u32[]{:S(2)}) collective-permute-start(f32[2,256,512]{2,1,0:T(8,128)} %get-tuple-element.8), channel_id=1, source_target_pairs={{1,17},{3,19},{5,21},{7,23},{8,24},{9,25},{10,26},{11,27},{12,28},... | collective-permute-start | bytes 3145736 | tf_op jit(solution)/shard_map/ppermute | solution.py:373
  18.4 4.2 %collective-permute-start.5 = (f32[512,256]{1,0:T(8,128)S(1)}, f32[512,256]{1,0:T(8,128)S(1)}, u32[]{:S(2)}, u32[]{:S(2)}) collective-permute-start(f32[512,256]{1,0:T(8,128)S(1)} %dynamic-slice_bitcast_fusion), channel_id=1, source_target_pairs={{0,8},{1,9},{2,10},{3,11},{4,12},{5,13},{6,14},{7,15},{8,0},{9,17}... | collective-permute-start | bytes 1572872 | tf_op jit(solution)/shard_map/ppermute | solution.py:367
  23.8 4.9 %collective-permute-start.6 = (f32[512,256]{1,0:T(8,128)S(1)}, f32[512,256]{1,0:T(8,128)S(1)}, u32[]{:S(2)}, u32[]{:S(2)}) collective-permute-start(f32[512,256]{1,0:T(8,128)S(1)} %slice.44), channel_id=1, source_target_pairs={{1,17},{3,19},{5,21},{7,23},{17,33},{19,35},{21,37},{23,39},{33,49... | collective-permute-start | bytes 1572872 | tf_op jit(solution)/shard_map/ppermute | solution.py:368
  30.7 26.9 %collective-permute-done.2.from_lower = f32[2,256,512]{2,1,0:T(8,128)S(1)} collective-permute-done((f32[2,256,512]{2,1,0:T(8,128)}, f32[2,256,512]{2,1,0:T(8,128)S(1)}, u32[]{:S(2)}, u32[]{:S(2)}) %collective-permute-start.2) | collective-permute-done | bytes 1048608 | tf_op jit(solution)/shard_map/ppermute | solution.py:373
  60.4 3.6 %shard_map.89.wave = f32[2,512,256]{2,1,0:T(8,128)S(1)} custom-call(s32[2]{0:T(128)S(1)} %pad_add_fusion.pos, s32[2]{0:T(128)S(1)} %bitcast.34, s32[2]{0:T(128)S(1)} %collective-permute-done.lower, s32[2]{0:T(128)S(1)} %collective-permute-done.1.upper, f32[2,256,1024]{2,1,0:T(8,128)S(1)} %shard_map.86.spec, ...), custom_call_target="tpu_custom_call" | custom-call | tf_op jit(solution)/shard_map/pallas_call | solution.py:108
  64.0 13.8 %collective-permute-done.6.far_amp = f32[512,256]{1,0:T(8,128)S(1)} collective-permute-done((f32[512,256]{1,0:T(8,128)S(1)}, f32[512,256]{1,0:T(8,128)S(1)}, u32[]{:S(2)}, u32[]{:S(2)}) %collective-permute-start.6) | collective-permute-done | bytes 524320 | tf_op jit(solution)/shard_map/ppermute | solution.py:368
  77.8 3.6 %shard_map.91 = (f32[2,512,256]{2,1,0:T(8,128)S(1)}, f32[2,256,256]{2,1,0:T(8,128)S(1)}) custom-call(s32[2]{0:T(128)S(1)} %pad_add_fusion.pos, f32[2,512,256]{2,1,0:T(8,128)S(1)} %shard_map.89.wave, f32[2,256,256]{2,1,0:T(8,128)S(1)} %collective-permute-done.4.other, f32[512,512]{1,0:T(8,128)S(1)} %bitcast.27, ...), custom_call_target="tpu_custom_call" | custom-call | tf_op jit(solution)/shard_map/pallas_call | solution.py:108
  81.7 3.6 %shard_map.92.part = f32[2,256,512]{2,1,0:T(8,128)S(1)} custom-call(s32[2]{0:T(128)S(1)} %pad_add_fusion.pos, f32[2,512,256]{2,1,0:T(8,128)S(1)} %get-tuple-element.10.fit, bf16[4,512,512]{2,1,0:T(8,128)(2,1)S(1)} %copy-done), custom_call_target="tpu_custom_call" | custom-call | tf_op jit(solution)/shard_map/pallas_call | solution.py:108
  85.3 7.7 %collective-permute-done.7.other = f32[2,256,256]{2,1,0:T(8,128)S(1)} collective-permute-done((f32[2,256,256]{2,1,0:T(8,128)S(1)}, f32[2,256,256]{2,1,0:T(8,128)S(1)}, u32[]{:S(2)}, u32[]{:S(2)}) %collective-permute-start.7) | collective-permute-done | bytes 524320 | tf_op jit(solution)/shard_map/ppermute | solution.py:383
  94.8 19.5 %all_to_all.10.own = f32[8,2,32,512]{3,2,1,0:T(8,128)S(1)} all-to-all(f32[8,2,32,512]{3,2,1,0:T(8,128)S(1)} %shard_map.93), channel_id=1, replica_groups={{0,2,4,6,1,3,5,7},{8,10,12,14,9,11,13,15},{16,18,20,22,17,19,21,23},{24..., dimensions={0} | all-to-all | bytes 2097152 | tf_op jit(solution)/shard_map/all_to_all | solution.py:387
  117.9 4.3 %collective-permute-start.8 = (f32[4,2,32,512]{3,2,1,0:T(8,128)}, f32[4,2,32,512]{3,2,1,0:T(8,128)S(1)}, u32[]{:S(2)}, u32[]{:S(2)}) collective-permute-start(f32[4,2,32,512]{3,2,1,0:T(8,128)} %get-tuple-element.23), channel_id=1, source_target_pairs={{0,16},{8,24},{16,32},{24,40},{32,48},{40,56},{48,64},{56,72},{64,... | collective-permute-start | bytes 1572872 | tf_op jit(solution)/shard_map/ppermute | solution.py:389
  125.1 7.2 %all-reduce = s32[48]{0:T(128)S(1)} all-reduce(s32[48]{0:T(128)S(1)} %add_dynamic-update-slice_fusion), channel_id=2, replica_groups=mesh['row'=32,'col'=8] {'col'}, use_global_device_ids=true, to_apply=%add | all-reduce | flops 48 | bytes 384
  132.5 17.2 %collective-permute-done.11.upper_odd = f32[4,2,32,512]{3,2,1,0:T(8,128)S(1)} collective-permute-done((f32[4,2,32,512]{3,2,1,0:T(8,128)}, f32[4,2,32,512]{3,2,1,0:T(8,128)S(1)}, u32[]{:S(2)}, u32[]{:S(2)}) %collective-permute-start.11) | collective-permute-done | bytes 524320 | tf_op jit(solution)/shard_map/ppermute | solution.py:390
  149.6 6.1 %collective-permute-done.8.lower_even = f32[4,2,32,512]{3,2,1,0:T(8,128)S(1)} collective-permute-done((f32[4,2,32,512]{3,2,1,0:T(8,128)}, f32[4,2,32,512]{3,2,1,0:T(8,128)S(1)}, u32[]{:S(2)}, u32[]{:S(2)}) %collective-permute-start.8) | collective-permute-done | bytes 524320 | tf_op jit(solution)/shard_map/ppermute | solution.py:389
  155.7 5.5 %shard_map.94 = (f32[4096,128]{1,0:T(8,128)S(1)}, f32[8,2,32,1024]{3,2,1,0:T(8,128)S(1)}) custom-call(s32[2]{0:T(128)S(1)} %pad_add_fusion.pos, s32[8,6]{1,0:T(8,128)S(1)} %reshape.13.leds, f32[8,2,32,512]{3,2,1,0:T(8,128)S(1)} %all_to_all.10.own, f32[4,2,32,512]{3,2,1,0:T(8,128)S(1)} %collective-permute-done.8.lower_even, ...), custom_call_target="tpu_custom_call" | custom-call | tf_op jit(solution)/shard_map/pallas_call | solution.py:108
  163.9 7.2 %all-to-all-start.1 = ((f32[256,16,128]{2,1,0:T(8,128)}), f32[256,16,128]{2,1,0:T(8,128)S(1)}, u32[]{:S(2)}, u32[]{:S(2)}) async-start(f32[256,16,128]{2,1,0:T(8,128)} %bitcast.28), calls=%async_computation.1 | async-start | bytes 4194304 | tf_op jit(solution)/shard_map/all_to_all | solution.py:412
  181.3 2.9 %collective-permute-done.12.refs_1_ = f32[2,32,1024]{2,1,0:T(8,128)S(1)} collective-permute-done((f32[2,32,1024]{2,1,0:T(8,128)S(1)}, f32[2,32,1024]{2,1,0:T(8,128)S(1)}, u32[]{:S(2)}, u32[]{:S(2)}) %collective-permute-start.12) | collective-permute-done | bytes 262176 | tf_op jit(solution)/shard_map/ppermute | solution.py:408
  184.2 3.2 %collective-permute-start.17 = (f32[2,32,1024]{2,1,0:T(8,128)S(1)}, f32[2,32,1024]{2,1,0:T(8,128)S(1)}, u32[]{:S(2)}, u32[]{:S(2)}) collective-permute-start(f32[2,32,1024]{2,1,0:T(8,128)S(1)} %get-tuple-element.15), channel_id=1, source_target_pairs={{0,6},{1,7},{2,0},{3,1},{4,2},{5,3},{6,4},{7,5},{8,14},{9,15},{10,... | collective-permute-start | bytes 786440 | tf_op jit(solution)/shard_map/ppermute | solution.py:408
  187.3 16.1 %collective-permute-done.13.refs_2_ = f32[2,32,1024]{2,1,0:T(8,128)S(1)} collective-permute-done((f32[2,32,1024]{2,1,0:T(8,128)S(1)}, f32[2,32,1024]{2,1,0:T(8,128)S(1)}, u32[]{:S(2)}, u32[]{:S(2)}) %collective-permute-start.13) | collective-permute-done | bytes 262176 | tf_op jit(solution)/shard_map/ppermute | solution.py:408
  203.5 7.3 %collective-permute-done.14.refs_3_ = f32[2,32,1024]{2,1,0:T(8,128)S(1)} collective-permute-done((f32[2,32,1024]{2,1,0:T(8,128)S(1)}, f32[2,32,1024]{2,1,0:T(8,128)S(1)}, u32[]{:S(2)}, u32[]{:S(2)}) %collective-permute-start.14) | collective-permute-done | bytes 262176 | tf_op jit(solution)/shard_map/ppermute | solution.py:408
  210.7 7.1 %collective-permute-done.15.refs_4_ = f32[2,32,1024]{2,1,0:T(8,128)S(1)} collective-permute-done((f32[2,32,1024]{2,1,0:T(8,128)S(1)}, f32[2,32,1024]{2,1,0:T(8,128)S(1)}, u32[]{:S(2)}, u32[]{:S(2)}) %collective-permute-start.15) | collective-permute-done | bytes 262176 | tf_op jit(solution)/shard_map/ppermute | solution.py:408
  224.4 4.3 %shard_map.96 = f32[2,32,8192]{2,1,0:T(8,128)} custom-call(f32[4096,128]{1,0:T(8,128)S(1)} %bitcast.25, f32[2,32,256]{2,1,0:T(8,128)S(1)} %copy-done.7, bf16[4,256,256]{2,1,0:T(8,128)(2,1)S(1)} %copy-done.2), custom_call_target="tpu_custom_call" | custom-call | tf_op jit(solution)/shard_map/pallas_call | solution.py:108
  (58 shorter events, 40.7 us)
Async XLA Ops:
  0.6 10.2 %collective-permute-start = (s32[2]{0:T(128)}, s32[2]{0:T(128)S(1)}, u32[]{:S(2)}, u32[]{:S(2)}) collective-permute-start(s32[2]{0:T(128)} %bitcast.29), channel_id=1, source_target_pairs={{0,16},{1,17},{2,18},{3,19},{4,20},{5,21},{6,22},{7,23},{8,24},{9,... | collective-permute-start | bytes 32 | tf_op jit(solution)/shard_map/ppermute | solution.py:358
  4.5 6.3 %collective-permute-start.1 = (s32[2]{0:T(128)}, s32[2]{0:T(128)S(1)}, u32[]{:S(2)}, u32[]{:S(2)}) collective-permute-start(s32[2]{0:T(128)} %bitcast.30), channel_id=1, source_target_pairs={{24,8},{25,9},{26,10},{27,11},{28,12},{29,13},{30,14},{31,15},{40,... | collective-permute-start | bytes 32 | tf_op jit(solution)/shard_map/ppermute | solution.py:359
  12.8 44.7 %collective-permute-start.2 = (f32[2,256,512]{2,1,0:T(8,128)}, f32[2,256,512]{2,1,0:T(8,128)S(1)}, u32[]{:S(2)}, u32[]{:S(2)}) collective-permute-start(f32[2,256,512]{2,1,0:T(8,128)} %get-tuple-element.8), channel_id=1, source_target_pairs={{1,17},{3,19},{5,21},{7,23},{8,24},{9,25},{10,26},{11,27},{12,28},... | collective-permute-start | bytes 3145736 | tf_op jit(solution)/shard_map/ppermute | solution.py:373
  15.6 42.0 %collective-permute-start.3 = (f32[2,256,512]{2,1,0:T(8,128)}, f32[2,256,512]{2,1,0:T(8,128)}, u32[]{:S(2)}, u32[]{:S(2)}) collective-permute-start(f32[2,256,512]{2,1,0:T(8,128)} %get-tuple-element.9), channel_id=1, source_target_pairs={{16,0},{18,2},{20,4},{22,6},{24,8},{25,9},{26,10},{27,11},{28,12},... | collective-permute-start | bytes 3145736 | tf_op jit(solution)/shard_map/ppermute | solution.py:372
  18.4 45.6 %collective-permute-start.5 = (f32[512,256]{1,0:T(8,128)S(1)}, f32[512,256]{1,0:T(8,128)S(1)}, u32[]{:S(2)}, u32[]{:S(2)}) collective-permute-start(f32[512,256]{1,0:T(8,128)S(1)} %dynamic-slice_bitcast_fusion), channel_id=1, source_target_pairs={{0,8},{1,9},{2,10},{3,11},{4,12},{5,13},{6,14},{7,15},{8,0},{9,17}... | collective-permute-start | bytes 1572872 | tf_op jit(solution)/shard_map/ppermute | solution.py:367
  22.6 34.9 %copy-start = (bf16[4,512,512]{2,1,0:T(8,128)(2,1)S(1)}, bf16[4,512,512]{2,1,0:T(8,128)(2,1)}, u32[]{:S(2)}) copy-start(bf16[4,512,512]{2,1,0:T(8,128)(2,1)} %constant.35.clone.table) | copy-start | bytes 6291460
  23.8 54.0 %collective-permute-start.6 = (f32[512,256]{1,0:T(8,128)S(1)}, f32[512,256]{1,0:T(8,128)S(1)}, u32[]{:S(2)}, u32[]{:S(2)}) collective-permute-start(f32[512,256]{1,0:T(8,128)S(1)} %slice.44), channel_id=1, source_target_pairs={{1,17},{3,19},{5,21},{7,23},{17,33},{19,35},{21,37},{23,39},{33,49... | collective-permute-start | bytes 1572872 | tf_op jit(solution)/shard_map/ppermute | solution.py:368
  60.3 17.5 %collective-permute-start.4 = (f32[2,256,256]{2,1,0:T(8,128)S(1)}, f32[2,256,256]{2,1,0:T(8,128)S(1)}, u32[]{:S(2)}, u32[]{:S(2)}) collective-permute-start(f32[2,256,256]{2,1,0:T(8,128)S(1)} %shard_map.90), channel_id=1, source_target_pairs={{0,8},{1,249},{2,10},{3,251},{4,12},{5,253},{6,14},{7,255},{8,0},{... | collective-permute-start | bytes 1572872 | tf_op jit(solution)/shard_map/ppermute | solution.py:378
  81.4 11.6 %collective-permute-start.7 = (f32[2,256,256]{2,1,0:T(8,128)S(1)}, f32[2,256,256]{2,1,0:T(8,128)S(1)}, u32[]{:S(2)}, u32[]{:S(2)}) collective-permute-start(f32[2,256,256]{2,1,0:T(8,128)S(1)} %get-tuple-element.11), channel_id=1, source_target_pairs={{0,8},{1,249},{2,10},{3,251},{4,12},{5,253},{6,14},{7,255},{8,0},{... | collective-permute-start | bytes 1572872 | tf_op jit(solution)/shard_map/ppermute | solution.py:383
  94.7 29.0 %copy-start.9 = (u32[256]{0:T(256)S(1)}, u32[256]{0:T(256)}, u32[]{:S(2)}) copy-start(u32[256]{0:T(256)} %constant.42) | copy-start | bytes 3076
  94.7 61.0 %copy-start.2 = (bf16[4,256,256]{2,1,0:T(8,128)(2,1)S(1)}, bf16[4,256,256]{2,1,0:T(8,128)(2,1)}, u32[]{:S(2)}) copy-start(bf16[4,256,256]{2,1,0:T(8,128)(2,1)} %constant.36.clone.table) | copy-start | bytes 1572868
  94.7 61.0 %copy-start.7 = (f32[2,32,256]{2,1,0:T(8,128)S(1)}, f32[2,32,256]{2,1,0:T(8,128)}, u32[]{:S(2)}) copy-start(f32[2,32,256]{2,1,0:T(8,128)} %constant.37.clone.twist) | copy-start | bytes 196612
  115.3 17.1 %collective-permute-start.10 = (f32[4,2,32,512]{3,2,1,0:T(8,128)}, f32[4,2,32,512]{3,2,1,0:T(8,128)S(1)}, u32[]{:S(2)}, u32[]{:S(2)}) collective-permute-start(f32[4,2,32,512]{3,2,1,0:T(8,128)} %get-tuple-element.23), channel_id=1, source_target_pairs={{24,8},{40,24},{56,40},{72,56},{88,72},{104,88},{120,104},{136,120... | collective-permute-start | bytes 1572872 | tf_op jit(solution)/shard_map/ppermute | solution.py:392
  116.0 33.6 %collective-permute-start.11 = (f32[4,2,32,512]{3,2,1,0:T(8,128)}, f32[4,2,32,512]{3,2,1,0:T(8,128)S(1)}, u32[]{:S(2)}, u32[]{:S(2)}) collective-permute-start(f32[4,2,32,512]{3,2,1,0:T(8,128)} %get-tuple-element.22), channel_id=1, source_target_pairs={{16,0},{24,8},{32,16},{40,24},{48,32},{56,40},{64,48},{72,56},{80,... | collective-permute-start | bytes 1572872 | tf_op jit(solution)/shard_map/ppermute | solution.py:390
  117.9 37.7 %collective-permute-start.8 = (f32[4,2,32,512]{3,2,1,0:T(8,128)}, f32[4,2,32,512]{3,2,1,0:T(8,128)S(1)}, u32[]{:S(2)}, u32[]{:S(2)}) collective-permute-start(f32[4,2,32,512]{3,2,1,0:T(8,128)} %get-tuple-element.23), channel_id=1, source_target_pairs={{0,16},{8,24},{16,32},{24,40},{32,48},{40,56},{48,64},{56,72},{64,... | collective-permute-start | bytes 1572872 | tf_op jit(solution)/shard_map/ppermute | solution.py:389
  122.2 33.5 %collective-permute-start.9 = (f32[4,2,32,512]{3,2,1,0:T(8,128)}, f32[4,2,32,512]{3,2,1,0:T(8,128)}, u32[]{:S(2)}, u32[]{:S(2)}) collective-permute-start(f32[4,2,32,512]{3,2,1,0:T(8,128)} %get-tuple-element.22), channel_id=1, source_target_pairs={{8,24},{24,40},{40,56},{56,72},{72,88},{88,104},{104,120},{120,136... | collective-permute-start | bytes 1572872 | tf_op jit(solution)/shard_map/ppermute | solution.py:391
  163.9 60.6 %all-to-all-start.1 = ((f32[256,16,128]{2,1,0:T(8,128)}), f32[256,16,128]{2,1,0:T(8,128)S(1)}, u32[]{:S(2)}, u32[]{:S(2)}) async-start(f32[256,16,128]{2,1,0:T(8,128)} %bitcast.28), calls=%async_computation.1 | async-start | bytes 4194304 | tf_op jit(solution)/shard_map/all_to_all | solution.py:412
  172.7 11.5 %collective-permute-start.12 = (f32[2,32,1024]{2,1,0:T(8,128)S(1)}, f32[2,32,1024]{2,1,0:T(8,128)S(1)}, u32[]{:S(2)}, u32[]{:S(2)}) collective-permute-start(f32[2,32,1024]{2,1,0:T(8,128)S(1)} %get-tuple-element.20), channel_id=1, source_target_pairs={{0,1},{1,2},{2,3},{3,4},{4,5},{5,6},{6,7},{7,0},{8,9},{9,10},{10,1... | collective-permute-start | bytes 786440 | tf_op jit(solution)/shard_map/ppermute | solution.py:408
  174.4 29.1 %collective-permute-start.13 = (f32[2,32,1024]{2,1,0:T(8,128)S(1)}, f32[2,32,1024]{2,1,0:T(8,128)S(1)}, u32[]{:S(2)}, u32[]{:S(2)}) collective-permute-start(f32[2,32,1024]{2,1,0:T(8,128)S(1)} %get-tuple-element.19), channel_id=1, source_target_pairs={{0,2},{1,3},{2,4},{3,5},{4,6},{5,7},{6,0},{7,1},{8,10},{9,11},{10,... | collective-permute-start | bytes 786440 | tf_op jit(solution)/shard_map/ppermute | solution.py:408
  175.6 35.2 %collective-permute-start.14 = (f32[2,32,1024]{2,1,0:T(8,128)S(1)}, f32[2,32,1024]{2,1,0:T(8,128)S(1)}, u32[]{:S(2)}, u32[]{:S(2)}) collective-permute-start(f32[2,32,1024]{2,1,0:T(8,128)S(1)} %get-tuple-element.18), channel_id=1, source_target_pairs={{0,3},{1,4},{2,5},{3,6},{4,7},{5,0},{6,1},{7,2},{8,11},{9,12},{10,... | collective-permute-start | bytes 786440 | tf_op jit(solution)/shard_map/ppermute | solution.py:408
  177.2 40.6 %collective-permute-start.15 = (f32[2,32,1024]{2,1,0:T(8,128)S(1)}, f32[2,32,1024]{2,1,0:T(8,128)S(1)}, u32[]{:S(2)}, u32[]{:S(2)}) collective-permute-start(f32[2,32,1024]{2,1,0:T(8,128)S(1)} %get-tuple-element.17), channel_id=1, source_target_pairs={{0,4},{1,5},{2,6},{3,7},{4,0},{5,1},{6,2},{7,3},{8,12},{9,13},{10,... | collective-permute-start | bytes 786440 | tf_op jit(solution)/shard_map/ppermute | solution.py:408
  178.6 40.0 %collective-permute-start.16 = (f32[2,32,1024]{2,1,0:T(8,128)S(1)}, f32[2,32,1024]{2,1,0:T(8,128)S(1)}, u32[]{:S(2)}, u32[]{:S(2)}) collective-permute-start(f32[2,32,1024]{2,1,0:T(8,128)S(1)} %get-tuple-element.16), channel_id=1, source_target_pairs={{0,5},{1,6},{2,7},{3,0},{4,1},{5,2},{6,3},{7,4},{8,13},{9,14},{10,... | collective-permute-start | bytes 786440 | tf_op jit(solution)/shard_map/ppermute | solution.py:408
  184.2 34.5 %collective-permute-start.17 = (f32[2,32,1024]{2,1,0:T(8,128)S(1)}, f32[2,32,1024]{2,1,0:T(8,128)S(1)}, u32[]{:S(2)}, u32[]{:S(2)}) collective-permute-start(f32[2,32,1024]{2,1,0:T(8,128)S(1)} %get-tuple-element.15), channel_id=1, source_target_pairs={{0,6},{1,7},{2,0},{3,1},{4,2},{5,3},{6,4},{7,5},{8,14},{9,15},{10,... | collective-permute-start | bytes 786440 | tf_op jit(solution)/shard_map/ppermute | solution.py:408
  203.5 16.3 %collective-permute-start.18 = (f32[2,32,1024]{2,1,0:T(8,128)S(1)}, f32[2,32,1024]{2,1,0:T(8,128)S(1)}, u32[]{:S(2)}, u32[]{:S(2)}) collective-permute-start(f32[2,32,1024]{2,1,0:T(8,128)S(1)} %get-tuple-element.14), channel_id=1, source_target_pairs={{0,7},{1,0},{2,1},{3,2},{4,3},{5,4},{6,5},{7,6},{8,15},{9,8},{10,9... | collective-permute-start | bytes 786440 | tf_op jit(solution)/shard_map/ppermute | solution.py:408
  (6 other events, 37.4 us)

commit v3 on v2

--- a/solution.py
+++ b/solution.py
@@ -21,8 +21,8 @@
 ORDER = [0, 2, 4, 6, 1, 3, 5, 7]
 F32 = jnp.float32
 BF16 = jnp.bfloat16
-SLOW = 10**11
 VMEM_BYTES = 32 * 1024 * 1024
+ROWS_VMEM_BYTES = 59 * 1024 * 1024
 
 
 def halves(table):
@@ -52,22 +52,32 @@
     return jnp.dot(left, right, preferred_element_type=F32)
 
 
-def mm3(left, right):
-    return mm(left[0], right[0]) + mm(left[0], right[1]) + mm(left[1], right[0])
+def six(first, second, axis):
+    return jnp.concatenate([first[0], first[1], first[0], second[0], second[1], second[0]], axis=axis)
+
+
+def six_table(first, second, axis):
+    return jnp.concatenate([first[0], first[0], first[1], second[0], second[0], second[1]], axis=axis)
+
+
+def minus(pair):
+    return -pair[0], -pair[1]
 
 
 def complex_times_table(re, im, cos, sin, sign):
-    rc, rs, ic, is_ = mm3(re, cos), mm3(re, sin), mm3(im, cos), mm3(im, sin)
-    if sign > 0:
-        return rc - is_, rs + ic
-    return rc + is_, ic - rs
+    first, second = (minus(im), re) if sign > 0 else (im, minus(re))
+    return (
+        mm(six(re, first, 1), six_table(cos, sin, 0)),
+        mm(six(second, im, 1), six_table(sin, cos, 0)),
+    )
 
 
 def table_times_complex(cos, sin, sign, re, im):
-    rc, rs, ic, is_ = mm3(cos, re), mm3(sin, re), mm3(cos, im), mm3(sin, im)
-    if sign > 0:
-        return rc - is_, rs + ic
-    return rc + is_, ic - rs
+    first, second = (minus(im), re) if sign > 0 else (im, minus(re))
+    return (
+        mm(six_table(cos, sin, 1), six(re, first, 0)),
+        mm(six_table(sin, cos, 1), six(second, im, 0)),
+    )
 
 
 def turn(value, numer, denom):
@@ -103,16 +113,16 @@
     return first + second
 
 
-def call(kernel, outs, smem, *args, cost=None):
+def call(kernel, outs, smem, *args, cost=None, hbm=False, limit=VMEM_BYTES):
     specs = [pl.BlockSpec(memory_space=pltpu.SMEM if at in smem else pltpu.VMEM) for at in range(len(args))]
     return lambda scratch=(): pl.pallas_call(
         kernel,
         out_shape=tuple(jax.ShapeDtypeStruct(shape, F32) for shape in outs),
         in_specs=specs,
-        out_specs=tuple(pl.BlockSpec(memory_space=pltpu.VMEM) for _ in outs),
+        out_specs=tuple(pl.BlockSpec(memory_space=pltpu.HBM if hbm else pltpu.VMEM) for _ in outs),
         scratch_shapes=scratch,
         cost_estimate=cost and pl.CostEstimate(flops=cost, bytes_accessed=0, transcendentals=0),
-        compiler_params=pltpu.CompilerParams(vmem_limit_bytes=VMEM_BYTES),
+        compiler_params=pltpu.CompilerParams(vmem_limit_bytes=limit),
     )(*args)
 
 
@@ -192,7 +202,7 @@
     wave[0], wave[1] = table_times_complex(cos, sin, 1, split(re), split(im))
 
 
-def fit_kernel(pos, wave, other, amplitude, near_amp, far_amp, table, fit, send):
+def fit_kernel(pos, far_amp, near_amp, amplitude, wave, other, table, fit, send):
     parity = lax.rem(pos[0], 2)
     moved = jnp.logical_and(parity == 0, lax.rem(pos[1], 2) == 1)
     cos, sin = half_cols(table, 1 - parity)
@@ -227,7 +237,7 @@
         grad[at, 1] = back_im[col * LOW : col * LOW + LOW]
 
 
-def rows_kernel(pos, leds, own, lower_even, lower_odd, upper_even, upper_odd, twist, table, outgoing, shares, pencil, digits):
+def rows_kernel(pos, leds, own, lower_odd, upper_even, lower_even, upper_odd, twist, table, outgoing, shares, pencil, spectra, digits, sems):
     row, col = pos[0], pos[1]
     cols = lax.broadcasted_iota(jnp.int32, (LOW, M), 1)
     rows = lax.broadcasted_iota(jnp.int32, (LOW, M), 0) + col * LOW
@@ -235,7 +245,6 @@
         lower, upper = (lower_even, upper_even) if at < 4 else (lower_odd, upper_odd)
         corner = [leds[source_col, index] for index in range(6)]
         around = corners((row, source_col), corner[:2], corner[2:4], corner[4:])
-        place = lax.rem(source_col - col + N_COL, N_COL)
         for part in range(2):
             left = right = 0.0
             for (at_row, at_col), source in zip(around, (own[at, part], lower[at % 4, part], upper[at % 4, part])):
@@ -244,8 +253,14 @@
                 right = right + jnp.where(cols < at_col, value, 0.0)
             pencil[source_col, part, :, :M] = left
             pencil[source_col, part, :, M:] = right
-            shares[place, part, :, :M] = left
-            shares[place, part, :, M:] = right
+    copies = [
+        pltpu.make_async_copy(
+            pencil.at[source_col], shares.at[lax.rem(source_col - col + N_COL, N_COL)], sems.at[source_col]
+        )
+        for source_col in range(N_COL)
+    ]
+    for copy in copies:
+        copy.start()
     for group in range(LOW // 8):
         for tile in range(2):
             lanes = slice(tile * 128, tile * 128 + 128)
@@ -274,7 +289,12 @@
     for part, flat in enumerate(complex_times_table(re, im, cos, sin, 1)):
         turned = flat.T
         for at in range(8):
-            outgoing[pl.ds(part * 8 + at, PARTS, 16), :] = turned[:, at * 128 : at * 128 + 128]
+            spectra[pl.ds(part * 8 + at, PARTS, 16), :] = turned[:, at * 128 : at * 128 + 128]
+    last = pltpu.make_async_copy(spectra, outgoing, sems.at[N_COL])
+    last.start()
+    for copy in copies:
+        copy.wait()
+    last.wait()
 
 
 def assemble_kernel(pos, *refs):
@@ -285,7 +305,7 @@
             total[part, where, :] = share[part]
 
 
-def final_kernel(incoming, twist, table, image, digits):
+def final_kernel(incoming, twist, table, result, image, digits, sems):
     pair = []
     for part in range(2):
         flat = jnp.concatenate([incoming[pl.ds(part * 8 + at, PARTS, 16), :] for at in range(8)], axis=1)
@@ -293,6 +313,7 @@
     cos = (table[0], table[1])
     sin = (table[2], table[3])
     digits[0], digits[1] = complex_times_table(*pair, cos, sin, 1)
+    copies = []
     for group in range(LOW // 8):
         for tile in range(2):
             lanes = slice(tile * 128, tile * 128 + 128)
@@ -311,6 +332,11 @@
                         group * 8 : group * 8 + 8,
                         at * 256 + tile * 128 : at * 256 + tile * 128 + 128,
                     ] = value[part]
+        rows = pl.ds(group * 8, 8)
+        copies.append(pltpu.make_async_copy(image.at[:, rows], result.at[:, rows], sems.at[group]))
+        copies[-1].start()
+    for copy in copies:
+        copy.wait()
 
 
 def moves(rule):
@@ -367,8 +393,8 @@
     near_amp = lax.ppermute(near_half, BOTH, NEAR)
     far_amp = lax.ppermute(measured[:, :ROWS], BOTH, FAR)
 
-    (staged,) = call(stage_kernel, [(2, ROWS, COLS)], (), spectrum)()
-    to_lower, to_upper = call(pack_kernel, [(2,) + half, (2,) + half], smem, *where, staged)()
+    (staged,) = call(stage_kernel, [(2, ROWS, COLS)], (), spectrum, limit=4 * 1024 * 1024)()
+    to_lower, to_upper = call(pack_kernel, [(2,) + half, (2,) + half], smem, *where, staged, limit=4 * 1024 * 1024)()
     from_upper = lax.ppermute(to_lower, BOTH, DOWN)
     from_lower = lax.ppermute(to_upper, BOTH, UP)
     (rolled,) = call(pupil_kernel, [(2,) + half], smem, *where, pupil)()
@@ -378,7 +404,7 @@
     other = lax.ppermute(send, BOTH, PARTNERS)
     (wave,) = call(keep_kernel, [(2, M, ROWS)], smem, *sources)()
     fit, send = call(
-        fit_kernel, [(2, M, ROWS), quarter], (0,), pos, wave, other, measured, near_amp, far_amp, window_table
+        fit_kernel, [(2, M, ROWS), quarter], (0,), pos, far_amp, near_amp, measured, wave, other, window_table
     )()
     other = lax.ppermute(send, BOTH, PARTNERS)
     (part,) = call(stay_kernel, [(2,) + half], (0,), pos, fit, window_table)()
@@ -397,13 +423,22 @@
         pos,
         leds,
         own,
-        lower_even,
         lower_odd,
         upper_even,
+        lower_even,
         upper_odd,
         twist,
         part_table,
-    )([pltpu.VMEM((N_COL, 2, LOW, COLS), F32), pltpu.VMEM((4, COLS, 128), F32)])
+        hbm=True,
+        limit=ROWS_VMEM_BYTES,
+    )(
+        [
+            pltpu.VMEM((N_COL, 2, LOW, COLS), F32),
+            pltpu.VMEM((PARTS * 16, 128), F32),
+            pltpu.VMEM((4, COLS, 128), F32),
+            pltpu.SemaphoreType.DMA((N_COL + 1,)),
+        ]
+    )
     back_shares = [shares[0]] + [
         lax.ppermute(shares[step], "col", [(at, (at + step) % N_COL) for at in range(N_COL)])
         for step in range(1, N_COL)
@@ -412,8 +447,8 @@
     incoming = lax.all_to_all(
         outgoing.reshape(PARTS, 16, 128), ("row", "col"), split_axis=0, concat_axis=0, tiled=True
     ).reshape(PARTS * 16, 128)
-    (image,) = call(final_kernel, [(2, LOW, N)], (), incoming, twist, part_table)(
-        [pltpu.VMEM((2, COLS, PARTS), F32)]
+    (image,) = call(final_kernel, [(2, LOW, N)], (), incoming, twist, part_table, hbm=True)(
+        [pltpu.VMEM((2, LOW, N), F32), pltpu.VMEM((2, COLS, PARTS), F32), pltpu.SemaphoreType.DMA((LOW // 8,))]
     )
     return (total, image)
 

time: 229 us -> 228 us (level)
    ppermute x1, waiting for transfers between devices: 17.2 us -> 0.01 us  [on_device(): lax.ppermute(odd, 'row', [(row, row - 2) for row in range(2, N_ROW)] + [(...]
    ppermute x1, waiting for transfers between devices: 6.05 us -> 20.5 us  [on_device(): lax.ppermute(even, 'row', [(row, row + 2) for row in range(N_ROW - 2)])]
    all_to_all x1, starting transfers between devices: 7.16 us -> 12.1 us  [on_device(): lax.all_to_all(outgoing.reshape(PARTS, 16, 128), ('row', 'col'), split_ax...]
    ppermute x1, starting transfers between devices: 4.29 us -> 1.31 us  [on_device(): lax.ppermute(even, 'row', [(row, row + 2) for row in range(N_ROW - 2)])]
    unnamed x22 -> x32, local copies, waits for them, and re-layouts: 4.9 us -> 4.17 us
  transfers between devices with their start and end apart: 20 -> 20, of which waited for: 13 -> 12; matrix products, arithmetic and copies ran while one was open for 2% -> 3% of each run, Pallas kernels for 6% -> 6%
where the time goes in v3:
time: 228 us
  waiting for transfers between devices  112 us (49%)
  starting transfers between devices  46.5 us (20%)
  Pallas kernels  30.5 us (13%)
  blocking collectives  26.1 us (11%)
  local copies, waits for them, and re-layouts  10.1 us (4%)
    ppermute x7, waiting for transfers between devices, on_device(): lax.ppermute(shares[step], 'col', [(at, (at + step) % N_COL) for at in ra...  35.4 us
    pallas_call x11, Pallas kernels, call(): pl.pallas_call(kernel, out_shape=tuple((jax.ShapeDtypeStruct(shape, F32)...  30.5 us
    ppermute x1, waiting for transfers between devices, on_device(): from_lower = lax.ppermute(to_upper, BOTH, UP)  26.8 us
    ppermute x1, waiting for transfers between devices, on_device(): lax.ppermute(even, 'row', [(row, row + 2) for row in range(N_ROW - 2)])  20.5 us
    all_to_all x1, blocking collectives, on_device(): lax.all_to_all(grad, 'col', split_axis=0, concat_axis=0, tiled=True, axis...  19.4 us
    ppermute x1, waiting for transfers between devices, on_device(): far_amp = lax.ppermute(measured[:, :ROWS], BOTH, FAR)  14 us
    all_to_all x1, starting transfers between devices, on_device(): lax.all_to_all(outgoing.reshape(PARTS, 16, 128), ('row', 'col'), split_ax...  12.1 us
    ppermute x7, starting transfers between devices, on_device(): lax.ppermute(shares[step], 'col', [(at, (at + step) % N_COL) for at in ra...  11.6 us
  transfers between devices with their start and end apart: 20, of which 12 were waited for; matrix products, arithmetic and copies ran while one was open for 3% of the time, Pallas kernels for 6%

profile of v3, /device:TPU:1, one launch (start us, length us, event | category | flops | bytes accessed | tf_op | source)
XLA Modules:
  0.0 227.5 jit_solution(9403399019692448273)
XLA Ops:
  0.6 3.9 %collective-permute-start = (s32[2]{0:T(128)}, s32[2]{0:T(128)S(1)}, u32[]{:S(2)}, u32[]{:S(2)}) collective-permute-start(s32[2]{0:T(128)} %bitcast.28), channel_id=1, source_target_pairs={{0,16},{1,17},{2,18},{3,19},{4,20},{5,21},{6,22},{7,23},{8,24},{9,... | collective-permute-start | bytes 32 | tf_op jit(solution)/shard_map/ppermute | solution.py:384
  7.0 3.8 %collective-permute-done.lower = s32[2]{0:T(128)S(1)} collective-permute-done((s32[2]{0:T(128)}, s32[2]{0:T(128)S(1)}, u32[]{:S(2)}, u32[]{:S(2)}) %collective-permute-start) | collective-permute-done | bytes 40 | tf_op jit(solution)/shard_map/ppermute | solution.py:384
  12.8 2.7 %collective-permute-start.4 = (f32[2,256,512]{2,1,0:T(8,128)}, f32[2,256,512]{2,1,0:T(8,128)S(1)}, u32[]{:S(2)}, u32[]{:S(2)}) collective-permute-start(f32[2,256,512]{2,1,0:T(8,128)} %get-tuple-element.8), channel_id=1, source_target_pairs={{1,17},{3,19},{5,21},{7,23},{8,24},{9,25},{10,26},{11,27},{12,28},... | collective-permute-start | bytes 3145736 | tf_op jit(solution)/shard_map/ppermute | solution.py:399
  18.4 4.2 %collective-permute-start.3 = (f32[512,256]{1,0:T(8,128)S(1)}, f32[512,256]{1,0:T(8,128)S(1)}, u32[]{:S(2)}, u32[]{:S(2)}) collective-permute-start(f32[512,256]{1,0:T(8,128)S(1)} %dynamic-slice_bitcast_fusion), channel_id=1, source_target_pairs={{0,8},{1,9},{2,10},{3,11},{4,12},{5,13},{6,14},{7,15},{8,0},{9,17}... | collective-permute-start | bytes 1572872 | tf_op jit(solution)/shard_map/ppermute | solution.py:393
  23.8 4.9 %collective-permute-start.2 = (f32[512,256]{1,0:T(8,128)S(1)}, f32[512,256]{1,0:T(8,128)S(1)}, u32[]{:S(2)}, u32[]{:S(2)}) collective-permute-start(f32[512,256]{1,0:T(8,128)S(1)} %slice.44), channel_id=1, source_target_pairs={{1,17},{3,19},{5,21},{7,23},{17,33},{19,35},{21,37},{23,39},{33,49... | collective-permute-start | bytes 1572872 | tf_op jit(solution)/shard_map/ppermute | solution.py:394
  30.7 26.8 %collective-permute-done.4.from_lower = f32[2,256,512]{2,1,0:T(8,128)S(1)} collective-permute-done((f32[2,256,512]{2,1,0:T(8,128)}, f32[2,256,512]{2,1,0:T(8,128)S(1)}, u32[]{:S(2)}, u32[]{:S(2)}) %collective-permute-start.4) | collective-permute-done | bytes 1048608 | tf_op jit(solution)/shard_map/ppermute | solution.py:399
  57.6 2.6 %shard_map.90 = f32[2,256,256]{2,1,0:T(8,128)S(1)} custom-call(s32[2]{0:T(128)S(1)} %pad_add_fusion.pos, s32[2]{0:T(128)S(1)} %bitcast.32, s32[2]{0:T(128)S(1)} %collective-permute-done.lower, s32[2]{0:T(128)S(1)} %collective-permute-done.1.upper, f32[2,256,1024]{2,1,0:T(8,128)S(1)} %shard_map.86.spec, f32[2,256,512]{2,1,0:T(8,128)S(1)} %collective-permute-done.4.from_lower, ...), custom_call_target="tpu_custom_call" | custom-call | tf_op jit(solution)/shard_map/pallas_call | solution.py:118
  60.3 3.5 %shard_map.89.wave = f32[2,512,256]{2,1,0:T(8,128)S(1)} custom-call(s32[2]{0:T(128)S(1)} %pad_add_fusion.pos, s32[2]{0:T(128)S(1)} %bitcast.33, s32[2]{0:T(128)S(1)} %collective-permute-done.lower, s32[2]{0:T(128)S(1)} %collective-permute-done.1.upper, f32[2,256,1024]{2,1,0:T(8,128)S(1)} %shard_map.86.spec, ...), custom_call_target="tpu_custom_call" | custom-call | tf_op jit(solution)/shard_map/pallas_call | solution.py:118
  63.8 14.0 %collective-permute-done.2.far_amp = f32[512,256]{1,0:T(8,128)S(1)} collective-permute-done((f32[512,256]{1,0:T(8,128)S(1)}, f32[512,256]{1,0:T(8,128)S(1)}, u32[]{:S(2)}, u32[]{:S(2)}) %collective-permute-start.2) | collective-permute-done | bytes 524320 | tf_op jit(solution)/shard_map/ppermute | solution.py:394
  77.8 2.8 %shard_map.91 = (f32[2,512,256]{2,1,0:T(8,128)S(1)}, f32[2,256,256]{2,1,0:T(8,128)S(1)}) custom-call(s32[2]{0:T(128)S(1)} %pad_add_fusion.pos, f32[512,256]{1,0:T(8,128)S(1)} %collective-permute-done.2.far_amp, f32[512,256]{1,0:T(8,128)S(1)} %collective-permute-done.3.near_amp, f32[512,512]{1,0:T(8,128)S(1)} %bitcast.27, f32[2,512,256]{2,1,0:T(8,128)S(1)} %shard_map.89.wave, ...), custom_call_target="tpu_custom_call" | custom-call | tf_op jit(solution)/shard_map/pallas_call | solution.py:118
  83.1 8.9 %collective-permute-done.7.other = f32[2,256,256]{2,1,0:T(8,128)S(1)} collective-permute-done((f32[2,256,256]{2,1,0:T(8,128)S(1)}, f32[2,256,256]{2,1,0:T(8,128)S(1)}, u32[]{:S(2)}, u32[]{:S(2)}) %collective-permute-start.7) | collective-permute-done | bytes 524320 | tf_op jit(solution)/shard_map/ppermute | solution.py:409
  93.7 19.4 %all_to_all.10.own = f32[8,2,32,512]{3,2,1,0:T(8,128)S(1)} all-to-all(f32[8,2,32,512]{3,2,1,0:T(8,128)S(1)} %shard_map.93), channel_id=1, replica_groups={{0,2,4,6,1,3,5,7},{8,10,12,14,9,11,13,15},{16,18,20,22,17,19,21,23},{24..., dimensions={0} | all-to-all | bytes 2097152 | tf_op jit(solution)/shard_map/all_to_all | solution.py:413
  120.6 6.7 %all-reduce = s32[48]{0:T(128)S(1)} all-reduce(s32[48]{0:T(128)S(1)} %add_dynamic-update-slice_fusion), channel_id=2, replica_groups=mesh['row'=32,'col'=8] {'col'}, use_global_device_ids=true, to_apply=%add | all-reduce | flops 48 | bytes 384
  128.0 20.5 %collective-permute-done.10.lower_even = f32[4,2,32,512]{3,2,1,0:T(8,128)S(1)} collective-permute-done((f32[4,2,32,512]{3,2,1,0:T(8,128)}, f32[4,2,32,512]{3,2,1,0:T(8,128)S(1)}, u32[]{:S(2)}, u32[]{:S(2)}) %collective-permute-start.10) | collective-permute-done | bytes 524320 | tf_op jit(solution)/shard_map/ppermute | solution.py:415
  150.4 7.7 %shard_map.94 = (f32[4096,128]{1,0:T(8,128)}, f32[8,2,32,1024]{3,2,1,0:T(8,128)}) custom-call(s32[2]{0:T(128)} %copy-done.6, s32[8,6]{1,0:T(8,128)} %reshape.13.leds, f32[8,2,32,512]{3,2,1,0:T(8,128)} %copy-done.9, f32[4,2,32,512]{3,2,1,0:T(8,128)} %copy-done.12, f32[4,2,32,512]{3,2,1,0:T(8,128)} %copy-done.13, f32[4,2,32,512]{3,2,1,0:T(8,128)} %copy-done.10, ...), custom_call_target="tpu_custom_call" | custom-call | tf_op jit(solution)/shard_map/pallas_call | solution.py:118
  158.1 12.1 %all-to-all-start.1 = ((f32[256,16,128]{2,1,0:T(8,128)}), f32[256,16,128]{2,1,0:T(8,128)S(1)}, u32[]{:S(2)}, u32[]{:S(2)}) async-start(f32[256,16,128]{2,1,0:T(8,128)} %bitcast.35), calls=%async_computation.1 | async-start | bytes 4194304 | tf_op jit(solution)/shard_map/all_to_all | solution.py:447
  177.8 2.6 %collective-permute-start.16 = (f32[2,32,1024]{2,1,0:T(8,128)S(1)}, f32[2,32,1024]{2,1,0:T(8,128)S(1)}, u32[]{:S(2)}, u32[]{:S(2)}) collective-permute-start(f32[2,32,1024]{2,1,0:T(8,128)S(1)} %get-tuple-element.16), channel_id=1, source_target_pairs={{0,5},{1,6},{2,7},{3,0},{4,1},{5,2},{6,3},{7,4},{8,13},{9,14},{10,... | collective-permute-start | bytes 786440 | tf_op jit(solution)/shard_map/ppermute | solution.py:443
  180.4 3.0 %collective-permute-done.12.refs_1_ = f32[2,32,1024]{2,1,0:T(8,128)S(1)} collective-permute-done((f32[2,32,1024]{2,1,0:T(8,128)S(1)}, f32[2,32,1024]{2,1,0:T(8,128)S(1)}, u32[]{:S(2)}, u32[]{:S(2)}) %collective-permute-start.12) | collective-permute-done | bytes 262176 | tf_op jit(solution)/shard_map/ppermute | solution.py:443
  183.4 3.1 %collective-permute-start.17 = (f32[2,32,1024]{2,1,0:T(8,128)S(1)}, f32[2,32,1024]{2,1,0:T(8,128)S(1)}, u32[]{:S(2)}, u32[]{:S(2)}) collective-permute-start(f32[2,32,1024]{2,1,0:T(8,128)S(1)} %get-tuple-element.15), channel_id=1, source_target_pairs={{0,6},{1,7},{2,0},{3,1},{4,2},{5,3},{6,4},{7,5},{8,14},{9,15},{10,... | collective-permute-start | bytes 786440 | tf_op jit(solution)/shard_map/ppermute | solution.py:443
  186.5 16.1 %collective-permute-done.13.refs_2_ = f32[2,32,1024]{2,1,0:T(8,128)S(1)} collective-permute-done((f32[2,32,1024]{2,1,0:T(8,128)S(1)}, f32[2,32,1024]{2,1,0:T(8,128)S(1)}, u32[]{:S(2)}, u32[]{:S(2)}) %collective-permute-start.13) | collective-permute-done | bytes 262176 | tf_op jit(solution)/shard_map/ppermute | solution.py:443
  202.6 7.3 %collective-permute-done.14.refs_3_ = f32[2,32,1024]{2,1,0:T(8,128)S(1)} collective-permute-done((f32[2,32,1024]{2,1,0:T(8,128)S(1)}, f32[2,32,1024]{2,1,0:T(8,128)S(1)}, u32[]{:S(2)}, u32[]{:S(2)}) %collective-permute-start.14) | collective-permute-done | bytes 262176 | tf_op jit(solution)/shard_map/ppermute | solution.py:443
  209.9 7.1 %collective-permute-done.15.refs_4_ = f32[2,32,1024]{2,1,0:T(8,128)S(1)} collective-permute-done((f32[2,32,1024]{2,1,0:T(8,128)S(1)}, f32[2,32,1024]{2,1,0:T(8,128)S(1)}, u32[]{:S(2)}, u32[]{:S(2)}) %collective-permute-start.15) | collective-permute-done | bytes 262176 | tf_op jit(solution)/shard_map/ppermute | solution.py:443
  221.0 2.6 %all-to-all-done.1 = f32[256,16,128]{2,1,0:T(8,128)S(1)} async-done(((f32[256,16,128]{2,1,0:T(8,128)}), f32[256,16,128]{2,1,0:T(8,128)S(1)}, u32[]{:S(2)}, u32[]{:S(2)}) %all-to-all-start.1) | async-done | bytes 2097184 | tf_op jit(solution)/shard_map/all_to_all | solution.py:447
  223.6 3.7 %shard_map.96 = f32[2,32,8192]{2,1,0:T(8,128)} custom-call(f32[4096,128]{1,0:T(8,128)S(1)} %bitcast.25, f32[2,32,256]{2,1,0:T(8,128)S(1)} %copy-done.5, bf16[4,256,256]{2,1,0:T(8,128)(2,1)S(1)} %copy-done.2), custom_call_target="tpu_custom_call" | custom-call | tf_op jit(solution)/shard_map/pallas_call | solution.py:118
  (68 shorter events, 35.7 us)
Async XLA Ops:
  0.6 10.2 %collective-permute-start = (s32[2]{0:T(128)}, s32[2]{0:T(128)S(1)}, u32[]{:S(2)}, u32[]{:S(2)}) collective-permute-start(s32[2]{0:T(128)} %bitcast.28), channel_id=1, source_target_pairs={{0,16},{1,17},{2,18},{3,19},{4,20},{5,21},{6,22},{7,23},{8,24},{9,... | collective-permute-start | bytes 32 | tf_op jit(solution)/shard_map/ppermute | solution.py:384
  4.5 6.3 %collective-permute-start.1 = (s32[2]{0:T(128)}, s32[2]{0:T(128)S(1)}, u32[]{:S(2)}, u32[]{:S(2)}) collective-permute-start(s32[2]{0:T(128)} %bitcast.29), channel_id=1, source_target_pairs={{24,8},{25,9},{26,10},{27,11},{28,12},{29,13},{30,14},{31,15},{40,... | collective-permute-start | bytes 32 | tf_op jit(solution)/shard_map/ppermute | solution.py:385
  7.0 85.0 %copy-start.6 = (s32[2]{0:T(128)}, s32[2]{0:T(128)S(1)}, u32[]{:S(2)}) copy-start(s32[2]{0:T(128)S(1)} %pad_add_fusion.pos) | copy-start | bytes 28
  12.8 44.7 %collective-permute-start.4 = (f32[2,256,512]{2,1,0:T(8,128)}, f32[2,256,512]{2,1,0:T(8,128)S(1)}, u32[]{:S(2)}, u32[]{:S(2)}) collective-permute-start(f32[2,256,512]{2,1,0:T(8,128)} %get-tuple-element.8), channel_id=1, source_target_pairs={{1,17},{3,19},{5,21},{7,23},{8,24},{9,25},{10,26},{11,27},{12,28},... | collective-permute-start | bytes 3145736 | tf_op jit(solution)/shard_map/ppermute | solution.py:399
  15.6 42.0 %collective-permute-start.5 = (f32[2,256,512]{2,1,0:T(8,128)}, f32[2,256,512]{2,1,0:T(8,128)}, u32[]{:S(2)}, u32[]{:S(2)}) collective-permute-start(f32[2,256,512]{2,1,0:T(8,128)} %get-tuple-element.9), channel_id=1, source_target_pairs={{16,0},{18,2},{20,4},{22,6},{24,8},{25,9},{26,10},{27,11},{28,12},... | collective-permute-start | bytes 3145736 | tf_op jit(solution)/shard_map/ppermute | solution.py:398
  18.4 45.4 %collective-permute-start.3 = (f32[512,256]{1,0:T(8,128)S(1)}, f32[512,256]{1,0:T(8,128)S(1)}, u32[]{:S(2)}, u32[]{:S(2)}) collective-permute-start(f32[512,256]{1,0:T(8,128)S(1)} %dynamic-slice_bitcast_fusion), channel_id=1, source_target_pairs={{0,8},{1,9},{2,10},{3,11},{4,12},{5,13},{6,14},{7,15},{8,0},{9,17}... | collective-permute-start | bytes 1572872 | tf_op jit(solution)/shard_map/ppermute | solution.py:393
  22.6 34.9 %copy-start = (bf16[4,512,512]{2,1,0:T(8,128)(2,1)S(1)}, bf16[4,512,512]{2,1,0:T(8,128)(2,1)}, u32[]{:S(2)}) copy-start(bf16[4,512,512]{2,1,0:T(8,128)(2,1)} %constant.35.clone.table) | copy-start | bytes 6291460
  23.8 54.0 %collective-permute-start.2 = (f32[512,256]{1,0:T(8,128)S(1)}, f32[512,256]{1,0:T(8,128)S(1)}, u32[]{:S(2)}, u32[]{:S(2)}) collective-permute-start(f32[512,256]{1,0:T(8,128)S(1)} %slice.44), channel_id=1, source_target_pairs={{1,17},{3,19},{5,21},{7,23},{17,33},{19,35},{21,37},{23,39},{33,49... | collective-permute-start | bytes 1572872 | tf_op jit(solution)/shard_map/ppermute | solution.py:394
  60.2 17.6 %collective-permute-start.6 = (f32[2,256,256]{2,1,0:T(8,128)S(1)}, f32[2,256,256]{2,1,0:T(8,128)S(1)}, u32[]{:S(2)}, u32[]{:S(2)}) collective-permute-start(f32[2,256,256]{2,1,0:T(8,128)S(1)} %shard_map.90), channel_id=1, source_target_pairs={{0,8},{1,249},{2,10},{3,251},{4,12},{5,253},{6,14},{7,255},{8,0},{... | collective-permute-start | bytes 1572872 | tf_op jit(solution)/shard_map/ppermute | solution.py:404
  80.6 11.4 %collective-permute-start.7 = (f32[2,256,256]{2,1,0:T(8,128)S(1)}, f32[2,256,256]{2,1,0:T(8,128)S(1)}, u32[]{:S(2)}, u32[]{:S(2)}) collective-permute-start(f32[2,256,256]{2,1,0:T(8,128)S(1)} %get-tuple-element.11), channel_id=1, source_target_pairs={{0,8},{1,249},{2,10},{3,251},{4,12},{5,253},{6,14},{7,255},{8,0},{... | collective-permute-start | bytes 1572872 | tf_op jit(solution)/shard_map/ppermute | solution.py:409
  113.1 35.4 %copy-start.9 = (f32[8,2,32,512]{3,2,1,0:T(8,128)}, f32[8,2,32,512]{3,2,1,0:T(8,128)S(1)}, u32[]{:S(2)}) copy-start(f32[8,2,32,512]{3,2,1,0:T(8,128)S(1)} %all_to_all.10.own) | copy-start | bytes 3145732
  114.3 34.2 %collective-permute-start.10 = (f32[4,2,32,512]{3,2,1,0:T(8,128)}, f32[4,2,32,512]{3,2,1,0:T(8,128)S(1)}, u32[]{:S(2)}, u32[]{:S(2)}) collective-permute-start(f32[4,2,32,512]{3,2,1,0:T(8,128)} %get-tuple-element.22), channel_id=1, source_target_pairs={{0,16},{8,24},{16,32},{24,40},{32,48},{40,56},{48,64},{56,72},{64,... | collective-permute-start | bytes 1572872 | tf_op jit(solution)/shard_map/ppermute | solution.py:415
  115.6 32.9 %collective-permute-start.11 = (f32[4,2,32,512]{3,2,1,0:T(8,128)}, f32[4,2,32,512]{3,2,1,0:T(8,128)S(1)}, u32[]{:S(2)}, u32[]{:S(2)}) collective-permute-start(f32[4,2,32,512]{3,2,1,0:T(8,128)} %get-tuple-element.23), channel_id=1, source_target_pairs={{16,0},{24,8},{32,16},{40,24},{48,32},{56,40},{64,48},{72,56},{80,... | collective-permute-start | bytes 1572872 | tf_op jit(solution)/shard_map/ppermute | solution.py:416
  117.5 31.0 %collective-permute-start.8 = (f32[4,2,32,512]{3,2,1,0:T(8,128)}, f32[4,2,32,512]{3,2,1,0:T(8,128)S(1)}, u32[]{:S(2)}, u32[]{:S(2)}) collective-permute-start(f32[4,2,32,512]{3,2,1,0:T(8,128)} %get-tuple-element.23), channel_id=1, source_target_pairs={{8,24},{24,40},{40,56},{56,72},{72,88},{88,104},{104,120},{120,136... | collective-permute-start | bytes 1572872 | tf_op jit(solution)/shard_map/ppermute | solution.py:417
  118.2 30.3 %collective-permute-start.9 = (f32[4,2,32,512]{3,2,1,0:T(8,128)}, f32[4,2,32,512]{3,2,1,0:T(8,128)S(1)}, u32[]{:S(2)}, u32[]{:S(2)}) collective-permute-start(f32[4,2,32,512]{3,2,1,0:T(8,128)} %get-tuple-element.22), channel_id=1, source_target_pairs={{24,8},{40,24},{56,40},{72,56},{88,72},{104,88},{120,104},{136,120... | collective-permute-start | bytes 1572872 | tf_op jit(solution)/shard_map/ppermute | solution.py:418
  158.1 65.5 %all-to-all-start.1 = ((f32[256,16,128]{2,1,0:T(8,128)}), f32[256,16,128]{2,1,0:T(8,128)S(1)}, u32[]{:S(2)}, u32[]{:S(2)}) async-start(f32[256,16,128]{2,1,0:T(8,128)} %bitcast.35), calls=%async_computation.1 | async-start | bytes 4194304 | tf_op jit(solution)/shard_map/all_to_all | solution.py:447
  170.2 48.8 %copy-start.7 = (s32[2]{0:T(128)S(1)}, s32[2]{0:T(128)}, u32[]{:S(2)}) copy-start(s32[2]{0:T(128)} %copy-done.6) | copy-start | bytes 28
  171.9 11.5 %collective-permute-start.12 = (f32[2,32,1024]{2,1,0:T(8,128)S(1)}, f32[2,32,1024]{2,1,0:T(8,128)S(1)}, u32[]{:S(2)}, u32[]{:S(2)}) collective-permute-start(f32[2,32,1024]{2,1,0:T(8,128)S(1)} %get-tuple-element.20), channel_id=1, source_target_pairs={{0,1},{1,2},{2,3},{3,4},{4,5},{5,6},{6,7},{7,0},{8,9},{9,10},{10,1... | collective-permute-start | bytes 786440 | tf_op jit(solution)/shard_map/ppermute | solution.py:443
  173.5 29.1 %collective-permute-start.13 = (f32[2,32,1024]{2,1,0:T(8,128)S(1)}, f32[2,32,1024]{2,1,0:T(8,128)S(1)}, u32[]{:S(2)}, u32[]{:S(2)}) collective-permute-start(f32[2,32,1024]{2,1,0:T(8,128)S(1)} %get-tuple-element.19), channel_id=1, source_target_pairs={{0,2},{1,3},{2,4},{3,5},{4,6},{5,7},{6,0},{7,1},{8,10},{9,11},{10,... | collective-permute-start | bytes 786440 | tf_op jit(solution)/shard_map/ppermute | solution.py:443
  174.7 35.2 %collective-permute-start.14 = (f32[2,32,1024]{2,1,0:T(8,128)S(1)}, f32[2,32,1024]{2,1,0:T(8,128)S(1)}, u32[]{:S(2)}, u32[]{:S(2)}) collective-permute-start(f32[2,32,1024]{2,1,0:T(8,128)S(1)} %get-tuple-element.18), channel_id=1, source_target_pairs={{0,3},{1,4},{2,5},{3,6},{4,7},{5,0},{6,1},{7,2},{8,11},{9,12},{10,... | collective-permute-start | bytes 786440 | tf_op jit(solution)/shard_map/ppermute | solution.py:443
  176.4 40.6 %collective-permute-start.15 = (f32[2,32,1024]{2,1,0:T(8,128)S(1)}, f32[2,32,1024]{2,1,0:T(8,128)S(1)}, u32[]{:S(2)}, u32[]{:S(2)}) collective-permute-start(f32[2,32,1024]{2,1,0:T(8,128)S(1)} %get-tuple-element.17), channel_id=1, source_target_pairs={{0,4},{1,5},{2,6},{3,7},{4,0},{5,1},{6,2},{7,3},{8,12},{9,13},{10,... | collective-permute-start | bytes 786440 | tf_op jit(solution)/shard_map/ppermute | solution.py:443
  177.8 40.0 %collective-permute-start.16 = (f32[2,32,1024]{2,1,0:T(8,128)S(1)}, f32[2,32,1024]{2,1,0:T(8,128)S(1)}, u32[]{:S(2)}, u32[]{:S(2)}) collective-permute-start(f32[2,32,1024]{2,1,0:T(8,128)S(1)} %get-tuple-element.16), channel_id=1, source_target_pairs={{0,5},{1,6},{2,7},{3,0},{4,1},{5,2},{6,3},{7,4},{8,13},{9,14},{10,... | collective-permute-start | bytes 786440 | tf_op jit(solution)/shard_map/ppermute | solution.py:443
  183.4 34.4 %collective-permute-start.17 = (f32[2,32,1024]{2,1,0:T(8,128)S(1)}, f32[2,32,1024]{2,1,0:T(8,128)S(1)}, u32[]{:S(2)}, u32[]{:S(2)}) collective-permute-start(f32[2,32,1024]{2,1,0:T(8,128)S(1)} %get-tuple-element.15), channel_id=1, source_target_pairs={{0,6},{1,7},{2,0},{3,1},{4,2},{5,3},{6,4},{7,5},{8,14},{9,15},{10,... | collective-permute-start | bytes 786440 | tf_op jit(solution)/shard_map/ppermute | solution.py:443
  202.6 16.3 %collective-permute-start.18 = (f32[2,32,1024]{2,1,0:T(8,128)S(1)}, f32[2,32,1024]{2,1,0:T(8,128)S(1)}, u32[]{:S(2)}, u32[]{:S(2)}) collective-permute-start(f32[2,32,1024]{2,1,0:T(8,128)S(1)} %get-tuple-element.14), channel_id=1, source_target_pairs={{0,7},{1,0},{2,1},{3,2},{4,3},{5,4},{6,5},{7,6},{8,15},{9,8},{10,9... | collective-permute-start | bytes 786440 | tf_op jit(solution)/shard_map/ppermute | solution.py:443
  (11 other events, 73.0 us)

commit v4 on v3

--- a/solution.py
+++ b/solution.py
@@ -22,6 +22,7 @@
 F32 = jnp.float32
 BF16 = jnp.bfloat16
 VMEM_BYTES = 32 * 1024 * 1024
+SLOW = 10**11
 ROWS_VMEM_BYTES = 59 * 1024 * 1024
 
 
@@ -152,12 +153,17 @@
         to_upper[part] = jnp.where(cols >= up[1], left, right)
 
 
-def pupil_kernel(pos, local, lower, upper, pupil, rolled):
+def pupil_kernel(pos, local, lower, upper, pupil, amplitude, near_amp, rolled, measured, far_half):
     (at_row, at_col), _, _ = corners(pos, local, lower, upper)
     shift = lax.rem(at_col, M)
     down = lax.rem(at_row + 2 * N, M)
     for part in range(2):
         rolled[part] = pltpu.roll(pltpu.roll(pupil[part], shift, 1), down, 0)[:ROWS]
+    low = lax.rem(pos[0], 2) == 0
+    moved = jnp.logical_and(low, lax.rem(pos[1], 2) == 1)
+    own = jnp.where(low, amplitude[:, :ROWS], amplitude[:, ROWS:])
+    measured[...] = jnp.where(moved, 0.0, own) + near_amp[...]
+    far_half[...] = amplitude[:, :ROWS]
 
 
 def stage_kernel(spec, staged):
@@ -202,17 +208,14 @@
     wave[0], wave[1] = table_times_complex(cos, sin, 1, split(re), split(im))
 
 
-def fit_kernel(pos, far_amp, near_amp, amplitude, wave, other, table, fit, send):
+def fit_kernel(pos, far_amp, measured, wave, other, table, fit, send):
     parity = lax.rem(pos[0], 2)
-    moved = jnp.logical_and(parity == 0, lax.rem(pos[1], 2) == 1)
     cos, sin = half_cols(table, 1 - parity)
     wave_re, wave_im = table_times_complex(cos, sin, 1, split(other[0]), split(other[1]))
     wave_re += wave[0]
     wave_im += wave[1]
-    measured = jnp.where(parity == 0, amplitude[:, :ROWS], amplitude[:, ROWS:])
-    measured = jnp.where(moved, far_amp[...], measured) + near_amp[...]
     modulus = jnp.sqrt(wave_re * wave_re + wave_im * wave_im + GAMMA)
-    keeping = 1.0 - measured / modulus
+    keeping = 1.0 - (measured[...] + far_amp[...]) / modulus
     fit[0] = wave_re * keeping
     fit[1] = wave_im * keeping
     cos, sin = half_rows(table, 1 - parity)
@@ -391,20 +394,22 @@
     quarter = (2, ROWS, ROWS)
     near_half = lax.dynamic_slice(measured, (jnp.int32(0), (1 - row % 2) * ROWS), (M, ROWS))
     near_amp = lax.ppermute(near_half, BOTH, NEAR)
-    far_amp = lax.ppermute(measured[:, :ROWS], BOTH, FAR)
 
     (staged,) = call(stage_kernel, [(2, ROWS, COLS)], (), spectrum, limit=4 * 1024 * 1024)()
-    to_lower, to_upper = call(pack_kernel, [(2,) + half, (2,) + half], smem, *where, staged, limit=4 * 1024 * 1024)()
+    to_lower, to_upper = call(pack_kernel, [(2,) + half, (2,) + half], smem, *where, staged, cost=SLOW, limit=4 * 1024 * 1024)()
     from_upper = lax.ppermute(to_lower, BOTH, DOWN)
     from_lower = lax.ppermute(to_upper, BOTH, UP)
-    (rolled,) = call(pupil_kernel, [(2,) + half], smem, *where, pupil)()
+    rolled, measured, far_half = call(
+        pupil_kernel, [(2,) + half, (M, ROWS), (M, ROWS)], smem, *where, pupil, measured, near_amp, cost=SLOW
+    )()
+    far_amp = lax.ppermute(far_half, BOTH, FAR)
 
     sources = (*where, staged, from_lower, from_upper, rolled, window_table)
     (send,) = call(send_kernel, [quarter], smem, *sources)()
     other = lax.ppermute(send, BOTH, PARTNERS)
     (wave,) = call(keep_kernel, [(2, M, ROWS)], smem, *sources)()
     fit, send = call(
-        fit_kernel, [(2, M, ROWS), quarter], (0,), pos, far_amp, near_amp, measured, wave, other, window_table
+        fit_kernel, [(2, M, ROWS), quarter], (0,), pos, far_amp, measured, wave, other, window_table
     )()
     other = lax.ppermute(send, BOTH, PARTNERS)
     (part,) = call(stay_kernel, [(2,) + half], (0,), pos, fit, window_table)()

time: 228 us -> 226 us (level)
  starting transfers between devices: 46.5 us -> 64.4 us
  waiting for transfers between devices: 112 us -> 95.9 us
    ppermute x1, starting transfers between devices: 4.89 us -> 25.9 us  [on_device(): far_amp = lax.ppermute(far_half, BOTH, FAR)]
    ppermute x1, waiting for transfers between devices: 26.8 us -> 12.4 us  [on_device(): from_lower = lax.ppermute(to_upper, BOTH, UP)]
    ppermute x1, waiting for transfers between devices: 14 us -> 4.86 us  [on_device(): far_amp = lax.ppermute(far_half, BOTH, FAR)]
    ppermute x1, waiting for transfers between devices: 0.01 us -> 5.54 us  [on_device(): lax.ppermute(odd, 'row', [(row, row - 2) for row in range(2, N_ROW)] + [(...]
    ppermute x2, waiting for transfers between devices: 8.92 us -> 13.5 us  [on_device(): other = lax.ppermute(send, BOTH, PARTNERS)]
    all_to_all x1, starting transfers between devices: 12.1 us -> 8.65 us  [on_device(): lax.all_to_all(outgoing.reshape(PARTS, 16, 128), ('row', 'col'), split_ax...]
    ppermute x1, waiting for transfers between devices: 3.81 us -> 0.37 us  [on_device(): lower = lax.ppermute(local, BOTH, FROM_LOWER)]
    ppermute x1, waiting for transfers between devices: 0.01 us -> 3.14 us  [on_device(): near_amp = lax.ppermute(near_half, BOTH, NEAR)]
  transfers between devices with their start and end apart: 20 -> 20, of which waited for: 12 -> 15; matrix products, arithmetic and copies ran while one was open for 3% -> 2% of each run, Pallas kernels for 6% -> 6%
where the time goes in v4:
time: 226 us; the launch traced here: 225 us
  waiting for transfers between devices  95.9 us (42%)
  starting transfers between devices  64.4 us (28%)
  Pallas kernels  28.3 us (13%)
  blocking collectives  26.1 us (12%)
  local copies, waits for them, and re-layouts  8.63 us (4%)
    ppermute x7, waiting for transfers between devices, on_device(): lax.ppermute(shares[step], 'col', [(at, (at + step) % N_COL) for at in ra...  35.4 us
    pallas_call x11, Pallas kernels, call(): pl.pallas_call(kernel, out_shape=tuple((jax.ShapeDtypeStruct(shape, F32)...  28.3 us
    ppermute x1, starting transfers between devices, on_device(): far_amp = lax.ppermute(far_half, BOTH, FAR)  25.9 us
    all_to_all x1, blocking collectives, on_device(): lax.all_to_all(grad, 'col', split_axis=0, concat_axis=0, tiled=True, axis...  19.4 us
    ppermute x1, waiting for transfers between devices, on_device(): lax.ppermute(even, 'row', [(row, row + 2) for row in range(N_ROW - 2)])  18 us
    ppermute x2, waiting for transfers between devices, on_device(): other = lax.ppermute(send, BOTH, PARTNERS)  13.5 us
    ppermute x1, waiting for transfers between devices, on_device(): from_lower = lax.ppermute(to_upper, BOTH, UP)  12.4 us
    ppermute x7, starting transfers between devices, on_device(): lax.ppermute(shares[step], 'col', [(at, (at + step) % N_COL) for at in ra...  11.6 us
  transfers between devices with their start and end apart: 20, of which 15 were waited for; matrix products, arithmetic and copies ran while one was open for 2% of the time, Pallas kernels for 6%

profile of v4, /device:TPU:1, one launch (start us, length us, event | category | flops | bytes accessed | tf_op | source)
XLA Modules:
  0.0 225.3 jit_solution(10176814850271026237)
XLA Ops:
  0.6 3.9 %collective-permute-start = (s32[2]{0:T(128)}, s32[2]{0:T(128)S(1)}, u32[]{:S(2)}, u32[]{:S(2)}) collective-permute-start(s32[2]{0:T(128)} %bitcast.27), channel_id=1, source_target_pairs={{0,16},{1,17},{2,18},{3,19},{4,20},{5,21},{6,22},{7,23},{8,24},{9,... | collective-permute-start | bytes 32 | tf_op jit(solution)/shard_map/ppermute | solution.py:387
  11.6 5.8 %collective-permute-start.4 = (f32[2,256,512]{2,1,0:T(8,128)S(1)}, f32[2,256,512]{2,1,0:T(8,128)S(1)}, u32[]{:S(2)}, u32[]{:S(2)}) collective-permute-start(f32[2,256,512]{2,1,0:T(8,128)S(1)} %get-tuple-element.13), channel_id=1, source_target_pairs={{1,17},{3,19},{5,21},{7,23},{8,24},{9,25},{10,26},{11,27},{12,28},... | collective-permute-start | bytes 3145736 | tf_op jit(solution)/shard_map/ppermute | solution.py:401
  18.2 3.1 %collective-permute-done.2.near_amp = f32[512,256]{1,0:T(8,128)S(1)} collective-permute-done((f32[512,256]{1,0:T(8,128)S(1)}, f32[512,256]{1,0:T(8,128)S(1)}, u32[]{:S(2)}, u32[]{:S(2)}) %collective-permute-start.2) | collective-permute-done | bytes 524320 | tf_op jit(solution)/shard_map/ppermute | solution.py:396
  23.5 25.9 %collective-permute-start.3 = (f32[512,256]{1,0:T(8,128)S(1)}, f32[512,256]{1,0:T(8,128)S(1)}, u32[]{:S(2)}, u32[]{:S(2)}) collective-permute-start(f32[512,256]{1,0:T(8,128)S(1)} %get-tuple-element.11), channel_id=1, source_target_pairs={{1,17},{3,19},{5,21},{7,23},{17,33},{19,35},{21,37},{23,39},{33,49... | collective-permute-start | bytes 1572872 | tf_op jit(solution)/shard_map/ppermute | solution.py:405
  49.4 12.4 %collective-permute-done.4.from_lower = f32[2,256,512]{2,1,0:T(8,128)S(1)} collective-permute-done((f32[2,256,512]{2,1,0:T(8,128)S(1)}, f32[2,256,512]{2,1,0:T(8,128)S(1)}, u32[]{:S(2)}, u32[]{:S(2)}) %collective-permute-start.4) | collective-permute-done | bytes 1048608 | tf_op jit(solution)/shard_map/ppermute | solution.py:401
  64.0 3.0 %shard_map.89.wave = f32[2,512,256]{2,1,0:T(8,128)S(1)} custom-call(s32[2]{0:T(128)S(1)} %pad_add_fusion.pos, s32[2]{0:T(128)S(1)} %bitcast.32, s32[2]{0:T(128)S(1)} %collective-permute-done.lower, s32[2]{0:T(128)S(1)} %collective-permute-done.1.upper, f32[2,256,1024]{2,1,0:T(8,128)S(1)} %shard_map.87.spec, ...), custom_call_target="tpu_custom_call" | custom-call | tf_op jit(solution)/shard_map/pallas_call | solution.py:119
  66.9 4.9 %collective-permute-done.3.far_amp = f32[512,256]{1,0:T(8,128)S(1)} collective-permute-done((f32[512,256]{1,0:T(8,128)S(1)}, f32[512,256]{1,0:T(8,128)S(1)}, u32[]{:S(2)}, u32[]{:S(2)}) %collective-permute-start.3) | collective-permute-done | bytes 524320 | tf_op jit(solution)/shard_map/ppermute | solution.py:405
  71.8 4.6 %collective-permute-done.6.other = f32[2,256,256]{2,1,0:T(8,128)S(1)} collective-permute-done((f32[2,256,256]{2,1,0:T(8,128)S(1)}, f32[2,256,256]{2,1,0:T(8,128)S(1)}, u32[]{:S(2)}, u32[]{:S(2)}) %collective-permute-start.6) | collective-permute-done | bytes 524320 | tf_op jit(solution)/shard_map/ppermute | solution.py:409
  76.4 2.8 %shard_map.91 = (f32[2,512,256]{2,1,0:T(8,128)S(1)}, f32[2,256,256]{2,1,0:T(8,128)S(1)}) custom-call(s32[2]{0:T(128)S(1)} %pad_add_fusion.pos, f32[512,256]{1,0:T(8,128)S(1)} %collective-permute-done.3.far_amp, f32[512,256]{1,0:T(8,128)S(1)} %get-tuple-element.12.measured, f32[2,512,256]{2,1,0:T(8,128)S(1)} %shard_map.89.wave, ...), custom_call_target="tpu_custom_call" | custom-call | tf_op jit(solution)/shard_map/pallas_call | solution.py:119
  81.7 8.9 %collective-permute-done.7.other = f32[2,256,256]{2,1,0:T(8,128)S(1)} collective-permute-done((f32[2,256,256]{2,1,0:T(8,128)S(1)}, f32[2,256,256]{2,1,0:T(8,128)S(1)}, u32[]{:S(2)}, u32[]{:S(2)}) %collective-permute-start.7) | collective-permute-done | bytes 524320 | tf_op jit(solution)/shard_map/ppermute | solution.py:414
  92.3 19.4 %all_to_all.10.own = f32[8,2,32,512]{3,2,1,0:T(8,128)S(1)} all-to-all(f32[8,2,32,512]{3,2,1,0:T(8,128)S(1)} %shard_map.93), channel_id=1, replica_groups={{0,2,4,6,1,3,5,7},{8,10,12,14,9,11,13,15},{16,18,20,22,17,19,21,23},{24..., dimensions={0} | all-to-all | bytes 2097152 | tf_op jit(solution)/shard_map/all_to_all | solution.py:418
  119.0 6.7 %all-reduce = s32[48]{0:T(128)S(1)} all-reduce(s32[48]{0:T(128)S(1)} %add_dynamic-update-slice_fusion), channel_id=2, replica_groups=mesh['row'=32,'col'=8] {'col'}, use_global_device_ids=true, to_apply=%add | all-reduce | flops 48 | bytes 384
  126.3 18.0 %collective-permute-done.10.lower_even = f32[4,2,32,512]{3,2,1,0:T(8,128)S(1)} collective-permute-done((f32[4,2,32,512]{3,2,1,0:T(8,128)}, f32[4,2,32,512]{3,2,1,0:T(8,128)S(1)}, u32[]{:S(2)}, u32[]{:S(2)}) %collective-permute-start.10) | collective-permute-done | bytes 524320 | tf_op jit(solution)/shard_map/ppermute | solution.py:420
  144.3 5.5 %collective-permute-done.11.upper_odd = f32[4,2,32,512]{3,2,1,0:T(8,128)S(1)} collective-permute-done((f32[4,2,32,512]{3,2,1,0:T(8,128)}, f32[4,2,32,512]{3,2,1,0:T(8,128)S(1)}, u32[]{:S(2)}, u32[]{:S(2)}) %collective-permute-start.11) | collective-permute-done | bytes 524320 | tf_op jit(solution)/shard_map/ppermute | solution.py:421
  151.6 7.7 %shard_map.94 = (f32[4096,128]{1,0:T(8,128)}, f32[8,2,32,1024]{3,2,1,0:T(8,128)}) custom-call(s32[2]{0:T(128)} %copy-done.5, s32[8,6]{1,0:T(8,128)} %reshape.13.leds, f32[8,2,32,512]{3,2,1,0:T(8,128)} %copy-done.9, f32[4,2,32,512]{3,2,1,0:T(8,128)} %copy-done.12, f32[4,2,32,512]{3,2,1,0:T(8,128)} %copy-done.13, f32[4,2,32,512]{3,2,1,0:T(8,128)} %copy-done.10, ...), custom_call_target="tpu_custom_call" | custom-call | tf_op jit(solution)/shard_map/pallas_call | solution.py:119
  159.3 8.7 %all-to-all-start.1 = ((f32[256,16,128]{2,1,0:T(8,128)}), f32[256,16,128]{2,1,0:T(8,128)S(1)}, u32[]{:S(2)}, u32[]{:S(2)}) async-start(f32[256,16,128]{2,1,0:T(8,128)} %bitcast.34), calls=%async_computation.1 | async-start | bytes 4194304 | tf_op jit(solution)/shard_map/all_to_all | solution.py:452
  175.6 2.6 %collective-permute-start.16 = (f32[2,32,1024]{2,1,0:T(8,128)S(1)}, f32[2,32,1024]{2,1,0:T(8,128)S(1)}, u32[]{:S(2)}, u32[]{:S(2)}) collective-permute-start(f32[2,32,1024]{2,1,0:T(8,128)S(1)} %get-tuple-element.22), channel_id=1, source_target_pairs={{0,5},{1,6},{2,7},{3,0},{4,1},{5,2},{6,3},{7,4},{8,13},{9,14},{10,... | collective-permute-start | bytes 786440 | tf_op jit(solution)/shard_map/ppermute | solution.py:448
  178.2 3.0 %collective-permute-done.12.refs_1_ = f32[2,32,1024]{2,1,0:T(8,128)S(1)} collective-permute-done((f32[2,32,1024]{2,1,0:T(8,128)S(1)}, f32[2,32,1024]{2,1,0:T(8,128)S(1)}, u32[]{:S(2)}, u32[]{:S(2)}) %collective-permute-start.12) | collective-permute-done | bytes 262176 | tf_op jit(solution)/shard_map/ppermute | solution.py:448
  181.1 3.1 %collective-permute-start.17 = (f32[2,32,1024]{2,1,0:T(8,128)S(1)}, f32[2,32,1024]{2,1,0:T(8,128)S(1)}, u32[]{:S(2)}, u32[]{:S(2)}) collective-permute-start(f32[2,32,1024]{2,1,0:T(8,128)S(1)} %get-tuple-element.21), channel_id=1, source_target_pairs={{0,6},{1,7},{2,0},{3,1},{4,2},{5,3},{6,4},{7,5},{8,14},{9,15},{10,... | collective-permute-start | bytes 786440 | tf_op jit(solution)/shard_map/ppermute | solution.py:448
  184.3 16.1 %collective-permute-done.13.refs_2_ = f32[2,32,1024]{2,1,0:T(8,128)S(1)} collective-permute-done((f32[2,32,1024]{2,1,0:T(8,128)S(1)}, f32[2,32,1024]{2,1,0:T(8,128)S(1)}, u32[]{:S(2)}, u32[]{:S(2)}) %collective-permute-start.13) | collective-permute-done | bytes 262176 | tf_op jit(solution)/shard_map/ppermute | solution.py:448
  200.4 7.3 %collective-permute-done.14.refs_3_ = f32[2,32,1024]{2,1,0:T(8,128)S(1)} collective-permute-done((f32[2,32,1024]{2,1,0:T(8,128)S(1)}, f32[2,32,1024]{2,1,0:T(8,128)S(1)}, u32[]{:S(2)}, u32[]{:S(2)}) %collective-permute-start.14) | collective-permute-done | bytes 262176 | tf_op jit(solution)/shard_map/ppermute | solution.py:448
  207.7 7.1 %collective-permute-done.15.refs_4_ = f32[2,32,1024]{2,1,0:T(8,128)S(1)} collective-permute-done((f32[2,32,1024]{2,1,0:T(8,128)S(1)}, f32[2,32,1024]{2,1,0:T(8,128)S(1)}, u32[]{:S(2)}, u32[]{:S(2)}) %collective-permute-start.15) | collective-permute-done | bytes 262176 | tf_op jit(solution)/shard_map/ppermute | solution.py:448
  218.7 2.6 %all-to-all-done.1 = f32[256,16,128]{2,1,0:T(8,128)S(1)} async-done(((f32[256,16,128]{2,1,0:T(8,128)}), f32[256,16,128]{2,1,0:T(8,128)S(1)}, u32[]{:S(2)}, u32[]{:S(2)}) %all-to-all-start.1) | async-done | bytes 2097184 | tf_op jit(solution)/shard_map/all_to_all | solution.py:452
  221.4 3.7 %shard_map.96 = f32[2,32,8192]{2,1,0:T(8,128)} custom-call(f32[4096,128]{1,0:T(8,128)S(1)} %bitcast.25, f32[2,32,256]{2,1,0:T(8,128)S(1)} %copy-done.3, bf16[4,256,256]{2,1,0:T(8,128)(2,1)S(1)} %copy-done.1), custom_call_target="tpu_custom_call" | custom-call | tf_op jit(solution)/shard_map/pallas_call | solution.py:119
  (67 shorter events, 36.8 us)
Async XLA Ops:
  0.6 10.2 %collective-permute-start = (s32[2]{0:T(128)}, s32[2]{0:T(128)S(1)}, u32[]{:S(2)}, u32[]{:S(2)}) collective-permute-start(s32[2]{0:T(128)} %bitcast.27), channel_id=1, source_target_pairs={{0,16},{1,17},{2,18},{3,19},{4,20},{5,21},{6,22},{7,23},{8,24},{9,... | collective-permute-start | bytes 32 | tf_op jit(solution)/shard_map/ppermute | solution.py:387
  4.5 6.3 %collective-permute-start.1 = (s32[2]{0:T(128)}, s32[2]{0:T(128)S(1)}, u32[]{:S(2)}, u32[]{:S(2)}) collective-permute-start(s32[2]{0:T(128)} %bitcast.28), channel_id=1, source_target_pairs={{24,8},{25,9},{26,10},{27,11},{28,12},{29,13},{30,14},{31,15},{40,... | collective-permute-start | bytes 32 | tf_op jit(solution)/shard_map/ppermute | solution.py:388
  6.3 15.0 %collective-permute-start.2 = (f32[512,256]{1,0:T(8,128)S(1)}, f32[512,256]{1,0:T(8,128)S(1)}, u32[]{:S(2)}, u32[]{:S(2)}) collective-permute-start(f32[512,256]{1,0:T(8,128)S(1)} %dynamic-slice_bitcast_fusion), channel_id=1, source_target_pairs={{0,8},{1,9},{2,10},{3,11},{4,12},{5,13},{6,14},{7,15},{8,0},{9,17}... | collective-permute-start | bytes 1572872 | tf_op jit(solution)/shard_map/ppermute | solution.py:396
  10.4 80.1 %copy-start.5 = (s32[2]{0:T(128)}, s32[2]{0:T(128)S(1)}, u32[]{:S(2)}) copy-start(s32[2]{0:T(128)S(1)} %pad_add_fusion.pos) | copy-start | bytes 28
  11.6 50.2 %collective-permute-start.4 = (f32[2,256,512]{2,1,0:T(8,128)S(1)}, f32[2,256,512]{2,1,0:T(8,128)S(1)}, u32[]{:S(2)}, u32[]{:S(2)}) collective-permute-start(f32[2,256,512]{2,1,0:T(8,128)S(1)} %get-tuple-element.13), channel_id=1, source_target_pairs={{1,17},{3,19},{5,21},{7,23},{8,24},{9,25},{10,26},{11,27},{12,28},... | collective-permute-start | bytes 3145736 | tf_op jit(solution)/shard_map/ppermute | solution.py:401
  17.4 44.4 %collective-permute-start.5 = (f32[2,256,512]{2,1,0:T(8,128)S(1)}, f32[2,256,512]{2,1,0:T(8,128)S(1)}, u32[]{:S(2)}, u32[]{:S(2)}) collective-permute-start(f32[2,256,512]{2,1,0:T(8,128)S(1)} %get-tuple-element.14), channel_id=1, source_target_pairs={{16,0},{18,2},{20,4},{22,6},{24,8},{25,9},{26,10},{27,11},{28,12},... | collective-permute-start | bytes 3145736 | tf_op jit(solution)/shard_map/ppermute | solution.py:400
  21.3 40.5 %copy-start = (bf16[4,512,512]{2,1,0:T(8,128)(2,1)S(1)}, bf16[4,512,512]{2,1,0:T(8,128)(2,1)}, u32[]{:S(2)}) copy-start(bf16[4,512,512]{2,1,0:T(8,128)(2,1)} %constant.35.clone.table) | copy-start | bytes 6291460
  23.5 48.3 %collective-permute-start.3 = (f32[512,256]{1,0:T(8,128)S(1)}, f32[512,256]{1,0:T(8,128)S(1)}, u32[]{:S(2)}, u32[]{:S(2)}) collective-permute-start(f32[512,256]{1,0:T(8,128)S(1)} %get-tuple-element.11), channel_id=1, source_target_pairs={{1,17},{3,19},{5,21},{7,23},{17,33},{19,35},{21,37},{23,39},{33,49... | collective-permute-start | bytes 1572872 | tf_op jit(solution)/shard_map/ppermute | solution.py:405
  63.9 12.5 %collective-permute-start.6 = (f32[2,256,256]{2,1,0:T(8,128)S(1)}, f32[2,256,256]{2,1,0:T(8,128)S(1)}, u32[]{:S(2)}, u32[]{:S(2)}) collective-permute-start(f32[2,256,256]{2,1,0:T(8,128)S(1)} %shard_map.90), channel_id=1, source_target_pairs={{0,8},{1,249},{2,10},{3,251},{4,12},{5,253},{6,14},{7,255},{8,0},{... | collective-permute-start | bytes 1572872 | tf_op jit(solution)/shard_map/ppermute | solution.py:409
  79.1 11.4 %collective-permute-start.7 = (f32[2,256,256]{2,1,0:T(8,128)S(1)}, f32[2,256,256]{2,1,0:T(8,128)S(1)}, u32[]{:S(2)}, u32[]{:S(2)}) collective-permute-start(f32[2,256,256]{2,1,0:T(8,128)S(1)} %get-tuple-element.17), channel_id=1, source_target_pairs={{0,8},{1,249},{2,10},{3,251},{4,12},{5,253},{6,14},{7,255},{8,0},{... | collective-permute-start | bytes 1572872 | tf_op jit(solution)/shard_map/ppermute | solution.py:414
  111.7 38.2 %copy-start.9 = (f32[8,2,32,512]{3,2,1,0:T(8,128)}, f32[8,2,32,512]{3,2,1,0:T(8,128)S(1)}, u32[]{:S(2)}) copy-start(f32[8,2,32,512]{3,2,1,0:T(8,128)S(1)} %all_to_all.10.own) | copy-start | bytes 3145732
  112.9 31.5 %collective-permute-start.10 = (f32[4,2,32,512]{3,2,1,0:T(8,128)}, f32[4,2,32,512]{3,2,1,0:T(8,128)S(1)}, u32[]{:S(2)}, u32[]{:S(2)}) collective-permute-start(f32[4,2,32,512]{3,2,1,0:T(8,128)} %get-tuple-element.28), channel_id=1, source_target_pairs={{0,16},{8,24},{16,32},{24,40},{32,48},{40,56},{48,64},{56,72},{64,... | collective-permute-start | bytes 1572872 | tf_op jit(solution)/shard_map/ppermute | solution.py:420
  114.2 35.7 %collective-permute-start.11 = (f32[4,2,32,512]{3,2,1,0:T(8,128)}, f32[4,2,32,512]{3,2,1,0:T(8,128)S(1)}, u32[]{:S(2)}, u32[]{:S(2)}) collective-permute-start(f32[4,2,32,512]{3,2,1,0:T(8,128)} %get-tuple-element.29), channel_id=1, source_target_pairs={{16,0},{24,8},{32,16},{40,24},{48,32},{56,40},{64,48},{72,56},{80,... | collective-permute-start | bytes 1572872 | tf_op jit(solution)/shard_map/ppermute | solution.py:421
  116.1 33.8 %collective-permute-start.8 = (f32[4,2,32,512]{3,2,1,0:T(8,128)}, f32[4,2,32,512]{3,2,1,0:T(8,128)S(1)}, u32[]{:S(2)}, u32[]{:S(2)}) collective-permute-start(f32[4,2,32,512]{3,2,1,0:T(8,128)} %get-tuple-element.29), channel_id=1, source_target_pairs={{8,24},{24,40},{40,56},{56,72},{72,88},{88,104},{104,120},{120,136... | collective-permute-start | bytes 1572872 | tf_op jit(solution)/shard_map/ppermute | solution.py:422
  116.8 33.1 %collective-permute-start.9 = (f32[4,2,32,512]{3,2,1,0:T(8,128)}, f32[4,2,32,512]{3,2,1,0:T(8,128)S(1)}, u32[]{:S(2)}, u32[]{:S(2)}) collective-permute-start(f32[4,2,32,512]{3,2,1,0:T(8,128)} %get-tuple-element.28), channel_id=1, source_target_pairs={{24,8},{40,24},{56,40},{72,56},{88,72},{104,88},{120,104},{136,120... | collective-permute-start | bytes 1572872 | tf_op jit(solution)/shard_map/ppermute | solution.py:423
  159.3 62.1 %all-to-all-start.1 = ((f32[256,16,128]{2,1,0:T(8,128)}), f32[256,16,128]{2,1,0:T(8,128)S(1)}, u32[]{:S(2)}, u32[]{:S(2)}) async-start(f32[256,16,128]{2,1,0:T(8,128)} %bitcast.34), calls=%async_computation.1 | async-start | bytes 4194304 | tf_op jit(solution)/shard_map/all_to_all | solution.py:452
  168.0 48.8 %copy-start.6 = (s32[2]{0:T(128)S(1)}, s32[2]{0:T(128)}, u32[]{:S(2)}) copy-start(s32[2]{0:T(128)} %copy-done.5) | copy-start | bytes 28
  169.6 11.5 %collective-permute-start.12 = (f32[2,32,1024]{2,1,0:T(8,128)S(1)}, f32[2,32,1024]{2,1,0:T(8,128)S(1)}, u32[]{:S(2)}, u32[]{:S(2)}) collective-permute-start(f32[2,32,1024]{2,1,0:T(8,128)S(1)} %get-tuple-element.26), channel_id=1, source_target_pairs={{0,1},{1,2},{2,3},{3,4},{4,5},{5,6},{6,7},{7,0},{8,9},{9,10},{10,1... | collective-permute-start | bytes 786440 | tf_op jit(solution)/shard_map/ppermute | solution.py:448
  171.3 29.1 %collective-permute-start.13 = (f32[2,32,1024]{2,1,0:T(8,128)S(1)}, f32[2,32,1024]{2,1,0:T(8,128)S(1)}, u32[]{:S(2)}, u32[]{:S(2)}) collective-permute-start(f32[2,32,1024]{2,1,0:T(8,128)S(1)} %get-tuple-element.25), channel_id=1, source_target_pairs={{0,2},{1,3},{2,4},{3,5},{4,6},{5,7},{6,0},{7,1},{8,10},{9,11},{10,... | collective-permute-start | bytes 786440 | tf_op jit(solution)/shard_map/ppermute | solution.py:448
  172.5 35.2 %collective-permute-start.14 = (f32[2,32,1024]{2,1,0:T(8,128)S(1)}, f32[2,32,1024]{2,1,0:T(8,128)S(1)}, u32[]{:S(2)}, u32[]{:S(2)}) collective-permute-start(f32[2,32,1024]{2,1,0:T(8,128)S(1)} %get-tuple-element.24), channel_id=1, source_target_pairs={{0,3},{1,4},{2,5},{3,6},{4,7},{5,0},{6,1},{7,2},{8,11},{9,12},{10,... | collective-permute-start | bytes 786440 | tf_op jit(solution)/shard_map/ppermute | solution.py:448
  174.2 40.6 %collective-permute-start.15 = (f32[2,32,1024]{2,1,0:T(8,128)S(1)}, f32[2,32,1024]{2,1,0:T(8,128)S(1)}, u32[]{:S(2)}, u32[]{:S(2)}) collective-permute-start(f32[2,32,1024]{2,1,0:T(8,128)S(1)} %get-tuple-element.23), channel_id=1, source_target_pairs={{0,4},{1,5},{2,6},{3,7},{4,0},{5,1},{6,2},{7,3},{8,12},{9,13},{10,... | collective-permute-start | bytes 786440 | tf_op jit(solution)/shard_map/ppermute | solution.py:448
  175.6 40.0 %collective-permute-start.16 = (f32[2,32,1024]{2,1,0:T(8,128)S(1)}, f32[2,32,1024]{2,1,0:T(8,128)S(1)}, u32[]{:S(2)}, u32[]{:S(2)}) collective-permute-start(f32[2,32,1024]{2,1,0:T(8,128)S(1)} %get-tuple-element.22), channel_id=1, source_target_pairs={{0,5},{1,6},{2,7},{3,0},{4,1},{5,2},{6,3},{7,4},{8,13},{9,14},{10,... | collective-permute-start | bytes 786440 | tf_op jit(solution)/shard_map/ppermute | solution.py:448
  181.1 34.4 %collective-permute-start.17 = (f32[2,32,1024]{2,1,0:T(8,128)S(1)}, f32[2,32,1024]{2,1,0:T(8,128)S(1)}, u32[]{:S(2)}, u32[]{:S(2)}) collective-permute-start(f32[2,32,1024]{2,1,0:T(8,128)S(1)} %get-tuple-element.21), channel_id=1, source_target_pairs={{0,6},{1,7},{2,0},{3,1},{4,2},{5,3},{6,4},{7,5},{8,14},{9,15},{10,... | collective-permute-start | bytes 786440 | tf_op jit(solution)/shard_map/ppermute | solution.py:448
  200.4 16.3 %collective-permute-start.18 = (f32[2,32,1024]{2,1,0:T(8,128)S(1)}, f32[2,32,1024]{2,1,0:T(8,128)S(1)}, u32[]{:S(2)}, u32[]{:S(2)}) collective-permute-start(f32[2,32,1024]{2,1,0:T(8,128)S(1)} %get-tuple-element.20), channel_id=1, source_target_pairs={{0,7},{1,0},{2,1},{3,2},{4,3},{5,4},{6,5},{7,6},{8,15},{9,8},{10,9... | collective-permute-start | bytes 786440 | tf_op jit(solution)/shard_map/ppermute | solution.py:448
  (11 other events, 66.6 us)

commit v5 on v4

--- a/solution.py
+++ b/solution.py
@@ -18,6 +18,7 @@
 N_COL = 8
 PARTS = N_ROW * N_COL
 LOW = 32
+RING = 8
 ORDER = [0, 2, 4, 6, 1, 3, 5, 7]
 F32 = jnp.float32
 BF16 = jnp.bfloat16
@@ -133,8 +134,10 @@
 
 def corners(pos, local, lower, upper):
     moved = jnp.logical_and(lax.rem(pos[0], 2) == 0, lax.rem(pos[1], 2) == 1)
+    first = lax.rem(pos[0], RING) == 0
     local, lower, upper = frame(pos, local), frame(pos, lower), frame(pos, upper)
-    here = tuple(jnp.where(moved, x, y) for x, y in zip(lower, local))
+    shared = tuple(jnp.where(first, x, y) for x, y in zip(upper, lower))
+    here = tuple(jnp.where(moved, x, y) for x, y in zip(shared, local))
     up = tuple(jnp.where(moved, x, y) for x, y in zip(local, upper))
     return here, lower, up
 
@@ -182,12 +185,15 @@
 
 def field_of(where, spec, from_lower, from_upper, pupil):
     (at_row, at_col), _, _ = corners(*where)
+    row, col = where[0][0], where[0][1]
+    around = jnp.logical_and(lax.rem(row, RING) == 0, lax.rem(col, 2) == 1)
+    ahead = jnp.where(around, RING * ROWS, M)
     cols = lax.broadcasted_iota(jnp.int32, (ROWS, M), 1)
     rows = lax.broadcasted_iota(jnp.int32, (ROWS, M), 0)
     field = []
     for part in range(2):
         own = jnp.where(cols >= at_col, spec[part, :, :M], spec[part, :, M:])
-        other = jnp.where(inside(rows + M, at_row), from_upper[part], from_lower[part])
+        other = jnp.where(inside(rows + ahead, at_row), from_upper[part], from_lower[part])
         field.append(jnp.where(inside(rows, at_row), own, other))
     re = split(pupil[0] * field[0] - pupil[1] * field[1])
     im = split(pupil[0] * field[1] + pupil[1] * field[0])
@@ -348,25 +354,39 @@
 
 
 def downward(row, core):
+    if row % RING == 0 and core == 1:
+        return row - RING if row >= RING else None
     return row - 2 if row >= 2 and (row % 2 == 1 or core == 0) else None
+
+
+def second(row):
+    return row + 2 if row % RING < RING - 2 else row - (RING - 2)
 
 
 def upward(row, core):
     if row % 2 == 0:
-        return (row + 2) % N_ROW if core == 1 else None
+        return second(row) if core == 1 else None
     return row + 2 if row + 2 < N_ROW else None
 
 
+def ring_step(row, by):
+    return row // RING * RING + (row + by) % RING
+
+
 def partner(row, core):
-    return row ^ 1 if core == 0 else (row + (1 if row % 2 == 1 else -1)) % N_ROW
+    return row ^ 1 if core == 0 else ring_step(row, 1 if row % 2 == 1 else -1)
 
 
 def near(row, core):
-    return row ^ 1 if core == 0 else (row + 1) % N_ROW
+    return row ^ 1 if core == 0 else ring_step(row, 1)
 
 
 def far(row, core):
-    return (row + 2) % N_ROW if core == 1 and row % 2 == 0 else None
+    return second(row) if core == 1 and row % 2 == 0 else None
+
+
+def from_upper_row(row, core):
+    return second(row) if core == 1 and row % 2 == 0 else (row - 2) % N_ROW
 
 
 BOTH = ("row", "col")
@@ -376,7 +396,7 @@
 NEAR = moves(near)
 FAR = moves(far)
 FROM_LOWER = moves(lambda row, core: (row + 2) % N_ROW)
-FROM_UPPER = moves(lambda row, core: row - 2 if row >= 2 and row % 2 == 1 else None)
+FROM_UPPER = moves(from_upper_row)
 
 
 def on_device(spectrum, pupil, amplitude, offsets, holds, window_table, part_table, twist):
@@ -418,8 +438,9 @@
     own = lax.all_to_all(grad, "col", split_axis=0, concat_axis=0, tiled=True, axis_index_groups=[ORDER])
     even, odd = own[:4], own[4:]
     lower_even = lax.ppermute(even, "row", [(row, row + 2) for row in range(N_ROW - 2)])
-    upper_odd = lax.ppermute(odd, "row", [(row, row - 2) for row in range(2, N_ROW)] + [(0, N_ROW - 2)])
-    lower_odd = lax.ppermute(odd, "row", [(row, row + 2) for row in range(1, N_ROW - 2, 2)])
+    upper_odd = lax.ppermute(odd, "row", [(row, row + RING - 2 if row % RING == 0 else row - 2) for row in range(N_ROW) if row != 1])
+    ahead = [(row, row + RING) for row in range(0, N_ROW - RING, RING)]
+    lower_odd = lax.ppermute(odd, "row", [(row, row + 2) for row in range(1, N_ROW - 2, 2)] + ahead)
     upper_even = lax.ppermute(even, "row", [(row, row - 2) for row in range(3, N_ROW, 2)])
     outgoing, shares = call(
         rows_kernel,

time: 226 us -> 223 us (0.987)
    ppermute x1, starting transfers between devices: 25.9 us -> 1.92 us  [on_device(): far_amp = lax.ppermute(far_half, BOTH, FAR)]
    ppermute x1, waiting for transfers between devices: 3.14 us -> 26.6 us  [on_device(): near_amp = lax.ppermute(near_half, BOTH, NEAR)]
    ppermute x1, waiting for transfers between devices: 18 us -> 5.16 us  [on_device(): lax.ppermute(even, 'row', [(row, row + 2) for row in range(N_ROW - 2)])]
    all_to_all x1, starting transfers between devices: 8.65 us -> 20.6 us  [on_device(): lax.all_to_all(outgoing.reshape(PARTS, 16, 128), ('row', 'col'), split_ax...]
    ppermute x2, waiting for transfers between devices: 13.5 us -> 7.98 us  [on_device(): other = lax.ppermute(send, BOTH, PARTNERS)]
    ppermute x2, starting transfers between devices: 2.61 us -> 7.24 us  [the longest x1 4.09 us: on_device(): lax.ppermute(odd, 'row', [(row, row + RING - 2 if row % RING == 0 else ro...]
    ppermute x1, starting transfers between devices: 5.84 us -> 1.92 us  [on_device(): from_lower = lax.ppermute(to_upper, BOTH, UP)]
    ppermute x1, starting transfers between devices: 0.65 us -> 4.2 us  [on_device(): upper = lax.ppermute(local, BOTH, FROM_UPPER)]
  transfers between devices with their start and end apart: 20 -> 20, of which waited for: 15 -> 14; matrix products, arithmetic and copies ran while one was open for 2% -> 2% of each run, Pallas kernels for 6% -> 6%
where the time goes in v5:
time: 223 us
  waiting for transfers between devices  94.2 us (42%)
  starting transfers between devices  62.5 us (28%)
  Pallas kernels  28.3 us (13%)
  blocking collectives  26.9 us (12%)
  local copies, waits for them, and re-layouts  8.83 us (4%)
    ppermute x7, waiting for transfers between devices, on_device(): lax.ppermute(shares[step], 'col', [(at, (at + step) % N_COL) for at in ra...  35.4 us
    pallas_call x11, Pallas kernels, call(): pl.pallas_call(kernel, out_shape=tuple((jax.ShapeDtypeStruct(shape, F32)...  28.3 us
    ppermute x1, waiting for transfers between devices, on_device(): near_amp = lax.ppermute(near_half, BOTH, NEAR)  26.6 us
    all_to_all x1, starting transfers between devices, on_device(): lax.all_to_all(outgoing.reshape(PARTS, 16, 128), ('row', 'col'), split_ax...  20.6 us
    all_to_all x1, blocking collectives, on_device(): lax.all_to_all(grad, 'col', split_axis=0, concat_axis=0, tiled=True, axis...  19.4 us
    ppermute x7, starting transfers between devices, on_device(): lax.ppermute(shares[step], 'col', [(at, (at + step) % N_COL) for at in ra...  11.6 us
    ppermute x1, waiting for transfers between devices, on_device(): from_lower = lax.ppermute(to_upper, BOTH, UP)  9.12 us
    ppermute x2, waiting for transfers between devices, on_device(): other = lax.ppermute(send, BOTH, PARTNERS)  7.98 us
  transfers between devices with their start and end apart: 20, of which 14 were waited for; matrix products, arithmetic and copies ran while one was open for 2% of the time, Pallas kernels for 6%

profile of v5, /device:TPU:1, one launch (start us, length us, event | category | flops | bytes accessed | tf_op | source)
XLA Modules:
  0.0 222.6 jit_solution(10421783489421631031)
XLA Ops:
  0.6 3.9 %collective-permute-start = (s32[2]{0:T(128)}, s32[2]{0:T(128)S(1)}, u32[]{:S(2)}, u32[]{:S(2)}) collective-permute-start(s32[2]{0:T(128)} %bitcast.27), channel_id=1, source_target_pairs={{0,16},{1,17},{2,18},{3,19},{4,20},{5,21},{6,22},{7,23},{8,24},{9,... | collective-permute-start | bytes 32 | tf_op jit(solution)/shard_map/ppermute | solution.py:407
  4.5 4.2 %collective-permute-start.1 = (s32[2]{0:T(128)}, s32[2]{0:T(128)S(1)}, u32[]{:S(2)}, u32[]{:S(2)}) collective-permute-start(s32[2]{0:T(128)} %bitcast.28), channel_id=1, source_target_pairs={{0,240},{1,17},{2,242},{3,19},{4,244},{5,21},{6,246},{7,23},{8,248... | collective-permute-start | bytes 32 | tf_op jit(solution)/shard_map/ppermute | solution.py:408
  17.9 26.6 %collective-permute-done.2.near_amp = f32[512,256]{1,0:T(8,128)S(1)} collective-permute-done((f32[512,256]{1,0:T(8,128)S(1)}, f32[512,256]{1,0:T(8,128)S(1)}, u32[]{:S(2)}, u32[]{:S(2)}) %collective-permute-start.2) | collective-permute-done | bytes 524320 | tf_op jit(solution)/shard_map/ppermute | solution.py:416
  48.6 9.1 %collective-permute-done.4.from_lower = f32[2,256,512]{2,1,0:T(8,128)S(1)} collective-permute-done((f32[2,256,512]{2,1,0:T(8,128)S(1)}, f32[2,256,512]{2,1,0:T(8,128)S(1)}, u32[]{:S(2)}, u32[]{:S(2)}) %collective-permute-start.4) | collective-permute-done | bytes 1048608 | tf_op jit(solution)/shard_map/ppermute | solution.py:421
  61.1 3.0 %shard_map.89.wave = f32[2,512,256]{2,1,0:T(8,128)S(1)} custom-call(s32[2]{0:T(128)S(1)} %pad_add_fusion.pos, s32[2]{0:T(128)S(1)} %bitcast.32, s32[2]{0:T(128)S(1)} %collective-permute-done.lower, s32[2]{0:T(128)S(1)} %collective-permute-done.1.upper, f32[2,256,1024]{2,1,0:T(8,128)S(1)} %shard_map.87.spec, ...), custom_call_target="tpu_custom_call" | custom-call | tf_op jit(solution)/shard_map/pallas_call | solution.py:120
  69.1 2.8 %shard_map.91 = (f32[2,512,256]{2,1,0:T(8,128)S(1)}, f32[2,256,256]{2,1,0:T(8,128)S(1)}) custom-call(s32[2]{0:T(128)S(1)} %pad_add_fusion.pos, f32[512,256]{1,0:T(8,128)S(1)} %collective-permute-done.3.far_amp, f32[512,256]{1,0:T(8,128)S(1)} %get-tuple-element.12.measured, f32[2,512,256]{2,1,0:T(8,128)S(1)} %shard_map.89.wave, ...), custom_call_target="tpu_custom_call" | custom-call | tf_op jit(solution)/shard_map/pallas_call | solution.py:120
  75.8 5.5 %collective-permute-done.7.other = f32[2,256,256]{2,1,0:T(8,128)S(1)} collective-permute-done((f32[2,256,256]{2,1,0:T(8,128)S(1)}, f32[2,256,256]{2,1,0:T(8,128)S(1)}, u32[]{:S(2)}, u32[]{:S(2)}) %collective-permute-start.7) | collective-permute-done | bytes 524320 | tf_op jit(solution)/shard_map/ppermute | solution.py:434
  83.0 19.4 %all_to_all.10.own = f32[8,2,32,512]{3,2,1,0:T(8,128)S(1)} all-to-all(f32[8,2,32,512]{3,2,1,0:T(8,128)S(1)} %shard_map.93), channel_id=1, replica_groups={{0,2,4,6,1,3,5,7},{8,10,12,14,9,11,13,15},{16,18,20,22,17,19,21,23},{24..., dimensions={0} | all-to-all | bytes 2097152 | tf_op jit(solution)/shard_map/all_to_all | solution.py:438
  103.7 4.2 %collective-permute-start.10 = (f32[4,2,32,512]{3,2,1,0:T(8,128)}, f32[4,2,32,512]{3,2,1,0:T(8,128)S(1)}, u32[]{:S(2)}, u32[]{:S(2)}) collective-permute-start(f32[4,2,32,512]{3,2,1,0:T(8,128)} %get-tuple-element.28), channel_id=1, source_target_pairs={{0,16},{8,24},{16,32},{24,40},{32,48},{40,56},{48,64},{56,72},{64,... | collective-permute-start | bytes 1572872 | tf_op jit(solution)/shard_map/ppermute | solution.py:440
  107.8 4.1 %collective-permute-start.11 = (f32[4,2,32,512]{3,2,1,0:T(8,128)}, f32[4,2,32,512]{3,2,1,0:T(8,128)S(1)}, u32[]{:S(2)}, u32[]{:S(2)}) collective-permute-start(f32[4,2,32,512]{3,2,1,0:T(8,128)} %get-tuple-element.29), channel_id=1, source_target_pairs={{0,48},{16,0},{24,8},{32,16},{40,24},{48,32},{56,40},{64,112},{72,... | collective-permute-start | bytes 1572872 | tf_op jit(solution)/shard_map/ppermute | solution.py:441
  111.9 3.1 %collective-permute-start.8 = (f32[4,2,32,512]{3,2,1,0:T(8,128)}, f32[4,2,32,512]{3,2,1,0:T(8,128)S(1)}, u32[]{:S(2)}, u32[]{:S(2)}) collective-permute-start(f32[4,2,32,512]{3,2,1,0:T(8,128)} %get-tuple-element.29), channel_id=1, source_target_pairs={{8,24},{24,40},{40,56},{56,72},{72,88},{88,104},{104,120},{120,136... | collective-permute-start | bytes 1572872 | tf_op jit(solution)/shard_map/ppermute | solution.py:443
  117.3 7.5 %all-reduce = s32[48]{0:T(128)S(1)} all-reduce(s32[48]{0:T(128)S(1)} %add_dynamic-update-slice_fusion), channel_id=2, replica_groups=mesh['row'=32,'col'=8] {'col'}, use_global_device_ids=true, to_apply=%add | all-reduce | flops 48 | bytes 384
  125.5 5.2 %collective-permute-done.10.lower_even = f32[4,2,32,512]{3,2,1,0:T(8,128)S(1)} collective-permute-done((f32[4,2,32,512]{3,2,1,0:T(8,128)}, f32[4,2,32,512]{3,2,1,0:T(8,128)S(1)}, u32[]{:S(2)}, u32[]{:S(2)}) %collective-permute-start.10) | collective-permute-done | bytes 524320 | tf_op jit(solution)/shard_map/ppermute | solution.py:440
  130.6 4.8 %collective-permute-done.8.lower_odd = f32[4,2,32,512]{3,2,1,0:T(8,128)S(1)} collective-permute-done((f32[4,2,32,512]{3,2,1,0:T(8,128)}, f32[4,2,32,512]{3,2,1,0:T(8,128)S(1)}, u32[]{:S(2)}, u32[]{:S(2)}) %collective-permute-start.8) | collective-permute-done | bytes 524320 | tf_op jit(solution)/shard_map/ppermute | solution.py:443
  137.0 7.7 %shard_map.94 = (f32[4096,128]{1,0:T(8,128)}, f32[8,2,32,1024]{3,2,1,0:T(8,128)}) custom-call(s32[2]{0:T(128)} %copy-done.5, s32[8,6]{1,0:T(8,128)} %reshape.13.leds, f32[8,2,32,512]{3,2,1,0:T(8,128)} %copy-done.9, f32[4,2,32,512]{3,2,1,0:T(8,128)} %copy-done.12, f32[4,2,32,512]{3,2,1,0:T(8,128)} %copy-done.13, f32[4,2,32,512]{3,2,1,0:T(8,128)} %copy-done.10, ...), custom_call_target="tpu_custom_call" | custom-call | tf_op jit(solution)/shard_map/pallas_call | solution.py:120
  144.7 20.6 %all-to-all-start.1 = ((f32[256,16,128]{2,1,0:T(8,128)}), f32[256,16,128]{2,1,0:T(8,128)S(1)}, u32[]{:S(2)}, u32[]{:S(2)}) async-start(f32[256,16,128]{2,1,0:T(8,128)} %bitcast.34), calls=%async_computation.1 | async-start | bytes 4194304 | tf_op jit(solution)/shard_map/all_to_all | solution.py:473
  172.9 2.6 %collective-permute-start.16 = (f32[2,32,1024]{2,1,0:T(8,128)S(1)}, f32[2,32,1024]{2,1,0:T(8,128)S(1)}, u32[]{:S(2)}, u32[]{:S(2)}) collective-permute-start(f32[2,32,1024]{2,1,0:T(8,128)S(1)} %get-tuple-element.22), channel_id=1, source_target_pairs={{0,5},{1,6},{2,7},{3,0},{4,1},{5,2},{6,3},{7,4},{8,13},{9,14},{10,... | collective-permute-start | bytes 786440 | tf_op jit(solution)/shard_map/ppermute | solution.py:469
  175.5 3.0 %collective-permute-done.12.refs_1_ = f32[2,32,1024]{2,1,0:T(8,128)S(1)} collective-permute-done((f32[2,32,1024]{2,1,0:T(8,128)S(1)}, f32[2,32,1024]{2,1,0:T(8,128)S(1)}, u32[]{:S(2)}, u32[]{:S(2)}) %collective-permute-start.12) | collective-permute-done | bytes 262176 | tf_op jit(solution)/shard_map/ppermute | solution.py:469
  178.5 3.1 %collective-permute-start.17 = (f32[2,32,1024]{2,1,0:T(8,128)S(1)}, f32[2,32,1024]{2,1,0:T(8,128)S(1)}, u32[]{:S(2)}, u32[]{:S(2)}) collective-permute-start(f32[2,32,1024]{2,1,0:T(8,128)S(1)} %get-tuple-element.21), channel_id=1, source_target_pairs={{0,6},{1,7},{2,0},{3,1},{4,2},{5,3},{6,4},{7,5},{8,14},{9,15},{10,... | collective-permute-start | bytes 786440 | tf_op jit(solution)/shard_map/ppermute | solution.py:469
  181.6 16.1 %collective-permute-done.13.refs_2_ = f32[2,32,1024]{2,1,0:T(8,128)S(1)} collective-permute-done((f32[2,32,1024]{2,1,0:T(8,128)S(1)}, f32[2,32,1024]{2,1,0:T(8,128)S(1)}, u32[]{:S(2)}, u32[]{:S(2)}) %collective-permute-start.13) | collective-permute-done | bytes 262176 | tf_op jit(solution)/shard_map/ppermute | solution.py:469
  197.7 7.3 %collective-permute-done.14.refs_3_ = f32[2,32,1024]{2,1,0:T(8,128)S(1)} collective-permute-done((f32[2,32,1024]{2,1,0:T(8,128)S(1)}, f32[2,32,1024]{2,1,0:T(8,128)S(1)}, u32[]{:S(2)}, u32[]{:S(2)}) %collective-permute-start.14) | collective-permute-done | bytes 262176 | tf_op jit(solution)/shard_map/ppermute | solution.py:469
  205.0 7.1 %collective-permute-done.15.refs_4_ = f32[2,32,1024]{2,1,0:T(8,128)S(1)} collective-permute-done((f32[2,32,1024]{2,1,0:T(8,128)S(1)}, f32[2,32,1024]{2,1,0:T(8,128)S(1)}, u32[]{:S(2)}, u32[]{:S(2)}) %collective-permute-start.15) | collective-permute-done | bytes 262176 | tf_op jit(solution)/shard_map/ppermute | solution.py:469
  216.1 2.6 %all-to-all-done.1 = f32[256,16,128]{2,1,0:T(8,128)S(1)} async-done(((f32[256,16,128]{2,1,0:T(8,128)}), f32[256,16,128]{2,1,0:T(8,128)S(1)}, u32[]{:S(2)}, u32[]{:S(2)}) %all-to-all-start.1) | async-done | bytes 2097184 | tf_op jit(solution)/shard_map/all_to_all | solution.py:473
  218.7 3.7 %shard_map.96 = f32[2,32,8192]{2,1,0:T(8,128)} custom-call(f32[4096,128]{1,0:T(8,128)S(1)} %bitcast.25, f32[2,32,256]{2,1,0:T(8,128)S(1)} %copy-done.3, bf16[4,256,256]{2,1,0:T(8,128)(2,1)S(1)} %copy-done.1), custom_call_target="tpu_custom_call" | custom-call | tf_op jit(solution)/shard_map/pallas_call | solution.py:120
  (67 shorter events, 43.8 us)
Async XLA Ops:
  0.6 12.9 %collective-permute-start = (s32[2]{0:T(128)}, s32[2]{0:T(128)S(1)}, u32[]{:S(2)}, u32[]{:S(2)}) collective-permute-start(s32[2]{0:T(128)} %bitcast.27), channel_id=1, source_target_pairs={{0,16},{1,17},{2,18},{3,19},{4,20},{5,21},{6,22},{7,23},{8,24},{9,... | collective-permute-start | bytes 32 | tf_op jit(solution)/shard_map/ppermute | solution.py:407
  4.5 9.0 %collective-permute-start.1 = (s32[2]{0:T(128)}, s32[2]{0:T(128)S(1)}, u32[]{:S(2)}, u32[]{:S(2)}) collective-permute-start(s32[2]{0:T(128)} %bitcast.28), channel_id=1, source_target_pairs={{0,240},{1,17},{2,242},{3,19},{4,244},{5,21},{6,246},{7,23},{8,248... | collective-permute-start | bytes 32 | tf_op jit(solution)/shard_map/ppermute | solution.py:408
  9.8 34.7 %collective-permute-start.2 = (f32[512,256]{1,0:T(8,128)S(1)}, f32[512,256]{1,0:T(8,128)S(1)}, u32[]{:S(2)}, u32[]{:S(2)}) collective-permute-start(f32[512,256]{1,0:T(8,128)S(1)} %dynamic-slice_bitcast_fusion), channel_id=1, source_target_pairs={{0,8},{1,9},{2,10},{3,11},{4,12},{5,13},{6,14},{7,15},{8,0},{9,17}... | collective-permute-start | bytes 1572872 | tf_op jit(solution)/shard_map/ppermute | solution.py:416
  13.5 67.8 %copy-start.5 = (s32[2]{0:T(128)}, s32[2]{0:T(128)S(1)}, u32[]{:S(2)}) copy-start(s32[2]{0:T(128)S(1)} %pad_add_fusion.pos) | copy-start | bytes 28
  14.7 43.0 %collective-permute-start.4 = (f32[2,256,512]{2,1,0:T(8,128)S(1)}, f32[2,256,512]{2,1,0:T(8,128)S(1)}, u32[]{:S(2)}, u32[]{:S(2)}) collective-permute-start(f32[2,256,512]{2,1,0:T(8,128)S(1)} %get-tuple-element.13), channel_id=1, source_target_pairs={{1,17},{3,19},{5,21},{7,23},{8,24},{9,25},{10,26},{11,27},{12,28},... | collective-permute-start | bytes 3145736 | tf_op jit(solution)/shard_map/ppermute | solution.py:421
  16.6 41.1 %collective-permute-start.5 = (f32[2,256,512]{2,1,0:T(8,128)S(1)}, f32[2,256,512]{2,1,0:T(8,128)S(1)}, u32[]{:S(2)}, u32[]{:S(2)}) collective-permute-start(f32[2,256,512]{2,1,0:T(8,128)S(1)} %get-tuple-element.14), channel_id=1, source_target_pairs={{16,0},{18,2},{20,4},{22,6},{24,8},{25,9},{26,10},{27,11},{28,12},... | collective-permute-start | bytes 3145736 | tf_op jit(solution)/shard_map/ppermute | solution.py:420
  46.6 20.0 %collective-permute-start.3 = (f32[512,256]{1,0:T(8,128)S(1)}, f32[512,256]{1,0:T(8,128)S(1)}, u32[]{:S(2)}, u32[]{:S(2)}) collective-permute-start(f32[512,256]{1,0:T(8,128)S(1)} %get-tuple-element.11), channel_id=1, source_target_pairs={{1,17},{3,19},{5,21},{7,23},{17,33},{19,35},{21,37},{23,39},{33,49... | collective-permute-start | bytes 1572872 | tf_op jit(solution)/shard_map/ppermute | solution.py:425
  59.7 9.3 %collective-permute-start.6 = (f32[2,256,256]{2,1,0:T(8,128)S(1)}, f32[2,256,256]{2,1,0:T(8,128)S(1)}, u32[]{:S(2)}, u32[]{:S(2)}) collective-permute-start(f32[2,256,256]{2,1,0:T(8,128)S(1)} %shard_map.90), channel_id=1, source_target_pairs={{0,8},{1,57},{2,10},{3,59},{4,12},{5,61},{6,14},{7,63},{8,0},{9,17... | collective-permute-start | bytes 1572872 | tf_op jit(solution)/shard_map/ppermute | solution.py:429
  71.8 9.5 %collective-permute-start.7 = (f32[2,256,256]{2,1,0:T(8,128)S(1)}, f32[2,256,256]{2,1,0:T(8,128)S(1)}, u32[]{:S(2)}, u32[]{:S(2)}) collective-permute-start(f32[2,256,256]{2,1,0:T(8,128)S(1)} %get-tuple-element.17), channel_id=1, source_target_pairs={{0,8},{1,57},{2,10},{3,59},{4,12},{5,61},{6,14},{7,63},{8,0},{9,17... | collective-permute-start | bytes 1572872 | tf_op jit(solution)/shard_map/ppermute | solution.py:434
  83.0 32.8 %copy-start.14 = (u32[256]{0:T(256)S(1)}, u32[256]{0:T(256)}, u32[]{:S(2)}) copy-start(u32[256]{0:T(256)} %constant.42) | copy-start | bytes 3076
  102.5 32.9 %copy-start.9 = (f32[8,2,32,512]{3,2,1,0:T(8,128)}, f32[8,2,32,512]{3,2,1,0:T(8,128)S(1)}, u32[]{:S(2)}) copy-start(f32[8,2,32,512]{3,2,1,0:T(8,128)S(1)} %all_to_all.10.own) | copy-start | bytes 3145732
  103.7 27.0 %collective-permute-start.10 = (f32[4,2,32,512]{3,2,1,0:T(8,128)}, f32[4,2,32,512]{3,2,1,0:T(8,128)S(1)}, u32[]{:S(2)}, u32[]{:S(2)}) collective-permute-start(f32[4,2,32,512]{3,2,1,0:T(8,128)} %get-tuple-element.28), channel_id=1, source_target_pairs={{0,16},{8,24},{16,32},{24,40},{32,48},{40,56},{48,64},{56,72},{64,... | collective-permute-start | bytes 1572872 | tf_op jit(solution)/shard_map/ppermute | solution.py:440
  107.8 22.8 %collective-permute-start.11 = (f32[4,2,32,512]{3,2,1,0:T(8,128)}, f32[4,2,32,512]{3,2,1,0:T(8,128)S(1)}, u32[]{:S(2)}, u32[]{:S(2)}) collective-permute-start(f32[4,2,32,512]{3,2,1,0:T(8,128)} %get-tuple-element.29), channel_id=1, source_target_pairs={{0,48},{16,0},{24,8},{32,16},{40,24},{48,32},{56,40},{64,112},{72,... | collective-permute-start | bytes 1572872 | tf_op jit(solution)/shard_map/ppermute | solution.py:441
  111.9 23.4 %collective-permute-start.8 = (f32[4,2,32,512]{3,2,1,0:T(8,128)}, f32[4,2,32,512]{3,2,1,0:T(8,128)S(1)}, u32[]{:S(2)}, u32[]{:S(2)}) collective-permute-start(f32[4,2,32,512]{3,2,1,0:T(8,128)} %get-tuple-element.29), channel_id=1, source_target_pairs={{8,24},{24,40},{40,56},{56,72},{72,88},{88,104},{104,120},{120,136... | collective-permute-start | bytes 1572872 | tf_op jit(solution)/shard_map/ppermute | solution.py:443
  115.1 20.3 %collective-permute-start.9 = (f32[4,2,32,512]{3,2,1,0:T(8,128)}, f32[4,2,32,512]{3,2,1,0:T(8,128)S(1)}, u32[]{:S(2)}, u32[]{:S(2)}) collective-permute-start(f32[4,2,32,512]{3,2,1,0:T(8,128)} %get-tuple-element.28), channel_id=1, source_target_pairs={{24,8},{40,24},{56,40},{72,56},{88,72},{104,88},{120,104},{136,120... | collective-permute-start | bytes 1572872 | tf_op jit(solution)/shard_map/ppermute | solution.py:444
  144.7 74.0 %all-to-all-start.1 = ((f32[256,16,128]{2,1,0:T(8,128)}), f32[256,16,128]{2,1,0:T(8,128)S(1)}, u32[]{:S(2)}, u32[]{:S(2)}) async-start(f32[256,16,128]{2,1,0:T(8,128)} %bitcast.34), calls=%async_computation.1 | async-start | bytes 4194304 | tf_op jit(solution)/shard_map/all_to_all | solution.py:473
  165.3 48.8 %copy-start.6 = (s32[2]{0:T(128)S(1)}, s32[2]{0:T(128)}, u32[]{:S(2)}) copy-start(s32[2]{0:T(128)} %copy-done.5) | copy-start | bytes 28
  167.0 11.5 %collective-permute-start.12 = (f32[2,32,1024]{2,1,0:T(8,128)S(1)}, f32[2,32,1024]{2,1,0:T(8,128)S(1)}, u32[]{:S(2)}, u32[]{:S(2)}) collective-permute-start(f32[2,32,1024]{2,1,0:T(8,128)S(1)} %get-tuple-element.26), channel_id=1, source_target_pairs={{0,1},{1,2},{2,3},{3,4},{4,5},{5,6},{6,7},{7,0},{8,9},{9,10},{10,1... | collective-permute-start | bytes 786440 | tf_op jit(solution)/shard_map/ppermute | solution.py:469
  168.6 29.1 %collective-permute-start.13 = (f32[2,32,1024]{2,1,0:T(8,128)S(1)}, f32[2,32,1024]{2,1,0:T(8,128)S(1)}, u32[]{:S(2)}, u32[]{:S(2)}) collective-permute-start(f32[2,32,1024]{2,1,0:T(8,128)S(1)} %get-tuple-element.25), channel_id=1, source_target_pairs={{0,2},{1,3},{2,4},{3,5},{4,6},{5,7},{6,0},{7,1},{8,10},{9,11},{10,... | collective-permute-start | bytes 786440 | tf_op jit(solution)/shard_map/ppermute | solution.py:469
  169.8 35.2 %collective-permute-start.14 = (f32[2,32,1024]{2,1,0:T(8,128)S(1)}, f32[2,32,1024]{2,1,0:T(8,128)S(1)}, u32[]{:S(2)}, u32[]{:S(2)}) collective-permute-start(f32[2,32,1024]{2,1,0:T(8,128)S(1)} %get-tuple-element.24), channel_id=1, source_target_pairs={{0,3},{1,4},{2,5},{3,6},{4,7},{5,0},{6,1},{7,2},{8,11},{9,12},{10,... | collective-permute-start | bytes 786440 | tf_op jit(solution)/shard_map/ppermute | solution.py:469
  171.5 40.6 %collective-permute-start.15 = (f32[2,32,1024]{2,1,0:T(8,128)S(1)}, f32[2,32,1024]{2,1,0:T(8,128)S(1)}, u32[]{:S(2)}, u32[]{:S(2)}) collective-permute-start(f32[2,32,1024]{2,1,0:T(8,128)S(1)} %get-tuple-element.23), channel_id=1, source_target_pairs={{0,4},{1,5},{2,6},{3,7},{4,0},{5,1},{6,2},{7,3},{8,12},{9,13},{10,... | collective-permute-start | bytes 786440 | tf_op jit(solution)/shard_map/ppermute | solution.py:469
  172.9 40.0 %collective-permute-start.16 = (f32[2,32,1024]{2,1,0:T(8,128)S(1)}, f32[2,32,1024]{2,1,0:T(8,128)S(1)}, u32[]{:S(2)}, u32[]{:S(2)}) collective-permute-start(f32[2,32,1024]{2,1,0:T(8,128)S(1)} %get-tuple-element.22), channel_id=1, source_target_pairs={{0,5},{1,6},{2,7},{3,0},{4,1},{5,2},{6,3},{7,4},{8,13},{9,14},{10,... | collective-permute-start | bytes 786440 | tf_op jit(solution)/shard_map/ppermute | solution.py:469
  178.5 34.4 %collective-permute-start.17 = (f32[2,32,1024]{2,1,0:T(8,128)S(1)}, f32[2,32,1024]{2,1,0:T(8,128)S(1)}, u32[]{:S(2)}, u32[]{:S(2)}) collective-permute-start(f32[2,32,1024]{2,1,0:T(8,128)S(1)} %get-tuple-element.21), channel_id=1, source_target_pairs={{0,6},{1,7},{2,0},{3,1},{4,2},{5,3},{6,4},{7,5},{8,14},{9,15},{10,... | collective-permute-start | bytes 786440 | tf_op jit(solution)/shard_map/ppermute | solution.py:469
  197.7 16.3 %collective-permute-start.18 = (f32[2,32,1024]{2,1,0:T(8,128)S(1)}, f32[2,32,1024]{2,1,0:T(8,128)S(1)}, u32[]{:S(2)}, u32[]{:S(2)}) collective-permute-start(f32[2,32,1024]{2,1,0:T(8,128)S(1)} %get-tuple-element.20), channel_id=1, source_target_pairs={{0,7},{1,0},{2,1},{3,2},{4,3},{5,4},{6,5},{7,6},{8,15},{9,8},{10,9... | collective-permute-start | bytes 786440 | tf_op jit(solution)/shard_map/ppermute | solution.py:469
  (11 other events, 97.7 us)

commit v6 on v5

--- a/solution.py
+++ b/solution.py
@@ -355,8 +355,8 @@
 
 def downward(row, core):
     if row % RING == 0 and core == 1:
-        return row - RING if row >= RING else None
-    return row - 2 if row >= 2 and (row % 2 == 1 or core == 0) else None
+        return (row - RING) % N_ROW
+    return (row - 2) % N_ROW if row % 2 == 1 or core == 0 else None
 
 
 def second(row):
@@ -366,7 +366,7 @@
 def upward(row, core):
     if row % 2 == 0:
         return second(row) if core == 1 else None
-    return row + 2 if row + 2 < N_ROW else None
+    return (row + 2) % N_ROW
 
 
 def ring_step(row, by):
@@ -437,11 +437,11 @@
 
     own = lax.all_to_all(grad, "col", split_axis=0, concat_axis=0, tiled=True, axis_index_groups=[ORDER])
     even, odd = own[:4], own[4:]
-    lower_even = lax.ppermute(even, "row", [(row, row + 2) for row in range(N_ROW - 2)])
-    upper_odd = lax.ppermute(odd, "row", [(row, row + RING - 2 if row % RING == 0 else row - 2) for row in range(N_ROW) if row != 1])
-    ahead = [(row, row + RING) for row in range(0, N_ROW - RING, RING)]
-    lower_odd = lax.ppermute(odd, "row", [(row, row + 2) for row in range(1, N_ROW - 2, 2)] + ahead)
-    upper_even = lax.ppermute(even, "row", [(row, row - 2) for row in range(3, N_ROW, 2)])
+    lower_even = lax.ppermute(even, "row", [(row, (row + 2) % N_ROW) for row in range(N_ROW)])
+    upper_odd = lax.ppermute(odd, "row", [(row, row + RING - 2 if row % RING == 0 else (row - 2) % N_ROW) for row in range(N_ROW)])
+    ahead = [(row, (row + RING) % N_ROW) for row in range(0, N_ROW, RING)]
+    lower_odd = lax.ppermute(odd, "row", [(row, (row + 2) % N_ROW) for row in range(1, N_ROW, 2)] + ahead)
+    upper_even = lax.ppermute(even, "row", [(row, (row - 2) % N_ROW) for row in range(1, N_ROW, 2)])
     outgoing, shares = call(
         rows_kernel,
         [(PARTS * 16, 128), (N_COL, 2, LOW, COLS)],

time: 223 us -> 219 us (0.982)
  starting transfers between devices: 62.5 us -> 59.4 us
    ppermute x4, starting transfers between devices: 12.1 us -> 8.26 us  [the longest x1 3.11 us: on_device(): lax.ppermute(odd, 'row', [(row, (row + 2) % N_ROW) for row in range(1, N_...]
    ppermute x1, starting transfers between devices: 1.29 us -> 3.73 us  [on_device(): from_upper = lax.ppermute(to_lower, BOTH, DOWN)]
    ppermute x1, waiting for transfers between devices: 26.6 us -> 24.1 us  [on_device(): near_amp = lax.ppermute(near_half, BOTH, NEAR)]
  transfers between devices with their start and end apart: 20 -> 20, of which waited for: 14 -> 15; matrix products, arithmetic and copies ran while one was open for 2% -> 2% of each run, Pallas kernels for 6% -> 6%
where the time goes in v6:
time: 219 us
  waiting for transfers between devices  93.2 us (43%)
  starting transfers between devices  59.4 us (27%)
  Pallas kernels  28.3 us (13%)
  blocking collectives  27.2 us (12%)
  local copies, waits for them, and re-layouts  8.83 us (4%)
    ppermute x7, waiting for transfers between devices, on_device(): lax.ppermute(shares[step], 'col', [(at, (at + step) % N_COL) for at in ra...  35.4 us
    pallas_call x11, Pallas kernels, call(): pl.pallas_call(kernel, out_shape=tuple((jax.ShapeDtypeStruct(shape, F32)...  28.3 us
    ppermute x1, waiting for transfers between devices, on_device(): near_amp = lax.ppermute(near_half, BOTH, NEAR)  24.1 us
    all_to_all x1, blocking collectives, on_device(): lax.all_to_all(grad, 'col', split_axis=0, concat_axis=0, tiled=True, axis...  19.4 us
    all_to_all x1, starting transfers between devices, on_device(): lax.all_to_all(outgoing.reshape(PARTS, 16, 128), ('row', 'col'), split_ax...  18.9 us
    ppermute x7, starting transfers between devices, on_device(): lax.ppermute(shares[step], 'col', [(at, (at + step) % N_COL) for at in ra...  11.6 us
    ppermute x2, waiting for transfers between devices, on_device(): other = lax.ppermute(send, BOTH, PARTNERS)  9.59 us
    ppermute x1, waiting for transfers between devices, on_device(): lax.ppermute(odd, 'row', [(row, row + RING - 2 if row % RING == 0 else (r...  9.48 us
  transfers between devices with their start and end apart: 20, of which 15 were waited for; matrix products, arithmetic and copies ran while one was open for 2% of the time, Pallas kernels for 6%

profile of v6, /device:TPU:1, one launch (start us, length us, event | category | flops | bytes accessed | tf_op | source)
XLA Modules:
  0.0 218.8 jit_solution(16465916266937525368)
XLA Ops:
  0.6 3.9 %collective-permute-start = (s32[2]{0:T(128)}, s32[2]{0:T(128)S(1)}, u32[]{:S(2)}, u32[]{:S(2)}) collective-permute-start(s32[2]{0:T(128)} %bitcast.27), channel_id=1, source_target_pairs={{0,16},{1,17},{2,18},{3,19},{4,20},{5,21},{6,22},{7,23},{8,24},{9,... | collective-permute-start | bytes 32 | tf_op jit(solution)/shard_map/ppermute | solution.py:407
  4.5 4.2 %collective-permute-start.1 = (s32[2]{0:T(128)}, s32[2]{0:T(128)S(1)}, u32[]{:S(2)}, u32[]{:S(2)}) collective-permute-start(s32[2]{0:T(128)} %bitcast.28), channel_id=1, source_target_pairs={{0,240},{1,17},{2,242},{3,19},{4,244},{5,21},{6,246},{7,23},{8,248... | collective-permute-start | bytes 32 | tf_op jit(solution)/shard_map/ppermute | solution.py:408
  16.6 3.7 %collective-permute-start.5 = (f32[2,256,512]{2,1,0:T(8,128)S(1)}, f32[2,256,512]{2,1,0:T(8,128)S(1)}, u32[]{:S(2)}, u32[]{:S(2)}) collective-permute-start(f32[2,256,512]{2,1,0:T(8,128)S(1)} %get-tuple-element.14), channel_id=1, source_target_pairs={{0,240},{1,193},{2,242},{3,195},{4,244},{5,197},{6,246},{7,199},{8... | collective-permute-start | bytes 3145736 | tf_op jit(solution)/shard_map/ppermute | solution.py:420
  20.4 24.1 %collective-permute-done.2.near_amp = f32[512,256]{1,0:T(8,128)S(1)} collective-permute-done((f32[512,256]{1,0:T(8,128)S(1)}, f32[512,256]{1,0:T(8,128)S(1)}, u32[]{:S(2)}, u32[]{:S(2)}) %collective-permute-start.2) | collective-permute-done | bytes 524320 | tf_op jit(solution)/shard_map/ppermute | solution.py:416
  48.6 9.1 %collective-permute-done.4.from_lower = f32[2,256,512]{2,1,0:T(8,128)S(1)} collective-permute-done((f32[2,256,512]{2,1,0:T(8,128)S(1)}, f32[2,256,512]{2,1,0:T(8,128)S(1)}, u32[]{:S(2)}, u32[]{:S(2)}) %collective-permute-start.4) | collective-permute-done | bytes 1048608 | tf_op jit(solution)/shard_map/ppermute | solution.py:421
  61.1 3.0 %shard_map.89.wave = f32[2,512,256]{2,1,0:T(8,128)S(1)} custom-call(s32[2]{0:T(128)S(1)} %pad_add_fusion.pos, s32[2]{0:T(128)S(1)} %bitcast.32, s32[2]{0:T(128)S(1)} %collective-permute-done.lower, s32[2]{0:T(128)S(1)} %collective-permute-done.1.upper, f32[2,256,1024]{2,1,0:T(8,128)S(1)} %shard_map.87.spec, ...), custom_call_target="tpu_custom_call" | custom-call | tf_op jit(solution)/shard_map/pallas_call | solution.py:120
  65.0 4.1 %collective-permute-done.6.other = f32[2,256,256]{2,1,0:T(8,128)S(1)} collective-permute-done((f32[2,256,256]{2,1,0:T(8,128)S(1)}, f32[2,256,256]{2,1,0:T(8,128)S(1)}, u32[]{:S(2)}, u32[]{:S(2)}) %collective-permute-start.6) | collective-permute-done | bytes 524320 | tf_op jit(solution)/shard_map/ppermute | solution.py:429
  69.1 2.8 %shard_map.91 = (f32[2,512,256]{2,1,0:T(8,128)S(1)}, f32[2,256,256]{2,1,0:T(8,128)S(1)}) custom-call(s32[2]{0:T(128)S(1)} %pad_add_fusion.pos, f32[512,256]{1,0:T(8,128)S(1)} %collective-permute-done.3.far_amp, f32[512,256]{1,0:T(8,128)S(1)} %get-tuple-element.12.measured, f32[2,512,256]{2,1,0:T(8,128)S(1)} %shard_map.89.wave, ...), custom_call_target="tpu_custom_call" | custom-call | tf_op jit(solution)/shard_map/pallas_call | solution.py:120
  75.8 5.5 %collective-permute-done.7.other = f32[2,256,256]{2,1,0:T(8,128)S(1)} collective-permute-done((f32[2,256,256]{2,1,0:T(8,128)S(1)}, f32[2,256,256]{2,1,0:T(8,128)S(1)}, u32[]{:S(2)}, u32[]{:S(2)}) %collective-permute-start.7) | collective-permute-done | bytes 524320 | tf_op jit(solution)/shard_map/ppermute | solution.py:434
  83.0 19.4 %all_to_all.10.own = f32[8,2,32,512]{3,2,1,0:T(8,128)S(1)} all-to-all(f32[8,2,32,512]{3,2,1,0:T(8,128)S(1)} %shard_map.93), channel_id=1, replica_groups={{0,2,4,6,1,3,5,7},{8,10,12,14,9,11,13,15},{16,18,20,22,17,19,21,23},{24..., dimensions={0} | all-to-all | bytes 2097152 | tf_op jit(solution)/shard_map/all_to_all | solution.py:438
  105.1 3.0 %collective-permute-start.11 = (f32[4,2,32,512]{3,2,1,0:T(8,128)}, f32[4,2,32,512]{3,2,1,0:T(8,128)S(1)}, u32[]{:S(2)}, u32[]{:S(2)}) collective-permute-start(f32[4,2,32,512]{3,2,1,0:T(8,128)} %get-tuple-element.29), channel_id=1, source_target_pairs={{0,48},{8,248},{16,0},{24,8},{32,16},{40,24},{48,32},{56,40},{64,1... | collective-permute-start | bytes 1572872 | tf_op jit(solution)/shard_map/ppermute | solution.py:441
  108.1 3.1 %collective-permute-start.8 = (f32[4,2,32,512]{3,2,1,0:T(8,128)}, f32[4,2,32,512]{3,2,1,0:T(8,128)S(1)}, u32[]{:S(2)}, u32[]{:S(2)}) collective-permute-start(f32[4,2,32,512]{3,2,1,0:T(8,128)} %get-tuple-element.29), channel_id=1, source_target_pairs={{8,24},{24,40},{40,56},{56,72},{72,88},{88,104},{104,120},{120,136... | collective-permute-start | bytes 1572872 | tf_op jit(solution)/shard_map/ppermute | solution.py:443
  113.4 7.8 %all-reduce = s32[48]{0:T(128)S(1)} all-reduce(s32[48]{0:T(128)S(1)} %add_dynamic-update-slice_fusion), channel_id=2, replica_groups=mesh['row'=32,'col'=8] {'col'}, use_global_device_ids=true, to_apply=%add | all-reduce | flops 48 | bytes 384
  123.2 9.5 %collective-permute-done.11.upper_odd = f32[4,2,32,512]{3,2,1,0:T(8,128)S(1)} collective-permute-done((f32[4,2,32,512]{3,2,1,0:T(8,128)}, f32[4,2,32,512]{3,2,1,0:T(8,128)S(1)}, u32[]{:S(2)}, u32[]{:S(2)}) %collective-permute-start.11) | collective-permute-done | bytes 524320 | tf_op jit(solution)/shard_map/ppermute | solution.py:441
  134.9 7.7 %shard_map.94 = (f32[4096,128]{1,0:T(8,128)}, f32[8,2,32,1024]{3,2,1,0:T(8,128)}) custom-call(s32[2]{0:T(128)} %copy-done.5, s32[8,6]{1,0:T(8,128)} %reshape.13.leds, f32[8,2,32,512]{3,2,1,0:T(8,128)} %copy-done.9, f32[4,2,32,512]{3,2,1,0:T(8,128)} %copy-done.12, f32[4,2,32,512]{3,2,1,0:T(8,128)} %copy-done.13, f32[4,2,32,512]{3,2,1,0:T(8,128)} %copy-done.10, ...), custom_call_target="tpu_custom_call" | custom-call | tf_op jit(solution)/shard_map/pallas_call | solution.py:120
  142.6 18.9 %all-to-all-start.1 = ((f32[256,16,128]{2,1,0:T(8,128)}), f32[256,16,128]{2,1,0:T(8,128)S(1)}, u32[]{:S(2)}, u32[]{:S(2)}) async-start(f32[256,16,128]{2,1,0:T(8,128)} %bitcast.34), calls=%async_computation.1 | async-start | bytes 4194304 | tf_op jit(solution)/shard_map/all_to_all | solution.py:473
  169.1 2.6 %collective-permute-start.16 = (f32[2,32,1024]{2,1,0:T(8,128)S(1)}, f32[2,32,1024]{2,1,0:T(8,128)S(1)}, u32[]{:S(2)}, u32[]{:S(2)}) collective-permute-start(f32[2,32,1024]{2,1,0:T(8,128)S(1)} %get-tuple-element.22), channel_id=1, source_target_pairs={{0,5},{1,6},{2,7},{3,0},{4,1},{5,2},{6,3},{7,4},{8,13},{9,14},{10,... | collective-permute-start | bytes 786440 | tf_op jit(solution)/shard_map/ppermute | solution.py:469
  171.7 3.0 %collective-permute-done.12.refs_1_ = f32[2,32,1024]{2,1,0:T(8,128)S(1)} collective-permute-done((f32[2,32,1024]{2,1,0:T(8,128)S(1)}, f32[2,32,1024]{2,1,0:T(8,128)S(1)}, u32[]{:S(2)}, u32[]{:S(2)}) %collective-permute-start.12) | collective-permute-done | bytes 262176 | tf_op jit(solution)/shard_map/ppermute | solution.py:469
  174.7 3.1 %collective-permute-start.17 = (f32[2,32,1024]{2,1,0:T(8,128)S(1)}, f32[2,32,1024]{2,1,0:T(8,128)S(1)}, u32[]{:S(2)}, u32[]{:S(2)}) collective-permute-start(f32[2,32,1024]{2,1,0:T(8,128)S(1)} %get-tuple-element.21), channel_id=1, source_target_pairs={{0,6},{1,7},{2,0},{3,1},{4,2},{5,3},{6,4},{7,5},{8,14},{9,15},{10,... | collective-permute-start | bytes 786440 | tf_op jit(solution)/shard_map/ppermute | solution.py:469
  177.8 16.1 %collective-permute-done.13.refs_2_ = f32[2,32,1024]{2,1,0:T(8,128)S(1)} collective-permute-done((f32[2,32,1024]{2,1,0:T(8,128)S(1)}, f32[2,32,1024]{2,1,0:T(8,128)S(1)}, u32[]{:S(2)}, u32[]{:S(2)}) %collective-permute-start.13) | collective-permute-done | bytes 262176 | tf_op jit(solution)/shard_map/ppermute | solution.py:469
  193.9 7.3 %collective-permute-done.14.refs_3_ = f32[2,32,1024]{2,1,0:T(8,128)S(1)} collective-permute-done((f32[2,32,1024]{2,1,0:T(8,128)S(1)}, f32[2,32,1024]{2,1,0:T(8,128)S(1)}, u32[]{:S(2)}, u32[]{:S(2)}) %collective-permute-start.14) | collective-permute-done | bytes 262176 | tf_op jit(solution)/shard_map/ppermute | solution.py:469
  201.2 7.1 %collective-permute-done.15.refs_4_ = f32[2,32,1024]{2,1,0:T(8,128)S(1)} collective-permute-done((f32[2,32,1024]{2,1,0:T(8,128)S(1)}, f32[2,32,1024]{2,1,0:T(8,128)S(1)}, u32[]{:S(2)}, u32[]{:S(2)}) %collective-permute-start.15) | collective-permute-done | bytes 262176 | tf_op jit(solution)/shard_map/ppermute | solution.py:469
  212.3 2.6 %all-to-all-done.1 = f32[256,16,128]{2,1,0:T(8,128)S(1)} async-done(((f32[256,16,128]{2,1,0:T(8,128)}), f32[256,16,128]{2,1,0:T(8,128)S(1)}, u32[]{:S(2)}, u32[]{:S(2)}) %all-to-all-start.1) | async-done | bytes 2097184 | tf_op jit(solution)/shard_map/all_to_all | solution.py:473
  214.9 3.7 %shard_map.96 = f32[2,32,8192]{2,1,0:T(8,128)} custom-call(f32[4096,128]{1,0:T(8,128)S(1)} %bitcast.25, f32[2,32,256]{2,1,0:T(8,128)S(1)} %copy-done.3, bf16[4,256,256]{2,1,0:T(8,128)(2,1)S(1)} %copy-done.1), custom_call_target="tpu_custom_call" | custom-call | tf_op jit(solution)/shard_map/pallas_call | solution.py:120
  (67 shorter events, 41.8 us)
Async XLA Ops:
  0.6 12.9 %collective-permute-start = (s32[2]{0:T(128)}, s32[2]{0:T(128)S(1)}, u32[]{:S(2)}, u32[]{:S(2)}) collective-permute-start(s32[2]{0:T(128)} %bitcast.27), channel_id=1, source_target_pairs={{0,16},{1,17},{2,18},{3,19},{4,20},{5,21},{6,22},{7,23},{8,24},{9,... | collective-permute-start | bytes 32 | tf_op jit(solution)/shard_map/ppermute | solution.py:407
  4.5 9.0 %collective-permute-start.1 = (s32[2]{0:T(128)}, s32[2]{0:T(128)S(1)}, u32[]{:S(2)}, u32[]{:S(2)}) collective-permute-start(s32[2]{0:T(128)} %bitcast.28), channel_id=1, source_target_pairs={{0,240},{1,17},{2,242},{3,19},{4,244},{5,21},{6,246},{7,23},{8,248... | collective-permute-start | bytes 32 | tf_op jit(solution)/shard_map/ppermute | solution.py:408
  9.8 34.7 %collective-permute-start.2 = (f32[512,256]{1,0:T(8,128)S(1)}, f32[512,256]{1,0:T(8,128)S(1)}, u32[]{:S(2)}, u32[]{:S(2)}) collective-permute-start(f32[512,256]{1,0:T(8,128)S(1)} %dynamic-slice_bitcast_fusion), channel_id=1, source_target_pairs={{0,8},{1,9},{2,10},{3,11},{4,12},{5,13},{6,14},{7,15},{8,0},{9,17}... | collective-permute-start | bytes 1572872 | tf_op jit(solution)/shard_map/ppermute | solution.py:416
  13.5 67.8 %copy-start.5 = (s32[2]{0:T(128)}, s32[2]{0:T(128)S(1)}, u32[]{:S(2)}) copy-start(s32[2]{0:T(128)S(1)} %pad_add_fusion.pos) | copy-start | bytes 28
  13.5 30.9 %copy-start.4 = (f32[1,1,512,512]{3,2,1,0:T(8,128)S(1)}, f32[1,1,512,512]{3,2,1,0:T(8,128)}, u32[]{:S(2)}) copy-start(f32[1,1,512,512]{3,2,1,0:T(8,128)} %param.10) | copy-start | bytes 3145732
  13.6 30.9 %copy-start.8 = (f32[2,512,512]{2,1,0:T(8,128)S(1)}, f32[2,512,512]{2,1,0:T(8,128)}, u32[]{:S(2)}) copy-start(f32[2,512,512]{2,1,0:T(8,128)} %pupil.1) | copy-start | bytes 6291460
  14.7 43.0 %collective-permute-start.4 = (f32[2,256,512]{2,1,0:T(8,128)S(1)}, f32[2,256,512]{2,1,0:T(8,128)S(1)}, u32[]{:S(2)}, u32[]{:S(2)}) collective-permute-start(f32[2,256,512]{2,1,0:T(8,128)S(1)} %get-tuple-element.13), channel_id=1, source_target_pairs={{1,17},{3,19},{5,21},{7,23},{8,24},{9,25},{10,26},{11,27},{12,28},... | collective-permute-start | bytes 3145736 | tf_op jit(solution)/shard_map/ppermute | solution.py:421
  16.6 41.1 %collective-permute-start.5 = (f32[2,256,512]{2,1,0:T(8,128)S(1)}, f32[2,256,512]{2,1,0:T(8,128)S(1)}, u32[]{:S(2)}, u32[]{:S(2)}) collective-permute-start(f32[2,256,512]{2,1,0:T(8,128)S(1)} %get-tuple-element.14), channel_id=1, source_target_pairs={{0,240},{1,193},{2,242},{3,195},{4,244},{5,197},{6,246},{7,199},{8... | collective-permute-start | bytes 3145736 | tf_op jit(solution)/shard_map/ppermute | solution.py:420
  46.6 18.3 %collective-permute-start.3 = (f32[512,256]{1,0:T(8,128)S(1)}, f32[512,256]{1,0:T(8,128)S(1)}, u32[]{:S(2)}, u32[]{:S(2)}) collective-permute-start(f32[512,256]{1,0:T(8,128)S(1)} %get-tuple-element.11), channel_id=1, source_target_pairs={{1,17},{3,19},{5,21},{7,23},{17,33},{19,35},{21,37},{23,39},{33,49... | collective-permute-start | bytes 1572872 | tf_op jit(solution)/shard_map/ppermute | solution.py:425
  59.7 9.3 %collective-permute-start.6 = (f32[2,256,256]{2,1,0:T(8,128)S(1)}, f32[2,256,256]{2,1,0:T(8,128)S(1)}, u32[]{:S(2)}, u32[]{:S(2)}) collective-permute-start(f32[2,256,256]{2,1,0:T(8,128)S(1)} %shard_map.90), channel_id=1, source_target_pairs={{0,8},{1,57},{2,10},{3,59},{4,12},{5,61},{6,14},{7,63},{8,0},{9,17... | collective-permute-start | bytes 1572872 | tf_op jit(solution)/shard_map/ppermute | solution.py:429
  71.8 9.5 %collective-permute-start.7 = (f32[2,256,256]{2,1,0:T(8,128)S(1)}, f32[2,256,256]{2,1,0:T(8,128)S(1)}, u32[]{:S(2)}, u32[]{:S(2)}) collective-permute-start(f32[2,256,256]{2,1,0:T(8,128)S(1)} %get-tuple-element.17), channel_id=1, source_target_pairs={{0,8},{1,57},{2,10},{3,59},{4,12},{5,61},{6,14},{7,63},{8,0},{9,17... | collective-permute-start | bytes 1572872 | tf_op jit(solution)/shard_map/ppermute | solution.py:434
  103.7 19.5 %collective-permute-start.10 = (f32[4,2,32,512]{3,2,1,0:T(8,128)}, f32[4,2,32,512]{3,2,1,0:T(8,128)S(1)}, u32[]{:S(2)}, u32[]{:S(2)}) collective-permute-start(f32[4,2,32,512]{3,2,1,0:T(8,128)} %get-tuple-element.28), channel_id=1, source_target_pairs={{0,16},{8,24},{16,32},{24,40},{32,48},{40,56},{48,64},{56,72},{64,... | collective-permute-start | bytes 1572872 | tf_op jit(solution)/shard_map/ppermute | solution.py:440
  105.1 27.5 %collective-permute-start.11 = (f32[4,2,32,512]{3,2,1,0:T(8,128)}, f32[4,2,32,512]{3,2,1,0:T(8,128)S(1)}, u32[]{:S(2)}, u32[]{:S(2)}) collective-permute-start(f32[4,2,32,512]{3,2,1,0:T(8,128)} %get-tuple-element.29), channel_id=1, source_target_pairs={{0,48},{8,248},{16,0},{24,8},{32,16},{40,24},{48,32},{56,40},{64,1... | collective-permute-start | bytes 1572872 | tf_op jit(solution)/shard_map/ppermute | solution.py:441
  108.1 25.1 %collective-permute-start.8 = (f32[4,2,32,512]{3,2,1,0:T(8,128)}, f32[4,2,32,512]{3,2,1,0:T(8,128)S(1)}, u32[]{:S(2)}, u32[]{:S(2)}) collective-permute-start(f32[4,2,32,512]{3,2,1,0:T(8,128)} %get-tuple-element.29), channel_id=1, source_target_pairs={{8,24},{24,40},{40,56},{56,72},{72,88},{88,104},{104,120},{120,136... | collective-permute-start | bytes 1572872 | tf_op jit(solution)/shard_map/ppermute | solution.py:443
  111.2 22.0 %collective-permute-start.9 = (f32[4,2,32,512]{3,2,1,0:T(8,128)}, f32[4,2,32,512]{3,2,1,0:T(8,128)S(1)}, u32[]{:S(2)}, u32[]{:S(2)}) collective-permute-start(f32[4,2,32,512]{3,2,1,0:T(8,128)} %get-tuple-element.28), channel_id=1, source_target_pairs={{8,248},{24,8},{40,24},{56,40},{72,56},{88,72},{104,88},{120,104},... | collective-permute-start | bytes 1572872 | tf_op jit(solution)/shard_map/ppermute | solution.py:444
  142.6 72.3 %all-to-all-start.1 = ((f32[256,16,128]{2,1,0:T(8,128)}), f32[256,16,128]{2,1,0:T(8,128)S(1)}, u32[]{:S(2)}, u32[]{:S(2)}) async-start(f32[256,16,128]{2,1,0:T(8,128)} %bitcast.34), calls=%async_computation.1 | async-start | bytes 4194304 | tf_op jit(solution)/shard_map/all_to_all | solution.py:473
  161.5 48.8 %copy-start.6 = (s32[2]{0:T(128)S(1)}, s32[2]{0:T(128)}, u32[]{:S(2)}) copy-start(s32[2]{0:T(128)} %copy-done.5) | copy-start | bytes 28
  163.2 11.5 %collective-permute-start.12 = (f32[2,32,1024]{2,1,0:T(8,128)S(1)}, f32[2,32,1024]{2,1,0:T(8,128)S(1)}, u32[]{:S(2)}, u32[]{:S(2)}) collective-permute-start(f32[2,32,1024]{2,1,0:T(8,128)S(1)} %get-tuple-element.26), channel_id=1, source_target_pairs={{0,1},{1,2},{2,3},{3,4},{4,5},{5,6},{6,7},{7,0},{8,9},{9,10},{10,1... | collective-permute-start | bytes 786440 | tf_op jit(solution)/shard_map/ppermute | solution.py:469
  164.8 29.1 %collective-permute-start.13 = (f32[2,32,1024]{2,1,0:T(8,128)S(1)}, f32[2,32,1024]{2,1,0:T(8,128)S(1)}, u32[]{:S(2)}, u32[]{:S(2)}) collective-permute-start(f32[2,32,1024]{2,1,0:T(8,128)S(1)} %get-tuple-element.25), channel_id=1, source_target_pairs={{0,2},{1,3},{2,4},{3,5},{4,6},{5,7},{6,0},{7,1},{8,10},{9,11},{10,... | collective-permute-start | bytes 786440 | tf_op jit(solution)/shard_map/ppermute | solution.py:469
  166.0 35.2 %collective-permute-start.14 = (f32[2,32,1024]{2,1,0:T(8,128)S(1)}, f32[2,32,1024]{2,1,0:T(8,128)S(1)}, u32[]{:S(2)}, u32[]{:S(2)}) collective-permute-start(f32[2,32,1024]{2,1,0:T(8,128)S(1)} %get-tuple-element.24), channel_id=1, source_target_pairs={{0,3},{1,4},{2,5},{3,6},{4,7},{5,0},{6,1},{7,2},{8,11},{9,12},{10,... | collective-permute-start | bytes 786440 | tf_op jit(solution)/shard_map/ppermute | solution.py:469
  167.7 40.6 %collective-permute-start.15 = (f32[2,32,1024]{2,1,0:T(8,128)S(1)}, f32[2,32,1024]{2,1,0:T(8,128)S(1)}, u32[]{:S(2)}, u32[]{:S(2)}) collective-permute-start(f32[2,32,1024]{2,1,0:T(8,128)S(1)} %get-tuple-element.23), channel_id=1, source_target_pairs={{0,4},{1,5},{2,6},{3,7},{4,0},{5,1},{6,2},{7,3},{8,12},{9,13},{10,... | collective-permute-start | bytes 786440 | tf_op jit(solution)/shard_map/ppermute | solution.py:469
  169.1 40.0 %collective-permute-start.16 = (f32[2,32,1024]{2,1,0:T(8,128)S(1)}, f32[2,32,1024]{2,1,0:T(8,128)S(1)}, u32[]{:S(2)}, u32[]{:S(2)}) collective-permute-start(f32[2,32,1024]{2,1,0:T(8,128)S(1)} %get-tuple-element.22), channel_id=1, source_target_pairs={{0,5},{1,6},{2,7},{3,0},{4,1},{5,2},{6,3},{7,4},{8,13},{9,14},{10,... | collective-permute-start | bytes 786440 | tf_op jit(solution)/shard_map/ppermute | solution.py:469
  174.7 34.4 %collective-permute-start.17 = (f32[2,32,1024]{2,1,0:T(8,128)S(1)}, f32[2,32,1024]{2,1,0:T(8,128)S(1)}, u32[]{:S(2)}, u32[]{:S(2)}) collective-permute-start(f32[2,32,1024]{2,1,0:T(8,128)S(1)} %get-tuple-element.21), channel_id=1, source_target_pairs={{0,6},{1,7},{2,0},{3,1},{4,2},{5,3},{6,4},{7,5},{8,14},{9,15},{10,... | collective-permute-start | bytes 786440 | tf_op jit(solution)/shard_map/ppermute | solution.py:469
  193.9 16.3 %collective-permute-start.18 = (f32[2,32,1024]{2,1,0:T(8,128)S(1)}, f32[2,32,1024]{2,1,0:T(8,128)S(1)}, u32[]{:S(2)}, u32[]{:S(2)}) collective-permute-start(f32[2,32,1024]{2,1,0:T(8,128)S(1)} %get-tuple-element.20), channel_id=1, source_target_pairs={{0,7},{1,0},{2,1},{3,2},{4,3},{5,4},{6,5},{7,6},{8,15},{9,8},{10,9... | collective-permute-start | bytes 786440 | tf_op jit(solution)/shard_map/ppermute | solution.py:469
  (11 other events, 97.0 us)
